TPU v7x, 32 devices: a whole 2x2x4 slice. The times are simulated.
32 devices in a mesh: dp: 4 (over y, core), fsdp: 8 (over z, x).
Axes of the slice: x: 2, y: 2, z: 4, core: 2. Of those that a mesh axis runs over, the one named last changes fastest.
Arguments:
- tokens: bfloat16 [2, 8, 512, 1024], P(None, 'fsdp', 'dp'), may hold values from -6 to 6
- cotangent: bfloat16 [2, 8, 512, 1024], P(None, 'fsdp', 'dp'), may hold values from -6 to 6
- in_weight: float32 [1024, 4096], P(('dp', 'fsdp')), may hold values from -0.1875 to 0.1875
- out_weight: float32 [2048, 1024], P(('dp', 'fsdp')), may hold values from -0.25 to 0.25
- xproj_weight: float32 [2048, 96], P(('dp', 'fsdp')), may hold values from -0.125 to 0.125
- dtproj_weight: float32 [64, 2048], P(None, ('dp', 'fsdp')), may hold values from -3 to 3
- chan_params: float32 [7, 2048], P(None, ('dp', 'fsdp')), may hold values from -7.5 to 2
- a_log: float32 [16, 2048], P(None, ('dp', 'fsdp')), may hold values from -4.5 to 1
- norm_gain: float32 [1024], P(('dp', 'fsdp')), may hold values from 0.5 to 1.5
- in_moments: float32 [2, 1024, 4096], P(None, ('dp', 'fsdp')), as said below
- out_moments: float32 [2, 2048, 1024], P(None, ('dp', 'fsdp')), as said below
- xproj_moments: float32 [2, 2048, 96], P(None, ('dp', 'fsdp')), as said below
- dtproj_moments: float32 [2, 64, 2048], P(None, None, ('dp', 'fsdp')), as said below
- chan_moments: float32 [2, 7, 2048], P(None, None, ('dp', 'fsdp')), as said below
- alog_moments: float32 [2, 16, 2048], P(None, None, ('dp', 'fsdp')), as said below
- gain_moments: float32 [2, 1024], P(None, ('dp', 'fsdp')), as said below
Outputs:
- block_output: bfloat16 [2, 8, 512, 1024], P(None, 'fsdp', 'dp')
- input_grad: float32 [2, 8, 512, 1024], P(None, 'fsdp', 'dp')
- grad_norm: float32 [], replicated
- next_in_moments: float32 [2, 1024, 4096], P(None, ('dp', 'fsdp'))
- next_in_weight: float32 [1024, 4096], P(('dp', 'fsdp'))
- next_out_moments: float32 [2, 2048, 1024], P(None, ('dp', 'fsdp'))
- next_out_weight: float32 [2048, 1024], P(('dp', 'fsdp'))
- next_xproj_moments: float32 [2, 2048, 96], P(None, ('dp', 'fsdp'))
- next_xproj_weight: float32 [2048, 96], P(('dp', 'fsdp'))
- next_dtproj_moments: float32 [2, 64, 2048], P(None, None, ('dp', 'fsdp'))
- next_dtproj_weight: float32 [64, 2048], P(None, ('dp', 'fsdp'))
- next_chan_moments: float32 [2, 7, 2048], P(None, None, ('dp', 'fsdp'))
- next_chan_params: float32 [7, 2048], P(None, ('dp', 'fsdp'))
- next_alog_moments: float32 [2, 16, 2048], P(None, None, ('dp', 'fsdp'))
- next_a_log: float32 [16, 2048], P(None, ('dp', 'fsdp'))
- next_gain_moments: float32 [2, 1024], P(None, ('dp', 'fsdp'))
- next_norm_gain: float32 [1024], P(('dp', 'fsdp'))
Inputs may be any that keep to these rules, and one draw needn't show every extreme that they name: `in_moments`: the roots of the second moments are positive. `out_moments`: the roots of the second moments are positive. `xproj_moments`: the roots of the second moments are positive. `dtproj_moments`: the roots of the second moments are positive. `chan_moments`: the roots of the second moments are positive. `alog_moments`: the roots of the second moments are positive. `gain_moments`: the roots of the second moments are positive.
All inputs are finite; a program needn't handle non-finite values.
Results may differ from a plain program's by a relative error of at most 0.009.
The roundings to bfloat16 on the way count: a program that leaves them out, or rounds other values in their place, can miss the bound.
Values may be sent and summed in bfloat16 or wider, within the bound.
No kernel may reach another device: no remote copies, remote signals or barrier semaphores. Data moves between devices by JAX's collectives and lax.ppermute only.
A program may use at most 192 MiB of HBM per device.

v0:
```python
import jax
import jax.numpy as jnp
from jax import lax
from jax.experimental import pallas as pl
from jax.experimental.pallas import tpu as pltpu
from jax.sharding import PartitionSpec as P

N = 16
R = 64
KW = 4
STEP = 7
ROWS = 128
T = 16
WIDE = R + 2 * N
REST = 32
GRADS = WIDE + R + REST
AT_DT = 128
AT_REST = 192
SMALL = 256
BIG = 512

bf16 = jnp.bfloat16
f32 = jnp.float32
LOG2E = 1.4426950408889634
clip_limit = 1.0
learn_rates = (0.03, 0.03, 0.03, 0.15, 0.3, 1.0, 0.3)


def dot(left, right, on_left, on_right):
    return lax.dot_general(
        left, right, (((on_left,), (on_right,)), ((), ())), preferred_element_type=f32
    )


def params(mib):
    return pltpu.CompilerParams(vmem_limit_bytes=mib * 1024 * 1024)


def cost(us):
    return pl.CostEstimate(flops=int(us * 8e7), bytes_accessed=int(us * 3e5), transcendentals=0)


def swap(x, axis, mask):
    peers = lax.axis_size(axis)
    return lax.ppermute(x, axis, [(i, i ^ mask) for i in range(peers)])


def after(x, *others):
    return lax.optimization_barrier((x,) + others)[0]


def masks(axis):
    peers = lax.axis_size(axis)
    return [1 << k for k in range(peers.bit_length() - 1)]


def in_order(parts, axis):
    peers = lax.axis_size(axis)
    for mask in masks(axis):
        pairs = parts.reshape((peers // (2 * mask), 2, mask) + parts.shape[1:])
        high = (lax.axis_index(axis) & mask) != 0
        parts = jnp.where(high, pairs[:, ::-1], pairs).reshape(parts.shape)
    return parts


def parts_dp_far(x):
    held = [x]
    for mask in masks("dp")[:0:-1]:
        held = [part for p in held for part in (p, swap(p, "dp", mask))]
    return held


def parts_dp_near(held):
    return [part for p in held for part in (p, swap(p, "dp", 1))]


def gather_far(x):
    peers = lax.axis_size("fsdp")
    depth = min(4, peers)
    return [x] + [swap(x, "fsdp", m * (peers // depth)) for m in range(1, depth)]


def gather_near(far):
    far = jnp.stack(far)
    near = lax.axis_size("fsdp") // far.shape[0]
    return [far] + [swap(far, "fsdp", m) for m in range(1, near)]


def merge_near(nears):
    parts = jnp.stack(nears, axis=1)
    return in_order(parts.reshape((-1,) + parts.shape[2:]), "fsdp")


def reduce_dp_near(parts):
    return [parts[p] + swap(parts[p + 1], "dp", 1).astype(f32) for p in range(0, len(parts), 2)]


def send_dp_far(parts):
    for mask in masks("dp")[1:-1]:
        parts = [
            parts[p] + swap(parts[p + 1].astype(bf16), "dp", mask).astype(f32)
            for p in range(0, len(parts), 2)
        ]
    return [parts[0]] + [
        swap(part.astype(bf16), "dp", masks("dp")[-1]) for part in parts[1:]
    ]


def send_dp(parts):
    return [parts[0]] + [swap(parts[m], "dp", m) for m in range(1, len(parts))]


def sum_dp_near(x):
    high = (lax.axis_index("dp") & 1) != 0
    split = x.reshape((2, x.shape[0] // 2) + x.shape[1:])
    mine = jnp.where(high, split[1], split[0])
    other = jnp.where(high, split[0], split[1])
    return mine + swap(other, "dp", 1)


def sum_dp_far(mine):
    high = (lax.axis_index("dp") & 1) != 0
    for mask in masks("dp")[1:]:
        mine = mine + swap(mine, "dp", mask)
    mine = mine.astype(bf16)
    other = swap(mine, "dp", 1)
    both = jnp.where(high, jnp.stack([other, mine]), jnp.stack([mine, other]))
    return both.reshape((-1,) + mine.shape[1:])


def reduce_near(parts):
    mine = parts[0].astype(f32)
    for m in range(1, len(parts)):
        mine = mine + swap(parts[m].astype(bf16), "fsdp", m).astype(f32)
    return mine


def split_near(x):
    peers = lax.axis_size("fsdp")
    depth = min(4, peers)
    x = in_order(x, "fsdp").reshape((depth, peers // depth) + x.shape[1:])
    return [x[:, m] for m in range(x.shape[1])]


def send_far(mine):
    depth = mine.shape[0]
    near = lax.axis_size("fsdp") // depth
    return [mine[0]] + [
        swap(mine[m].astype(bf16), "fsdp", m * near) for m in range(1, depth)
    ]


def assemble_first_kernel(me_ref, *refs):
    raws = refs[:-6]
    w_ref, small_ref, gain_ref, a_ref, chan_ref, gains = refs[-6:]
    near = len(raws)
    depth = raws[0].shape[0]
    model, width = w_ref.shape
    peers = near * depth
    own = width // peers
    fold = width // SMALL
    here = model // peers
    own_in = model // gains.shape[0]
    dps = here // own_in
    stretch = own // fold
    at_small = here + dps + -dps % 16
    for m in range(near):
        for d in range(depth):
            j = me_ref[1] ^ (d * near + m)
            for k in range(dps):
                to = pl.multiple_of((k * peers + j) * own_in, own_in)
                w_ref[pl.ds(to, own_in), :] = raws[m][d, k * own_in : (k + 1) * own_in, :]
                row = raws[m][d, here : here + 16, 0:128].astype(f32)[k : k + 1]
                gains[pl.ds(k * peers + j, 1), :] = row
            for f in range(fold):
                to = pl.multiple_of(j * own + f * stretch, stretch)
                small_ref[pl.ds(to, stretch), :] = raws[m][
                    d, at_small : at_small + stretch, f * SMALL : (f + 1) * SMALL
                ]
    row = lax.broadcasted_iota(jnp.int32, (own_in, model), 0)
    column = lax.broadcasted_iota(jnp.int32, (own_in, model), 1)
    tile = (column % own_in == row).astype(f32).astype(bf16)
    tiled = dot(gains[:, 0:own_in].astype(bf16), tile, 1, 0)
    row = lax.broadcasted_iota(jnp.int32, tiled.shape, 0)
    column = lax.broadcasted_iota(jnp.int32, tiled.shape, 1)
    gain_ref[...] = jnp.sum(jnp.where(column // own_in == row, tiled, 0.0), axis=0, keepdims=True)
    turned = small_ref[...].astype(f32).T
    a_ref[...] = -jnp.exp(turned[AT_REST : AT_REST + N])
    chan_ref[...] = turned[AT_REST + N : AT_REST + N + 8]


def assemble_second_kernel(me_ref, *refs):
    raws = refs[:-2]
    wg_ref, wo_ref = refs[-2:]
    near = len(raws)
    depth = raws[0].shape[0]
    model, width = wg_ref.shape
    peers = near * depth
    own = width // peers
    here = model // peers
    dps = lax.axis_size("dp")
    own_in = here // dps
    for m in range(near):
        for d in range(depth):
            j = me_ref[1] ^ (d * near + m)
            for k in range(dps):
                to = pl.multiple_of((k * peers + j) * own_in, own_in)
                wg_ref[pl.ds(to, own_in), :] = raws[m][d, k * own_in : (k + 1) * own_in, :]
            for c in range(model // width):
                to = pl.multiple_of(j * own, own)
                wo_ref[pl.ds(to, own), c * width : (c + 1) * width] = raws[m][
                    d, here + c * own : here + (c + 1) * own, :
                ]


def assemble(kernel, name, me, raws, shapes, scratch):
    whole = pl.BlockSpec(memory_space=pltpu.VMEM)
    return pl.pallas_call(
        kernel,
        in_specs=[pl.BlockSpec(memory_space=pltpu.SMEM)] + [whole] * len(raws),
        out_specs=[whole] * len(shapes),
        out_shape=[jax.ShapeDtypeStruct(shape, dtype) for shape, dtype in shapes],
        scratch_shapes=scratch,
        compiler_params=params(60),
        cost_estimate=cost(2),
        name=name,
    )(me, *raws)


def lay_pieces(whole, refs, me):
    piece = refs[0].shape[1]
    for p, ref in enumerate(refs):
        whole[pl.ds(pl.multiple_of((me ^ p) * piece, piece), piece), :] = ref[0]


def deal_pieces(refs, part, me, block):
    piece = refs[0].shape[1]
    per = part.shape[0] // piece
    for p, ref in enumerate(refs):
        at = (me ^ p) - block * per

        @pl.when((at >= 0) & (at < per))
        def _(ref=ref, at=at):
            ref[0] = part[pl.ds(pl.multiple_of(at * piece, piece), piece), :].astype(ref.dtype)


def piece_shapes(dps, seqs, piece, model, wide):
    return [
        jax.ShapeDtypeStruct((seqs, piece, model), bf16 if p % wide else f32) for p in range(dps)
    ]


def piece_specs(dps, piece, model):
    return [pl.BlockSpec((1, piece, model), lambda s, b, me: (s, 0, 0))] * dps


def enter_kernel(me_ref, gain_ref, w_ref, chan_ref, wx_ref, *refs):
    tok_refs = refs[:-7]
    normed_ref, conv_ref, pre_ref, act_ref, xt_ref, padded, whole = refs[-7:]
    block = pl.program_id(1)
    rows = conv_ref.shape[1]

    @pl.when(block == 0)
    def _():
        padded[0:8, :] = jnp.zeros((8, padded.shape[1]), f32)
        lay_pieces(whole, tok_refs, me_ref[0])

    @pl.when(block > 0)
    def _():
        padded[0:8, :] = padded[rows : rows + 8, :]

    x = whole[pl.ds(pl.multiple_of(block * rows, rows), rows), :].astype(f32)
    inv = lax.rsqrt(jnp.mean(x * x, axis=-1, keepdims=True) + 1e-05)
    normed = (x * inv * gain_ref[...]).astype(bf16)
    normed_ref[0] = normed
    conv = dot(normed, w_ref[...], 1, 0).astype(bf16)
    conv_ref[0] = conv
    padded[8 : rows + 8, :] = conv.astype(f32)
    pre = chan_ref[KW : KW + 1, :]
    for k in range(KW):
        pre = pre + chan_ref[k : k + 1, :] * padded[5 + k : 5 + k + rows, :]
    pre_ref[0] = pre
    act = (pre * jax.nn.sigmoid(pre)).astype(bf16)
    act_ref[0] = act
    xt_ref[...] = dot(wx_ref[:, 0:WIDE], act, 0, 1)


def enter(me, gain, w, chan, wx, tok):
    dps = len(tok)
    seqs, piece, model = tok[0].shape
    length = dps * piece
    width = w.shape[1]
    rows = min(BIG, length)
    blocks = length // rows

    def at(s, b, me):
        return (s, b, 0)

    def fixed(s, b, me):
        return (0, 0)

    return pl.pallas_call(
        enter_kernel,
        grid_spec=pltpu.PrefetchScalarGridSpec(
            num_scalar_prefetch=1,
            grid=(seqs, blocks),
            in_specs=[
                pl.BlockSpec((1, model), fixed),
                pl.BlockSpec((model, width), fixed),
                pl.BlockSpec((8, width), fixed),
                pl.BlockSpec((width, SMALL), fixed),
            ]
            + piece_specs(dps, piece, model),
            out_specs=[
                pl.BlockSpec((1, rows, model), at),
                pl.BlockSpec((1, rows, width), at),
                pl.BlockSpec((1, rows, width), at),
                pl.BlockSpec((1, rows, width), at),
                pl.BlockSpec((WIDE, rows), lambda s, b, me: (0, s * blocks + b)),
            ],
            scratch_shapes=[pltpu.VMEM((rows + 8, width), f32), pltpu.VMEM((length, model), bf16)],
        ),
        out_shape=[
            jax.ShapeDtypeStruct((seqs, length, model), bf16),
            jax.ShapeDtypeStruct((seqs, length, width), bf16),
            jax.ShapeDtypeStruct((seqs, length, width), f32),
            jax.ShapeDtypeStruct((seqs, length, width), bf16),
            jax.ShapeDtypeStruct((WIDE, seqs * length), f32),
        ],
        compiler_params=params(60),
        cost_estimate=cost(7),
        name="enter",
    )(me, gain, w, chan, wx, *tok)


def own_columns_of(rows):
    row = lax.broadcasted_iota(jnp.int32, (rows, T * N), 0)
    column = lax.broadcasted_iota(jnp.int32, (rows, T * N), 1)
    return column // N == row % T


def spread(block):
    row = lax.broadcasted_iota(jnp.int32, (N, T * N), 0)
    column = lax.broadcasted_iota(jnp.int32, (N, T * N), 1)
    tile = (column % N == row).astype(f32).astype(bf16)
    tiled = jnp.dot(block.astype(bf16), tile, preferred_element_type=f32)
    return jnp.where(own_columns_of(block.shape[0]), tiled, 0.0).astype(bf16)


def softplus(v):
    return jnp.maximum(v, 0.0) + jnp.log1p(jnp.exp(-jnp.abs(v)))


def forward_kernel(
    xt_ref, act_ref, dtw_ref, chan_ref, a_ref, gate_in_ref, h_ref, dt_ref, sp_ref, state, push
):
    @pl.when(pl.program_id(1) == 0)
    def _():
        state[...] = jnp.zeros_like(state)

    columns = xt_ref[...].astype(f32)
    rows_in = columns.T
    rank = rows_in[:, :R].astype(bf16)
    pre = dot(rank, dtw_ref[:, AT_DT : AT_DT + R], 1, 1) + chan_ref[KW + 1 : KW + 2, :]
    sp_ref[0] = pre
    steps = softplus(pre)
    dt_ref[0] = steps
    push[...] = steps * act_ref[0].astype(f32)
    scaled = a_ref[...] * LOG2E
    drive = columns[R : R + N]
    reads = spread(rows_in[:, R + N :])
    h = state[...]
    for k in range(ROWS // T):
        for j in range(T):
            t = k * T + j
            decay = jnp.exp2(dt_ref[0, t : t + 1, :] * scaled)
            h = decay * h + drive[:, t : t + 1] * push[t : t + 1, :]
            h_ref[0, t * N : (t + 1) * N, :] = h.astype(bf16)
        here = slice(k * T, (k + 1) * T)
        scanned = dot(reads[here], h_ref[0, k * T * N : (k + 1) * T * N, :], 1, 0)
        gate_in_ref[0, here, :] = scanned + chan_ref[KW + 2 : KW + 3, :] * act_ref[
            0, here, :
        ].astype(f32)
    state[...] = h


def scan_forward(xt, act, dtw, chan, a_matrix):
    seqs, length, width = act.shape
    blocks = length // ROWS

    def at(s, b):
        return (s, b, 0)

    def fixed(s, b):
        return (0, 0)

    return pl.pallas_call(
        forward_kernel,
        grid=(seqs, blocks),
        in_specs=[
            pl.BlockSpec((WIDE, ROWS), lambda s, b: (0, s * blocks + b)),
            pl.BlockSpec((1, ROWS, width), at),
            pl.BlockSpec((width, SMALL), fixed),
            pl.BlockSpec((8, width), fixed),
            pl.BlockSpec((N, width), fixed),
        ],
        out_specs=[
            pl.BlockSpec((1, ROWS, width), at),
            pl.BlockSpec((1, ROWS * N, width), at),
            pl.BlockSpec((1, ROWS, width), at),
            pl.BlockSpec((1, ROWS, width), at),
        ],
        out_shape=[
            jax.ShapeDtypeStruct((seqs, length, width), f32),
            jax.ShapeDtypeStruct((seqs, length * N, width), bf16),
            jax.ShapeDtypeStruct((seqs, length, width), f32),
            jax.ShapeDtypeStruct((seqs, length, width), f32),
        ],
        scratch_shapes=[pltpu.VMEM((N, width), f32), pltpu.VMEM((ROWS, width), f32)],
        compiler_params=params(60),
        cost_estimate=cost(18),
        name="scan_forward",
    )(xt, act, dtw, chan, a_matrix)


def middle_kernel(
    me_ref,
    gate_in_ref,
    act_ref,
    normed_ref,
    wg_ref,
    wo_ref,
    *refs,
):
    dps = lax.axis_size("dp")
    near = len(refs) - 2 * dps - 8
    cot_refs, part_refs = refs[:dps], refs[dps : 2 * dps]
    gout_refs = refs[2 * dps : 2 * dps + near]
    ggi_ref, ggp_ref, gin_ref, gskip_ref = refs[2 * dps + near : 2 * dps + near + 4]
    out_total, in_total, whole, part = refs[2 * dps + near + 4 :]
    block = pl.program_id(1)
    rows = act_ref.shape[1]
    start = (pl.program_id(0) == 0) & (block == 0)
    end = (pl.program_id(0) == pl.num_programs(0) - 1) & (block == pl.num_programs(1) - 1)

    @pl.when(start)
    def _():
        out_total[...] = jnp.zeros_like(out_total)
        in_total[...] = jnp.zeros_like(in_total)
        gskip_ref[...] = jnp.zeros_like(gskip_ref)

    @pl.when(block == 0)
    def _():
        lay_pieces(whole, cot_refs, me_ref[0])

    cot = whole[pl.ds(pl.multiple_of(block * rows, rows), rows), :]
    grad_gated = dot(cot, wo_ref[...], 1, 1)
    normed = normed_ref[0]
    gate = dot(normed, wg_ref[...], 1, 0).astype(bf16).astype(f32)
    sig = jax.nn.sigmoid(gate)
    gate_act = gate * sig
    gate_in = gate_in_ref[0]
    gated = (gate_in * gate_act).astype(bf16)
    ggi = grad_gated * gate_act
    ggi_ref[0] = ggi
    ggp = (grad_gated * gate_in * (sig * (1.0 + gate * (1.0 - sig)))).astype(bf16)
    ggp_ref[0] = ggp
    gskip_ref[...] += jnp.sum(ggi * act_ref[0].astype(f32), axis=0, keepdims=True)
    part[...] = dot(gated, wo_ref[...], 1, 0)
    deal_pieces(part_refs, part, me_ref[0], block)
    out_total[...] += dot(gated, cot, 0, 0)
    in_total[...] += dot(normed, ggp, 0, 0)

    @pl.when(end)
    def _():
        gin_ref[...] = in_total[...].astype(bf16)
        depth, own, _ = gout_refs[0].shape
        for j in range(near * depth):
            place = me_ref[1] ^ j
            for m, ref in enumerate(gout_refs):

                @pl.when(place % near == m)
                def _(ref=ref, place=place, j=j):
                    ref[place // near] = out_total[j * own : (j + 1) * own, :].astype(bf16)


def middle(me, gate_in, act, normed, wg, wo, cot, near, depth):
    dps = len(cot)
    seqs, piece, model = cot[0].shape
    length = dps * piece
    width = wo.shape[0]
    rows = min(BIG, length)
    blocks = length // rows
    own = width // (near * depth)

    def at(s, b, me):
        return (s, b, 0)

    def fixed(s, b, me):
        return (0, 0)

    return pl.pallas_call(
        middle_kernel,
        grid_spec=pltpu.PrefetchScalarGridSpec(
            num_scalar_prefetch=1,
            grid=(seqs, blocks),
            in_specs=[
                pl.BlockSpec((1, rows, width), at),
                pl.BlockSpec((1, rows, width), at),
                pl.BlockSpec((1, rows, model), at),
                pl.BlockSpec((model, width), fixed),
                pl.BlockSpec((width, model), fixed),
            ]
            + piece_specs(dps, piece, model),
            out_specs=piece_specs(dps, piece, model)
            + [pl.BlockSpec((depth, own, model), lambda s, b, me: (0, 0, 0))] * near
            + [
                pl.BlockSpec((1, rows, width), at),
                pl.BlockSpec((1, rows, width), at),
                pl.BlockSpec((model, width), fixed),
                pl.BlockSpec((1, width), fixed),
            ],
            scratch_shapes=[
                pltpu.VMEM((width, model), f32),
                pltpu.VMEM((model, width), f32),
                pltpu.VMEM((length, model), bf16),
                pltpu.VMEM((rows, model), f32),
            ],
        ),
        out_shape=piece_shapes(dps, seqs, piece, model, dps)
        + [jax.ShapeDtypeStruct((depth, own, model), bf16)] * near
        + [
            jax.ShapeDtypeStruct((seqs, length, width), f32),
            jax.ShapeDtypeStruct((seqs, length, width), bf16),
            jax.ShapeDtypeStruct((model, width), bf16),
            jax.ShapeDtypeStruct((1, width), f32),
        ],
        compiler_params=params(60),
        cost_estimate=cost(9),
        name="middle",
    )(me, gate_in, act, normed, wg, wo, *cot)


def backward_kernel(
    xt_ref,
    act_ref,
    dt_ref,
    sp_ref,
    ggi_ref,
    chan_ref,
    a_ref,
    h_ref,
    before_ref,
    dtw_ref,
    *refs,
):
    gsp_ref, gact_ref, gxt_ref, galog_ref, carried, total, g_buf, q_buf = refs[-8:]
    first = pl.program_id(0) == pl.num_programs(0) - 1

    @pl.when(pl.program_id(0) == 0)
    def _():
        carried[...] = jnp.zeros_like(carried)
        total[...] = jnp.zeros_like(total)

    columns = xt_ref[...].astype(f32)
    rows_in = columns.T
    a_now = a_ref[...]
    scaled = a_now * LOG2E
    read = columns[R + N :]
    ones = own_columns_of(T).astype(f32).astype(bf16)
    drives = spread(rows_in[:, R : R + N])
    ggi_low = ggi_ref[0].astype(bf16)
    push_low = (dt_ref[0] * act_ref[0].astype(f32)).astype(bf16)
    lanes = lax.broadcasted_iota(jnp.int32, (N, T), 1)
    p = carried[...]
    acc = total[...]
    for k in reversed(range(ROWS // T)):
        for j in reversed(range(T)):
            t = k * T + j
            step_row = dt_ref[0, t : t + 1, :]
            g = read[:, t : t + 1] * ggi_ref[0, t : t + 1, :] + p
            p = jnp.exp2(step_row * scaled) * g
            if t > 0:
                h_before = h_ref[0, (t - 1) * N : t * N, :].astype(f32)
            else:
                h_before = jnp.where(first, 0.0, before_ref[0].astype(f32))
            q = p * h_before
            acc = acc + q * step_row
            g_buf[t * N : (t + 1) * N, :] = g.astype(bf16)
            q_buf[t * N : (t + 1) * N, :] = (a_now * q).astype(bf16)
        here = slice(k * T, (k + 1) * T)
        states = slice(k * T * N, (k + 1) * T * N)
        pulled = dot(drives[here], g_buf[states, :], 1, 0)
        along = dot(ones, q_buf[states, :], 1, 0)
        act_now = act_ref[0, here, :].astype(f32)
        grad_steps = along + act_now * pulled
        gsp_ref[0, here, :] = (grad_steps * jax.nn.sigmoid(sp_ref[0, here, :])).astype(bf16)
        gact_ref[0, here, :] = (
            pulled * dt_ref[0, here, :] + chan_ref[KW + 2 : KW + 3, :] * ggi_ref[0, here, :]
        )
        both_d = dot(g_buf[states, :], push_low[here], 1, 1)
        both_r = dot(h_ref[0, states, :], ggi_low[here], 1, 1)
        gdrive = jnp.zeros((N, T), f32)
        gread = jnp.zeros((N, T), f32)
        for j in range(T):
            gdrive = jnp.where(lanes == j, both_d[j * N : (j + 1) * N], gdrive)
            gread = jnp.where(lanes == j, both_r[j * N : (j + 1) * N], gread)
        gxt_ref[R : R + N, here] = gdrive
        gxt_ref[R + N :, here] = gread
    carried[...] = p
    total[...] = acc
    gxt_ref[0:R, :] = dot(dtw_ref[:, AT_DT : AT_DT + R], gsp_ref[0], 0, 1)
    galog_ref[...] = acc * a_now


def scan_backward(s, earlier, xt, act, dt, sp, ggi, chan, a_matrix, states, dtw):
    seqs, length, width = act.shape
    blocks = length // ROWS

    def back(b):
        return (s, blocks - 1 - b, 0)

    def before(b):
        return (s, jnp.maximum((blocks - 1 - b) * ROWS - 1, 0), 0)

    def flat(b):
        return (0, s * blocks + blocks - 1 - b)

    def fixed(b):
        return (0, 0)

    return pl.pallas_call(
        backward_kernel,
        grid=(blocks,),
        in_specs=[
            pl.BlockSpec((WIDE, ROWS), flat),
            pl.BlockSpec((1, ROWS, width), back),
            pl.BlockSpec((1, ROWS, width), back),
            pl.BlockSpec((1, ROWS, width), back),
            pl.BlockSpec((1, ROWS, width), back),
            pl.BlockSpec((8, width), fixed),
            pl.BlockSpec((N, width), fixed),
            pl.BlockSpec((1, ROWS * N, width), back),
            pl.BlockSpec((1, N, width), before),
            pl.BlockSpec((width, SMALL), fixed),
        ]
        + [pl.BlockSpec(memory_space=pl.ANY)] * len(earlier),
        out_specs=[
            pl.BlockSpec((1, ROWS, width), back),
            pl.BlockSpec((1, ROWS, width), back),
            pl.BlockSpec((WIDE, ROWS), flat),
            pl.BlockSpec((N, width), fixed),
        ],
        out_shape=[
            jax.ShapeDtypeStruct((seqs, length, width), bf16),
            jax.ShapeDtypeStruct((seqs, length, width), f32),
            jax.ShapeDtypeStruct((WIDE, seqs * length), f32),
            jax.ShapeDtypeStruct((N, width), f32),
        ],
        scratch_shapes=[
            pltpu.VMEM((N, width), f32),
            pltpu.VMEM((N, width), f32),
            pltpu.VMEM((ROWS * N, width), bf16),
            pltpu.VMEM((ROWS * N, width), bf16),
        ],
        input_output_aliases={10 + k: k for k in range(len(earlier))},
        compiler_params=params(60),
        cost_estimate=cost(16),
        name=f"scan_backward_{s}",
    )(xt, act, dt, sp, ggi, chan, a_matrix, states, states, dtw, *earlier)


def leave_kernel(
    gact_ref,
    gxt_ref,
    xt_ref,
    gsp_ref,
    wx_ref,
    pre_ref,
    conv_ref,
    act_ref,
    normed_ref,
    chan_ref,
    gskip_ref,
    *refs,
):
    galog_refs = refs[:-6]
    gci_ref, gin_ref, small_ref, padded, in_total, sums = refs[-6:]
    block = pl.program_id(1)
    rows = gact_ref.shape[1]
    start = (pl.program_id(0) == 0) & (block == 0)
    end = (pl.program_id(0) == pl.num_programs(0) - 1) & (block == pl.num_programs(1) - 1)

    @pl.when(start)
    def _():
        in_total[...] = jnp.zeros_like(in_total)
        small_ref[...] = jnp.zeros_like(small_ref)
        sums[...] = jnp.zeros_like(sums)

    @pl.when(block == 0)
    def _():
        padded[rows : rows + 8, :] = jnp.zeros((8, padded.shape[1]), f32)

    @pl.when(block > 0)
    def _():
        padded[rows : rows + 8, :] = padded[0:8, :]

    gxt = gxt_ref[...]
    act = act_ref[0]
    grad_act = gact_ref[0] + dot(gxt, wx_ref[:, 0:WIDE], 0, 1)
    pre = pre_ref[0]
    sig = jax.nn.sigmoid(pre)
    grad_conv = grad_act * (sig * (1.0 + pre * (1.0 - sig)))
    padded[0:rows, :] = grad_conv
    conv = conv_ref[0].astype(f32)
    gci = jnp.zeros_like(grad_conv)
    for k in range(KW):
        moved = padded[KW - 1 - k : KW - 1 - k + rows, :]
        gci = gci + chan_ref[k : k + 1, :] * moved
        sums[N + k : N + k + 1, :] += jnp.sum(conv * moved, axis=0, keepdims=True)
    sums[N + KW : N + KW + 1, :] += jnp.sum(grad_conv, axis=0, keepdims=True)
    gsp = gsp_ref[0]
    sums[N + KW + 1 : N + KW + 2, :] += jnp.sum(gsp.astype(f32), axis=0, keepdims=True)
    low = gci.astype(bf16)
    gci_ref[0] = low
    in_total[...] += dot(normed_ref[0], low, 0, 0)
    small_ref[:, 0:WIDE] += dot(act, gxt, 0, 1)
    small_ref[:, WIDE : WIDE + R] += dot(gsp, xt_ref[0:R, :], 0, 1)

    @pl.when(end)
    def _():
        gin_ref[...] = in_total[...].astype(bf16)
        sums[0:N, :] = sum(ref[...] for ref in galog_refs)
        sums[N + KW + 2 : N + KW + 3, :] = gskip_ref[...]
        small_ref[:, WIDE + R :] = sums[...].T


def leave(gact, gxt, xt, gsp, wx, pre, conv, act, normed, chan, gskip, galog):
    seqs, length, width = act.shape
    model = normed.shape[2]
    rows = min(BIG, length)
    blocks = length // rows

    def back(s, b):
        return (s, blocks - 1 - b, 0)

    def flat(s, b):
        return (0, s * blocks + blocks - 1 - b)

    def fixed(s, b):
        return (0, 0)

    return pl.pallas_call(
        leave_kernel,
        grid=(seqs, blocks),
        in_specs=[
            pl.BlockSpec((1, rows, width), back),
            pl.BlockSpec((WIDE, rows), flat),
            pl.BlockSpec((WIDE, rows), flat),
            pl.BlockSpec((1, rows, width), back),
            pl.BlockSpec((width, SMALL), fixed),
            pl.BlockSpec((1, rows, width), back),
            pl.BlockSpec((1, rows, width), back),
            pl.BlockSpec((1, rows, width), back),
            pl.BlockSpec((1, rows, model), back),
            pl.BlockSpec((8, width), fixed),
            pl.BlockSpec((1, width), fixed),
        ]
        + [pl.BlockSpec((N, width), fixed)] * len(galog),
        out_specs=[
            pl.BlockSpec((1, rows, width), back),
            pl.BlockSpec((model, width), fixed),
            pl.BlockSpec((width, GRADS), fixed),
        ],
        out_shape=[
            jax.ShapeDtypeStruct((seqs, length, width), bf16),
            jax.ShapeDtypeStruct((model, width), bf16),
            jax.ShapeDtypeStruct((width, GRADS), f32),
        ],
        scratch_shapes=[
            pltpu.VMEM((rows + 8, width), f32),
            pltpu.VMEM((model, width), f32),
            pltpu.VMEM((REST, width), f32),
        ],
        compiler_params=params(60),
        cost_estimate=cost(8),
        name="leave",
    )(gact, gxt, xt, gsp, wx, pre, conv, act, normed, chan, gskip, *galog)


def rows_back_kernel(me_ref, gci_ref, ggp_ref, w0_ref, w1_ref, *refs):
    part = refs[-1]
    part[...] = dot(gci_ref[0], w0_ref[...], 1, 1) + dot(ggp_ref[0], w1_ref[...], 1, 1)
    deal_pieces(refs[:-1], part, me_ref[0], pl.program_id(1))


def rows_back(me, gci, ggp, w0, w1, dps):
    seqs, length, width = gci.shape
    model = w0.shape[0]
    piece = length // dps
    rows = min(BIG, length)
    blocks = length // rows

    def at(s, b, me):
        return (s, b, 0)

    def fixed(s, b, me):
        return (0, 0)

    return pl.pallas_call(
        rows_back_kernel,
        grid_spec=pltpu.PrefetchScalarGridSpec(
            num_scalar_prefetch=1,
            grid=(seqs, blocks),
            in_specs=[
                pl.BlockSpec((1, rows, width), at),
                pl.BlockSpec((1, rows, width), at),
                pl.BlockSpec((model, width), fixed),
                pl.BlockSpec((model, width), fixed),
            ],
            out_specs=piece_specs(dps, piece, model),
            scratch_shapes=[pltpu.VMEM((rows, model), f32)],
        ),
        out_shape=piece_shapes(dps, seqs, piece, model, 2),
        compiler_params=params(60),
        cost_estimate=cost(5),
        name="rows_back",
    )(me, gci, ggp, w0, w1)


def finish_kernel(tok_ref, cot_ref, gain_ref, *refs):
    out_ref = refs[-1]
    grad = refs[0][0]
    for ref in refs[1:-1]:
        grad = grad + ref[0].astype(f32)
    x = tok_ref[0].astype(f32)
    inv = lax.rsqrt(jnp.mean(x * x, axis=-1, keepdims=True) + 1e-05)
    grad = grad * gain_ref[...]
    back = x * inv * inv * inv * jnp.mean(grad * x, axis=-1, keepdims=True)
    out_ref[0] = inv * grad - back + cot_ref[0].astype(f32)


def finish(tok, cot, gain, parts):
    seqs, piece, model = tok.shape
    rows = pl.BlockSpec((1, piece, model), lambda s: (s, 0, 0))
    return pl.pallas_call(
        finish_kernel,
        grid=(seqs,),
        in_specs=[rows, rows, pl.BlockSpec((1, model), lambda s: (0, 0))] + [rows] * len(parts),
        out_specs=rows,
        out_shape=jax.ShapeDtypeStruct(tok.shape, f32),
        compiler_params=params(60),
        cost_estimate=cost(3),
        name="finish",
    )(tok, cot, gain, *parts)


def collect_kernel(
    conv_ref, gate_ref, out_ref, small_ref, w_ref, gain_ref, gin_ref, gx_ref, gdt_ref, gchan_ref, galog_ref, ggain_ref, squares_ref, square
):
    own_in, columns = w_ref.shape
    width = conv_ref.shape[2]
    dps = columns // (2 * width)
    peers = conv_ref.shape[0] // dps
    own = small_ref.shape[0]
    total = jnp.zeros((1, 128), f32)

    def squares(x):
        x = jnp.sum(x * x, axis=0, keepdims=True)
        return jnp.sum(x, axis=1, keepdims=True)

    ggain = jnp.zeros((own_in, 1), f32)
    for half in range(2):
        for k in range(dps):
            parts = gate_ref if half else conv_ref
            grad = parts[k * peers].astype(f32)
            for j in range(1, peers):
                grad = grad + parts[k * peers + j].astype(f32)
            here = slice((half * dps + k) * width, (half * dps + k + 1) * width)
            gin_ref[:, here] = grad
            total = total + squares(grad)
            low = w_ref[:, here].astype(bf16).astype(f32)
            ggain = ggain + jnp.sum(grad * low, axis=1, keepdims=True)
    total = total + squares(out_ref[...])
    small = small_ref[...]
    total = total + squares(small)
    gx_ref[...] = small[:, :WIDE]
    square[...] = jnp.zeros_like(square)
    square[0:own, 0:GRADS] = small
    square[0:own_in, GRADS : GRADS + 1] = ggain
    turned = square[...].T
    gdt_ref[...] = turned[WIDE : WIDE + R, :own]
    galog_ref[...] = turned[WIDE + R : WIDE + R + N, :own]
    gchan_ref[...] = turned[WIDE + R + N : WIDE + R + N + KW + 3, :own]
    grad = turned[GRADS : GRADS + 1, :own_in] / gain_ref[...].astype(bf16).astype(f32)
    ggain_ref[...] = grad
    squares_ref[...] = total + squares(grad)


def collect(conv, gate, out, small, w, gain):
    own_in, columns = w.shape
    own = small.shape[0]
    shapes = [
        (own_in, columns),
        (own, WIDE),
        (R, own),
        (KW + 3, own),
        (N, own),
        (1, own_in),
        (1, 128),
    ]
    whole = pl.BlockSpec(memory_space=pltpu.VMEM)
    return pl.pallas_call(
        collect_kernel,
        in_specs=[whole] * 6,
        out_specs=[whole] * len(shapes),
        out_shape=[jax.ShapeDtypeStruct(shape, f32) for shape in shapes],
        scratch_shapes=[pltpu.VMEM((128, 256), f32)],
        compiler_params=params(16),
        cost_estimate=cost(3),
        name="collect",
    )(conv, gate, out, small, w, gain)


def adam_kernel(squares_ref, *refs):
    count = len(learn_rates)
    weights, moments, grads = refs[:count], refs[count : 2 * count], refs[2 * count : 3 * count]
    outs = refs[3 * count :]
    norm = jnp.sqrt(jnp.sum(squares_ref[...], axis=0)[:, 0:1])
    outs[2 * count][...] = norm
    factor = jnp.minimum(1.0, clip_limit / (norm + 1e-06))
    for place in range(count):
        rate = learn_rates[place]
        gradient = grads[place][...] * factor
        weight = weights[place][...]
        rows_first = len(moments[place].shape) == 3 and moments[place].shape[1] == 2
        at = (lambda k: (slice(None), k)) if rows_first else (lambda k: k)
        first = 0.9 * moments[place][at(0)] + 0.1 * gradient
        old = moments[place][at(1)]
        root = jnp.sqrt(0.95 * old * old + 0.05 * gradient * gradient)
        update = first / (1.0 - 0.9**STEP) / (root / (1.0 - 0.95**STEP) ** 0.5 + 1e-08)
        outs[2 * place][at(0)] = first
        outs[2 * place][at(1)] = root
        outs[2 * place + 1][...] = weight - rate * (update + 0.01 * weight)


def adam(squares, weights, moments, grads):
    shapes = []
    for weight, moment in zip(weights, moments):
        shapes.append(jax.ShapeDtypeStruct(moment.shape, f32))
        shapes.append(jax.ShapeDtypeStruct(weight.shape, f32))
    shapes.append(jax.ShapeDtypeStruct((1, 1), f32))
    whole = pl.BlockSpec(memory_space=pltpu.VMEM)
    return pl.pallas_call(
        adam_kernel,
        in_specs=[whole] * (1 + 3 * len(weights)),
        out_specs=[whole] * len(shapes),
        out_shape=shapes,
        compiler_params=params(16),
        cost_estimate=cost(4),
        name="adam",
    )(squares, *weights, *moments, *grads)


def shards(
    tokens,
    cotangent,
    in_weight,
    out_weight,
    xproj_weight,
    dtproj_weight,
    chan_params,
    a_log,
    norm_gain,
    in_moments,
    out_moments,
    xproj_moments,
    dtproj_moments,
    chan_moments,
    alog_moments,
    gain_moments,
):
    both = ("dp", "fsdp")
    dps = lax.axis_size("dp")
    fsdps = lax.axis_size("fsdp")
    depth = min(4, fsdps)
    near = fsdps // depth
    me = jnp.stack([lax.axis_index("dp"), lax.axis_index("fsdp")])
    batches, groups, piece, model = tokens.shape
    seqs = batches * groups
    length = piece * dps
    own_in = in_weight.shape[0]
    own = out_weight.shape[0]
    width = own * fsdps

    in_low = in_weight.astype(bf16).reshape(own_in, 2, dps, width).transpose(2, 1, 0, 3)
    gain_row = jnp.pad(norm_gain.astype(bf16)[None], ((0, 7), (0, width - own_in)))
    in_parts = jnp.concatenate(
        [in_low[:, 0], in_low[:, 1], jnp.broadcast_to(gain_row, (dps, 8, width))], axis=1
    )
    in_parts = lax.all_to_all(in_parts, "dp", 0, 0, tiled=True)
    small = jnp.concatenate(
        [
            xproj_weight.astype(bf16),
            jnp.zeros((own, AT_DT - WIDE), bf16),
            dtproj_weight.astype(bf16).T,
            a_log.astype(bf16).T,
            chan_params.astype(bf16).T,
            jnp.zeros((own, SMALL - AT_REST - N - KW - 3), bf16),
        ],
        axis=1,
    )
    fold = max(width // SMALL, 1)
    aligned = own_in % 16 == 0 and own % (16 * fold) == 0 and width % SMALL == 0
    if aligned:
        packed = jnp.concatenate(jnp.split(small, fold), axis=1)
    else:
        packed = small.reshape(-1, width)
    here = dps * own_in
    gain_rows = jnp.pad(in_parts[:, 2 * own_in], ((0, -dps % 16), (0, 0)))
    first = jnp.concatenate([in_parts[:, :own_in].reshape(here, width), gain_rows, packed])
    tok = parts_dp_far(tokens.reshape(seqs, piece, model))
    first, tok = lax.optimization_barrier((gather_far(first), tok))
    cot = parts_dp_far(after(cotangent.reshape(seqs, piece, model), first))
    tok = parts_dp_near(tok)
    first, cot = lax.optimization_barrier((gather_near(first), cot))

    def own_columns(parts):
        parts = parts.reshape(fsdps, dps, own_in, width)
        return parts.transpose(1, 0, 2, 3).reshape(model, width)

    if aligned:
        w_conv, small, gain, a_matrix, chan = assemble(
            assemble_first_kernel,
            "assemble_first",
            me,
            first,
            [
                ((model, width), bf16),
                ((width, SMALL), bf16),
                ((1, model), f32),
                ((N, width), f32),
                ((8, width), f32),
            ],
            [pltpu.VMEM((model // own_in, 128), f32)],
        )
    else:
        merged = merge_near(first)
        w_conv = own_columns(merged[:, :here])
        gain = merged[:, here : here + dps, :own_in].transpose(1, 0, 2)
        gain = gain.reshape(1, model).astype(f32)
        small = merged[:, here + dps + -dps % 16 :].reshape(width, SMALL)
        rest = small[:, AT_REST : AT_REST + REST].astype(f32).T
        a_matrix = -jnp.exp(rest[:N])
        chan = rest[N : N + 8]

    out_low = out_weight.astype(bf16).reshape(own, model // width, width).transpose(1, 0, 2)
    second = [
        in_parts[:, own_in : 2 * own_in].reshape(here, width),
        out_low.reshape(-1, width),
    ]
    far = gather_far(jnp.concatenate(second))
    normed, conv, pre, act, xt = enter(me, gain, w_conv, chan, small, tok)
    cot = parts_dp_near(cot)
    xt, far = lax.optimization_barrier((xt, far))
    xt = sum_dp_near(xt)
    xt, far = lax.optimization_barrier((xt, far))
    second = gather_near(far)
    xt = sum_dp_far(xt)
    if aligned:
        w_gate, w_out = assemble(
            assemble_second_kernel,
            "assemble_second",
            me,
            second,
            [((model, width), bf16), ((width, model), bf16)],
            [],
        )
    else:
        merged = merge_near(second)
        w_gate = own_columns(merged[:, :here])
        w_out = merged[:, here:].reshape(fsdps, model // width, own, width)
        w_out = w_out.transpose(0, 2, 1, 3).reshape(width, model)
    gate_in, states, dt, step_pre = scan_forward(xt, act, small, chan, a_matrix)
    outs = middle(me, gate_in, act, normed, w_gate, w_out, cot, near, depth)
    part, gout = outs[:dps], outs[dps : dps + near]
    ggi, ggp, gin_gate, gskip = outs[dps + near :]
    gate_parts = lax.all_to_all(gin_gate.reshape(-1, own_in, width), both, 0, 0, tiled=True)
    gout_near = reduce_near(gout)
    out_rows = send_dp(part)

    back = ()
    galog = []
    for s in reversed(range(seqs)):
        *back, one = scan_backward(s, back, xt, act, dt, step_pre, ggi, chan, a_matrix, states, small)
        galog.append(one)
        if s == seqs - 1:
            ggi, gout_near = lax.optimization_barrier((ggi, gout_near))
    gsp, gact, gxt = back
    gout_far = send_far(gout_near)
    gxt, out_rows, gout_far = lax.optimization_barrier((gxt, out_rows, gout_far))
    gxt = sum_dp_far(sum_dp_near(gxt))
    gxt, gate_parts = lax.optimization_barrier((gxt, gate_parts))
    gci, gin_conv, small_grad = leave(
        gact, gxt, xt, gsp, small, pre, conv, act, normed, chan, gskip, galog
    )
    conv_parts = lax.all_to_all(gin_conv.reshape(-1, own_in, width), both, 0, 0, tiled=True)
    grad_out = sum(part.astype(f32) for part in gout_far)
    out_rows = sum(part.astype(f32) for part in out_rows).reshape(tokens.shape)
    block_output = (tokens.astype(f32) + out_rows).astype(bf16)
    small_near = reduce_near(split_near(small_grad.reshape(fsdps, own, GRADS)))
    part_back = rows_back(me, gci, ggp, w_conv, w_gate, dps)
    small_near, part_back = lax.optimization_barrier((small_near, part_back))
    own_small = sum(part.astype(f32) for part in send_far(small_near))
    part_back = send_dp_far(reduce_dp_near(part_back))

    def flat2(x):
        return x.reshape(x.shape[:-1] + (1, x.shape[-1]))

    grad_in, grad_x, grad_dt, grad_chan, grad_alog, grad_gain, squares = collect(
        conv_parts, gate_parts, grad_out, own_small, in_weight, flat2(norm_gain)
    )
    grad_normed = sum(part.astype(f32) for part in after(part_back, squares)).reshape(tokens.shape)

    input_grad = finish(
        tokens.reshape(seqs, piece, model),
        cotangent.reshape(seqs, piece, model),
        gain,
        after(part_back, squares),
    ).reshape(tokens.shape)
    squares = lax.all_to_all(
        jnp.broadcast_to(squares[None], (dps * fsdps, 1, 128)), both, 0, 0, tiled=True
    )
    weights = (in_weight, out_weight, xproj_weight, dtproj_weight, chan_params, a_log, flat2(norm_gain))
    moments = (
        in_moments,
        out_moments,
        xproj_moments,
        dtproj_moments,
        chan_moments.transpose(1, 0, 2),
        alog_moments,
        flat2(gain_moments),
    )
    grads = (grad_in, grad_out, grad_x, grad_dt, grad_chan, grad_alog, grad_gain)
    updated = list(adam(squares, weights, moments, grads))
    grad_norm = updated.pop().reshape(())
    updated[8] = updated[8].transpose(1, 0, 2)
    updated[-2] = updated[-2].reshape(gain_moments.shape)
    updated[-1] = updated[-1].reshape(norm_gain.shape)
    return (block_output, input_grad, grad_norm) + tuple(updated)


def solution(mesh):
    both = ("dp", "fsdp")
    row_specs = (P(None, "fsdp", "dp", None),) * 2
    weight_specs = (
        P(both, None),
        P(both, None),
        P(both, None),
        P(None, both),
        P(None, both),
        P(None, both),
        P(both),
    )
    moment_specs = (
        P(None, both, None),
        P(None, both, None),
        P(None, both, None),
        P(None, None, both),
        P(None, None, both),
        P(None, None, both),
        P(None, both),
    )
    updated = tuple(spec for pair in zip(moment_specs, weight_specs) for spec in pair)
    return jax.shard_map(
        shards,
        mesh=mesh,
        in_specs=row_specs + weight_specs + moment_specs,
        out_specs=row_specs + (P(),) + updated,
        check_vma=False,
    )
```

profile of v0, /device:TPU:0, one launch (start us, length us, event | category | flops | bytes accessed | tf_op | source)
XLA Modules:
  0.0 230.4 jit_solution(14987019987723226771)
XLA Ops:
  0.7 0.7 convert_bitcast_fusion.1
  1.4 1.1 convert_element_type.111
  3.1 0.8 copy.73
  3.8 4.2 %all-to-all-start = ((bf16[4,72,512]{2,1,0:T(8,128)(2,1)}), bf16[4,72,512]{2,1,0:T(8,128)(2,1)S(1)}, u32[]{:S(2)}, u32[]{:S(2)}) async-start(bf16[4,72,512]{2,1,0:T(8,128)(2,1)} %copy.73), calls=%async_computation | async-start | bytes 589824 | tf_op jit(solution)/shard_map/all_to_all | solution.py:1001
  8.1 2.3 collective-permute-start.3
  10.8 4.3 %all-to-all-done = bf16[4,72,512]{2,1,0:T(8,128)(2,1)S(1)} async-done(((bf16[4,72,512]{2,1,0:T(8,128)(2,1)}), bf16[4,72,512]{2,1,0:T(8,128)(2,1)S(1)}, u32[]{:S(2)}, u32[]{:S(2)}) %all-to-all-start) | async-done | bytes 294944 | tf_op jit(solution)/shard_map/all_to_all | solution.py:1001
  15.1 4.1 %collective-permute-start.2 = (bf16[176,512]{1,0:T(8,128)(2,1)S(1)}, bf16[176,512]{1,0:T(8,128)(2,1)S(1)}, u32[]{:S(2)}, u32[]{:S(2)}) collective-permute-start(bf16[176,512]{1,0:T(8,128)(2,1)S(1)} %fusion.6), channel_id=1, source_target_pairs={{0,6},{1,7},{2,4},{3,5},{4,2},{5,3},{6,0},{7,1},{8,14},{9,15},{10,... | collective-permute-start | bytes 540680 | tf_op jit(solution)/shard_map/ppermute | solution.py:45
  19.9 4.9 %collective-permute-done.2 = bf16[176,512]{1,0:T(8,128)(2,1)S(1)} collective-permute-done((bf16[176,512]{1,0:T(8,128)(2,1)S(1)}, bf16[176,512]{1,0:T(8,128)(2,1)S(1)}, u32[]{:S(2)}, u32[]{:S(2)}) %collective-permute-start.2) | collective-permute-done | bytes 180256 | tf_op jit(solution)/shard_map/ppermute | solution.py:45
  24.8 9.1 %collective-permute-done.1 = bf16[176,512]{1,0:T(8,128)(2,1)S(1)} collective-permute-done((bf16[176,512]{1,0:T(8,128)(2,1)S(1)}, bf16[176,512]{1,0:T(8,128)(2,1)S(1)}, u32[]{:S(2)}, u32[]{:S(2)}) %collective-permute-start.1) | collective-permute-done | bytes 180256 | tf_op jit(solution)/shard_map/ppermute | solution.py:45
  33.9 0.8 copy-done.30
  34.8 1.6 collective-permute-start.4
  37.6 2.5 %collective-permute-start.10 = (bf16[256,512]{1,0:T(8,128)(2,1)S(1)}, bf16[256,512]{1,0:T(8,128)(2,1)}, u32[]{:S(2)}, u32[]{:S(2)}) collective-permute-start(bf16[256,512]{1,0:T(8,128)(2,1)S(1)} %pad_maximum_fusion.3), channel_id=1, source_target_pairs={{0,6},{1,7},{2,4},{3,5},{4,2},{5,3},{6,0},{7,1},{8,14},{9,15},{10,... | collective-permute-start | bytes 786440 | tf_op jit(solution)/shard_map/ppermute | solution.py:45
  40.1 8.9 %collective-permute-done.5.refs_2_ = bf16[2,128,1024]{2,1,0:T(8,128)(2,1)S(1)} collective-permute-done((bf16[2,128,1024]{2,1,0:T(8,128)(2,1)S(1)}, bf16[2,128,1024]{2,1,0:T(8,128)(2,1)S(1)}, u32[]{:S(2)}, u32[]{:S(2)}) %collective-permute-start.5) | collective-permute-done | bytes 524320 | tf_op jit(solution)/shard_map/ppermute | solution.py:45
  49.0 3.0 %collective-permute-done.4.refs_1_ = bf16[4,176,512]{2,1,0:T(8,128)(2,1)S(1)} collective-permute-done((bf16[4,176,512]{2,1,0:T(8,128)(2,1)S(1)}, bf16[4,176,512]{2,1,0:T(8,128)(2,1)S(1)}, u32[]{:S(2)}, u32[]{:S(2)}) %collective-permute-start.4) | collective-permute-done | bytes 720928 | tf_op jit(solution)/shard_map/ppermute | solution.py:45
  52.9 2.5 %assemble_first.1 = (bf16[1024,512]{1,0:T(8,128)(2,1)}, bf16[512,256]{1,0:T(8,128)(2,1)}, f32[1,1024]{1,0:T(1,128)}, f32[16,512]{1,0:T(8,128)}, f32[8,512]{1,0:T(8,128)}) custom-call(s32[2]{0:T(128)} %pad_add_fusion.me_ref, bf16[4,176,512]{2,1,0:T(8,128)(2,1)} %copy-done.19, bf16[4,176,512]{2,1,0:T(8,128)(2,1)} %copy-done.24), custom_call_target="tpu_custom_call" | custom-call | flops 160000000 | bytes 600000 | tf_op jit(solution)/shard_map/assemble_first/pallas_call | solution.py:218
  55.4 7.9 %enter.1 = (bf16[2,512,1024]{2,1,0:T(8,128)(2,1)}, bf16[2,512,512]{2,1,0:T(8,128)(2,1)}, f32[2,512,512]{2,1,0:T(8,128)}, bf16[2,512,512]{2,1,0:T(8,128)(2,1)}, f32[96,1024]{1,0:T(8,128)}) custom-call(s32[2]{0:T(128)} %pad_add_fusion.me_ref, f32[1,1024]{1,0:T(1,128)} %get-tuple-element.128.gain_ref, bf16[1024,512]{1,0:T(8,128)(2,1)} %get-tuple-element.129.w_ref.w0_ref, ...), custom_call_target="tpu_custom_call" | custom-call | flops 560000000 | bytes 2100000 | tf_op jit(solution)/shard_map/enter/pallas_call | solution.py:302
  63.4 0.7 collective-permute-done.8
  64.1 1.0 slice_select_fusion.1
  65.3 1.4 collective-permute-done.11
  66.7 1.1 select_add_fusion.1
  67.7 1.2 pad_maximum_fusion.refs_0_
  69.0 1.4 collective-permute-start.14
  70.4 0.8 collective-permute-start.12
  71.8 5.3 %collective-permute-done.12 = f32[48,1024]{1,0:T(8,128)S(1)} collective-permute-done((f32[48,1024]{1,0:T(8,128)S(1)}, f32[48,1024]{1,0:T(8,128)S(1)}, u32[]{:S(2)}, u32[]{:S(2)}) %collective-permute-start.12) | collective-permute-done | bytes 196640 | tf_op jit(solution)/shard_map/ppermute | solution.py:45
  77.2 1.3 collective-permute-done.13
  79.2 14.9 %scan_forward.1 = (f32[2,512,512]{2,1,0:T(8,128)}, bf16[2,8192,512]{2,1,0:T(8,128)(2,1)}, f32[2,512,512]{2,1,0:T(8,128)}, f32[2,512,512]{2,1,0:T(8,128)}) custom-call(bf16[96,1024]{1,0:T(8,128)(2,1)} %bitcast.108, bf16[2,512,512]{2,1,0:T(8,128)(2,1)} %get-tuple-element.141.act_ref, bf16[512,256]{1,0:T(8,128)(2,1)} %get-tuple-element.131.wx_ref.dtw_ref, ...), custom_call_target="tpu_custom_call" | custom-call | flops 1440000000 | bytes 5400000 | tf_op jit(solution)/shard_map/scan_forward/pallas_call | solution.py:397
  94.3 1.0 copy-done.21
  95.2 3.0 %assemble_second.1 = (bf16[1024,512]{1,0:T(8,128)(2,1)}, bf16[512,1024]{1,0:T(8,128)(2,1)}) custom-call(s32[2]{0:T(128)} %pad_add_fusion.me_ref, bf16[4,256,512]{2,1,0:T(8,128)(2,1)} %copy-done.18, bf16[4,256,512]{2,1,0:T(8,128)(2,1)} %copy-done.21), custom_call_target="tpu_custom_call" | custom-call | flops 160000000 | bytes 600000 | tf_op jit(solution)/shard_map/assemble_second/pallas_call | solution.py:218
  98.3 14.4 %middle.1 = (f32[2,128,1024]{2,1,0:T(8,128)}, bf16[2,128,1024]{2,1,0:T(8,128)(2,1)}, bf16[2,128,1024]{2,1,0:T(8,128)(2,1)}, bf16[2,128,1024]{2,1,0:T(8,128)(2,1)...) custom-call(s32[2]{0:T(128)} %pad_add_fusion.me_ref, ...), custom_call_target="tpu_custom_call" | custom-call | flops 720000000 | bytes 2700000 | tf_op jit(solution)/shard_map/middle/pallas_call | solution.py:502
  112.7 1.4 collective-permute-start.17
  114.2 2.8 %all-to-all-start.1 = ((bf16[32,32,512]{2,1,0:T(8,128)(2,1)}), bf16[32,32,512]{2,1,0:T(8,128)(2,1)S(1)}, u32[]{:S(2)}, u32[]{:S(2)}) async-start(bf16[32,32,512]{2,1,0:T(8,128)(2,1)} %bitcast.120), calls=%async_computation.1 | async-start | bytes 2097152 | tf_op jit(solution)/shard_map/all_to_all | solution.py:1088
  117.1 1.6 collective-permute-start.19
  118.9 14.3 %scan_backward_1.1 = (bf16[2,512,512]{2,1,0:T(8,128)(2,1)}, f32[2,512,512]{2,1,0:T(8,128)}, f32[96,1024]{1,0:T(8,128)}, f32[16,512]{1,0:T(8,128)}) custom-call(bf16[96,1024]{1,0:T(8,128)(2,1)} %bitcast.109, bf16[2,512,512]{2,1,0:T(8,128)(2,1)} %get-tuple-element.141.act_ref, f32[2,512,512]{2,1,0:T(8,128)} %get-tuple-element.143.dt_ref, ...), custom_call_target="tpu_custom_call" | custom-call | flops 1280000000 | bytes 4800000 | tf_op jit(solution)/shard_map/scan_backward_1/pallas_call | solution.py:632
  133.2 2.3 collective-permute-done.17
  135.5 0.8 copy-done.31
  136.3 1.4 convert_add_fusion.1
  137.8 0.7 slice_bitcast_fusion.1
  138.5 1.1 collective-permute-start.23
  139.7 3.2 %collective-permute-start.21 = (bf16[64,1024]{1,0:T(8,128)(2,1)}, bf16[64,1024]{1,0:T(8,128)(2,1)S(1)}, u32[]{:S(2)}, u32[]{:S(2)}) collective-permute-start(bf16[64,1024]{1,0:T(8,128)(2,1)} %get-tuple-element.295), channel_id=1, source_target_pairs={{0,2},{1,3},{2,0},{3,1},{4,6},{5,7},{6,4},{7,5},{8,10},{9,11},{10,... | collective-permute-start | bytes 393224 | tf_op jit(solution)/shard_map/ppermute | solution.py:45
  142.9 0.7 slice_bitcast_fusion
  143.6 14.2 %scan_backward_0.1 = (bf16[2,512,512]{2,1,0:T(8,128)(2,1)}, f32[2,512,512]{2,1,0:T(8,128)}, f32[96,1024]{1,0:T(8,128)}, f32[16,512]{1,0:T(8,128)}) custom-call(bf16[96,1024]{1,0:T(8,128)(2,1)} %bitcast.110, bf16[2,512,512]{2,1,0:T(8,128)(2,1)} %get-tuple-element.141.act_ref, ...), custom_call_target="tpu_custom_call", output_to_operand_aliasing={{0}: (10, {}), {1}: (11, {}), {2}: (12, {})} | custom-call | flops 1280000000 | bytes 4800000 | tf_op jit(solution)/shard_map/scan_backward_0/pallas_call | solution.py:632
  158.6 1.0 slice_select_fusion
  159.8 1.4 collective-permute-done.24
  161.2 1.1 select_add_fusion
  162.9 6.3 %collective-permute-done.25 = f32[48,1024]{1,0:T(8,128)S(1)} collective-permute-done((f32[48,1024]{1,0:T(8,128)S(1)}, f32[48,1024]{1,0:T(8,128)S(1)}, u32[]{:S(2)}, u32[]{:S(2)}) %collective-permute-start.25) | collective-permute-done | bytes 196640 | tf_op jit(solution)/shard_map/ppermute | solution.py:45
  169.4 1.3 collective-permute-done.26
  171.4 10.3 %leave.1 = (bf16[2,512,512]{2,1,0:T(8,128)(2,1)}, bf16[1024,512]{1,0:T(8,128)(2,1)}, f32[512,192]{1,0:T(8,128)}) custom-call(f32[2,512,512]{2,1,0:T(8,128)} %get-tuple-element.173.gact_ref, bf16[96,1024]{1,0:T(8,128)(2,1)} %bitcast.125, bf16[96,1024]{1,0:T(8,128)(2,1)} %bitcast.111, bf16[2,512,512]{2,1,0:T(8,128)(2,1)} %get-tuple-element.177.gsp_ref, ...), custom_call_target="tpu_custom_call" | custom-call | flops 640000000 | bytes 2400000 | tf_op jit(solution)/shard_map/leave/pallas_call | solution.py:753
  181.7 3.6 %all-to-all-start.2 = ((bf16[32,32,512]{2,1,0:T(8,128)(2,1)}), bf16[32,32,512]{2,1,0:T(8,128)(2,1)S(1)}, u32[]{:S(2)}, u32[]{:S(2)}) async-start(bf16[32,32,512]{2,1,0:T(8,128)(2,1)} %bitcast.121), calls=%async_computation.2 | async-start | bytes 2097152 | tf_op jit(solution)/shard_map/all_to_all | solution.py:1107
  186.2 1.6 collective-permute-start.27
  187.8 6.7 %rows_back.1 = (f32[2,128,1024]{2,1,0:T(8,128)}, bf16[2,128,1024]{2,1,0:T(8,128)(2,1)}, f32[2,128,1024]{2,1,0:T(8,128)}, bf16[2,128,1024]{2,1,0:T(8,128)(2,1)}) custom-call(s32[2]{0:T(128)} %pad_add_fusion.me_ref, bf16[2,512,512]{2,1,0:T(8,128)(2,1)} %get-tuple-element.184.gci_ref, bf16[2,512,512]{2,1,0:T(8,128)(2,1)} %get-tuple-element.185.ggp_ref, ...), custom_call_target="tpu_custom_call" | custom-call | flops 400000000 | bytes 1500000 | tf_op jit(solution)/shard_map/rows_back/pallas_call | solution.py:810
  194.5 6.7 %collective-permute-done.27 = bf16[4,64,192]{2,1,0:T(8,128)(2,1)} collective-permute-done((bf16[4,64,192]{2,1,0:T(8,128)(2,1)}, bf16[4,64,192]{2,1,0:T(8,128)(2,1)}, u32[]{:S(2)}, u32[]{:S(2)}) %collective-permute-start.27) | collective-permute-done | bytes 98336 | tf_op jit(solution)/shard_map/ppermute | solution.py:45
  201.3 0.9 fusion.4
  202.3 3.0 %fusion.1 = bf16[2,1,128,1024]{3,2,1,0:T(8,128)(2,1)} fusion(bf16[2,128,1024]{2,1,0:T(8,128)(2,1)} %collective-permute-done.20, bf16[2,128,1024]{2,1,0:T(8,128)(2,1)} %copy-done.26, f32[2,128,1024]{2,1,0:T(8,128)} %get-tuple-element.169, bf16[2,128,1024]{2,1,0:T(8,128)(2,1)} %copy-done.25, bf16[2,1,128,1024]{3,2,1,0:T(8,128)(2,1)S(1)} %copy-done.17), kind=kLoop, calls=%fused_computation.12 | loop fusion | flops 2359296 | bytes 3670016
  205.4 1.4 collective-permute-start.33
  206.8 2.1 collective-permute-start.32
  208.9 0.9 add_convert_fusion
  209.8 1.5 collective-permute-start.30
  211.4 2.7 %collective-permute-done.32 = bf16[64,192]{1,0:T(8,128)(2,1)S(1)} collective-permute-done((bf16[64,192]{1,0:T(8,128)(2,1)S(1)}, bf16[64,192]{1,0:T(8,128)(2,1)S(1)}, u32[]{:S(2)}, u32[]{:S(2)}) %collective-permute-start.32) | collective-permute-done | bytes 24608 | tf_op jit(solution)/shard_map/ppermute | solution.py:45
  214.8 0.8 copy-done.4
  216.2 3.7 %all-to-all-start.3 = ((f32[32,1,128]{2,1,0:T(1,128)}), f32[32,1,128]{2,1,0:T(1,128)S(1)}, u32[]{:S(2)}, u32[]{:S(2)}) async-start(f32[32,1,128]{2,1,0:T(1,128)} %broadcast_in_dim.25), calls=%async_computation.3 | async-start | bytes 32768 | tf_op jit(solution)/shard_map/all_to_all | solution.py:1131
  219.9 2.5 %convert_add_fusion.refs_0_ = f32[2,128,1024]{2,1,0:T(8,128)} fusion(f32[2,128,1024]{2,1,0:T(8,128)} %get-tuple-element.190, bf16[2,128,1024]{2,1,0:T(8,128)(2,1)} %collective-permute-done.28), kind=kLoop, calls=%fused_computation.4 | loop fusion | flops 524288 | bytes 2621440 | tf_op jit(solution)/shard_map/add | solution.py:95
  222.5 2.4 %collective-permute-done.30.refs_1_ = bf16[2,128,1024]{2,1,0:T(8,128)(2,1)} collective-permute-done((bf16[2,128,1024]{2,1,0:T(8,128)(2,1)}, bf16[2,128,1024]{2,1,0:T(8,128)(2,1)}, u32[]{:S(2)}, u32[]{:S(2)}) %collective-permute-start.30) | collective-permute-done | bytes 524320 | tf_op jit(solution)/shard_map/ppermute | solution.py:45
  224.9 2.8 %finish.1 = f32[2,128,1024]{2,1,0:T(8,128)} custom-call(bf16[2,128,1024]{2,1,0:T(8,128)(2,1)} %bitcast.105, bf16[2,128,1024]{2,1,0:T(8,128)(2,1)} %bitcast.113, f32[1,1024]{1,0:T(1,128)} %get-tuple-element.128.gain_ref, f32[2,128,1024]{2,1,0:T(8,128)} %convert_add_fusion.refs_0_, bf16[2,128,1024]{2,1,0:T(8,128)(2,1)} %collective-permute-done.30.refs_1_), custom_call_target="tpu_custom_call" | custom-call | flops 240000000 | bytes 900000 | tf_op jit(solution)/shard_map/finish/pallas_call | solution.py:846
  227.8 2.5 %adam.1 = (f32[2,32,4096]{2,1,0:T(8,128)}, f32[32,4096]{1,0:T(8,128)}, f32[2,64,1024]{2,1,0:T(8,128)}, f32[64,1024]{1,0:T(8,128)}, f32[2,64,96]{2,1,0:T(8,128)},...) custom-call(f32[32,1,128]{2,1,0:T(1,128)S(1)} %all-to-all-done.3.squ, ...), custom_call_target="tpu_custom_call" | custom-call | flops 320000000 | bytes 1200000 | tf_op jit(solution)/shard_map/adam/pallas_call | solution.py:954
  (153 shorter events, 10.4 us)
Async XLA Ops:
  0.7 7.4 %copy-start.16 = (bf16[2,1,128,1024]{3,2,1,0:T(8,128)(2,1)S(1)}, bf16[2,1,128,1024]{3,2,1,0:T(8,128)(2,1)}, u32[]{:S(2)}) copy-start(bf16[2,1,128,1024]{3,2,1,0:T(8,128)(2,1)} %param.16) | copy-start | bytes 1572868
  0.7 9.6 %copy-start.12 = (f32[7,64]{1,0:T(8,128)S(1)}, f32[7,64]{1,0:T(8,128)}, u32[]{:S(2)}) copy-start(f32[7,64]{1,0:T(8,128)} %refs_4_.1) | copy-start | bytes 5380
  0.7 9.6 %copy-start.10 = (f32[16,64]{1,0:T(8,128)S(1)}, f32[16,64]{1,0:T(8,128)}, u32[]{:S(2)}) copy-start(f32[16,64]{1,0:T(8,128)} %refs_5_.1) | copy-start | bytes 12292
  0.7 9.9 %copy-start.6 = (f32[64,96]{1,0:T(8,128)S(1)}, f32[64,96]{1,0:T(8,128)}, u32[]{:S(2)}) copy-start(f32[64,96]{1,0:T(8,128)} %refs_2_.1) | copy-start | bytes 73732
  0.7 9.9 %copy-start.7 = (f32[64,64]{1,0:T(8,128)S(1)}, f32[64,64]{1,0:T(8,128)}, u32[]{:S(2)}) copy-start(f32[64,64]{1,0:T(8,128)} %refs_3_.1) | copy-start | bytes 49156
  3.0 33.4 %copy-start.20 = (bf16[2,1,128,1024]{3,2,1,0:T(8,128)(2,1)S(1)}, bf16[2,1,128,1024]{3,2,1,0:T(8,128)(2,1)}, u32[]{:S(2)}) copy-start(bf16[2,1,128,1024]{3,2,1,0:T(8,128)(2,1)} %param.17) | copy-start | bytes 1572868
  3.0 34.5 %copy-start.1 = (f32[64,1024]{1,0:T(8,128)S(1)}, f32[64,1024]{1,0:T(8,128)}, u32[]{:S(2)}) copy-start(f32[64,1024]{1,0:T(8,128)} %refs_1_.1) | copy-start | bytes 786436
  3.8 11.3 %all-to-all-start = ((bf16[4,72,512]{2,1,0:T(8,128)(2,1)}), bf16[4,72,512]{2,1,0:T(8,128)(2,1)S(1)}, u32[]{:S(2)}, u32[]{:S(2)}) async-start(bf16[4,72,512]{2,1,0:T(8,128)(2,1)} %copy.73), calls=%async_computation | async-start | bytes 589824 | tf_op jit(solution)/shard_map/all_to_all | solution.py:1001
  8.1 25.9 %collective-permute-start.3 = (bf16[2,128,1024]{2,1,0:T(8,128)(2,1)S(1)}, bf16[2,128,1024]{2,1,0:T(8,128)(2,1)S(1)}, u32[]{:S(2)}, u32[]{:S(2)}) collective-permute-start(bf16[2,128,1024]{2,1,0:T(8,128)(2,1)S(1)} %bitcast.106), channel_id=1, source_target_pairs={{0,16},{8,24},{16,0},{24,8},{1,17},{9,25},{17,1},{25,9},{2,18},{10... | collective-permute-start | bytes 1572872 | tf_op jit(solution)/shard_map/ppermute | solution.py:45
  15.1 9.7 %collective-permute-start.2 = (bf16[176,512]{1,0:T(8,128)(2,1)S(1)}, bf16[176,512]{1,0:T(8,128)(2,1)S(1)}, u32[]{:S(2)}, u32[]{:S(2)}) collective-permute-start(bf16[176,512]{1,0:T(8,128)(2,1)S(1)} %fusion.6), channel_id=1, source_target_pairs={{0,6},{1,7},{2,4},{3,5},{4,2},{5,3},{6,0},{7,1},{8,14},{9,15},{10,... | collective-permute-start | bytes 540680 | tf_op jit(solution)/shard_map/ppermute | solution.py:45
  19.3 14.6 %collective-permute-start.1 = (bf16[176,512]{1,0:T(8,128)(2,1)S(1)}, bf16[176,512]{1,0:T(8,128)(2,1)S(1)}, u32[]{:S(2)}, u32[]{:S(2)}) collective-permute-start(bf16[176,512]{1,0:T(8,128)(2,1)S(1)} %fusion.6), channel_id=1, source_target_pairs={{0,4},{1,5},{2,6},{3,7},{4,0},{5,1},{6,2},{7,3},{8,12},{9,13},{10,... | collective-permute-start | bytes 540680 | tf_op jit(solution)/shard_map/ppermute | solution.py:45
  19.3 14.6 %collective-permute-start = (bf16[176,512]{1,0:T(8,128)(2,1)S(1)}, bf16[176,512]{1,0:T(8,128)(2,1)S(1)}, u32[]{:S(2)}, u32[]{:S(2)}) collective-permute-start(bf16[176,512]{1,0:T(8,128)(2,1)S(1)} %fusion.6), channel_id=1, source_target_pairs={{0,2},{1,3},{2,0},{3,1},{4,6},{5,7},{6,4},{7,5},{8,10},{9,11},{10,... | collective-permute-start | bytes 540680 | tf_op jit(solution)/shard_map/ppermute | solution.py:45
  34.8 17.9 %copy-start.19 = (bf16[4,176,512]{2,1,0:T(8,128)(2,1)}, bf16[4,176,512]{2,1,0:T(8,128)(2,1)S(1)}, u32[]{:S(2)}) copy-start(bf16[4,176,512]{2,1,0:T(8,128)(2,1)S(1)} %pad_maximum_fusion.1.refs_0_) | copy-start | bytes 2162692
  34.8 17.2 %collective-permute-start.4 = (bf16[4,176,512]{2,1,0:T(8,128)(2,1)S(1)}, bf16[4,176,512]{2,1,0:T(8,128)(2,1)S(1)}, u32[]{:S(2)}, u32[]{:S(2)}) collective-permute-start(bf16[4,176,512]{2,1,0:T(8,128)(2,1)S(1)} %pad_maximum_fusion.1.refs_0_), channel_id=1, source_target_pairs={{0,1},{1,0},{2,3},{3,2},{4,5},{5,4},{6,7},{7,6},{8,9},{9,8},{10,11... | collective-permute-start | bytes 2162696 | tf_op jit(solution)/shard_map/ppermute | solution.py:45
  36.4 12.6 %collective-permute-start.5 = (bf16[2,128,1024]{2,1,0:T(8,128)(2,1)S(1)}, bf16[2,128,1024]{2,1,0:T(8,128)(2,1)S(1)}, u32[]{:S(2)}, u32[]{:S(2)}) collective-permute-start(bf16[2,128,1024]{2,1,0:T(8,128)(2,1)S(1)} %bitcast.114), channel_id=1, source_target_pairs={{0,16},{8,24},{16,0},{24,8},{1,17},{9,25},{17,1},{25,9},{2,18},{10... | collective-permute-start | bytes 1572872 | tf_op jit(solution)/shard_map/ppermute | solution.py:45
  37.0 18.4 %collective-permute-start.6 = (bf16[2,128,1024]{2,1,0:T(8,128)(2,1)S(1)}, bf16[2,128,1024]{2,1,0:T(8,128)(2,1)}, u32[]{:S(2)}, u32[]{:S(2)}) collective-permute-start(bf16[2,128,1024]{2,1,0:T(8,128)(2,1)S(1)} %bitcast.107), channel_id=1, source_target_pairs={{0,8},{8,0},{16,24},{24,16},{1,9},{9,1},{17,25},{25,17},{2,10},{10... | collective-permute-start | bytes 1572872 | tf_op jit(solution)/shard_map/ppermute | solution.py:45
  37.0 18.4 %collective-permute-start.7 = (bf16[2,128,1024]{2,1,0:T(8,128)(2,1)}, bf16[2,128,1024]{2,1,0:T(8,128)(2,1)}, u32[]{:S(2)}, u32[]{:S(2)}) collective-permute-start(bf16[2,128,1024]{2,1,0:T(8,128)(2,1)} %copy-done.30), channel_id=1, source_target_pairs={{0,8},{8,0},{16,24},{24,16},{1,9},{9,1},{17,25},{25,17},{2,10},{10... | collective-permute-start | bytes 1572872 | tf_op jit(solution)/shard_map/ppermute | solution.py:45
  37.6 25.8 %collective-permute-start.10 = (bf16[256,512]{1,0:T(8,128)(2,1)S(1)}, bf16[256,512]{1,0:T(8,128)(2,1)}, u32[]{:S(2)}, u32[]{:S(2)}) collective-permute-start(bf16[256,512]{1,0:T(8,128)(2,1)S(1)} %pad_maximum_fusion.3), channel_id=1, source_target_pairs={{0,6},{1,7},{2,4},{3,5},{4,2},{5,3},{6,0},{7,1},{8,14},{9,15},{10,... | collective-permute-start | bytes 786440 | tf_op jit(solution)/shard_map/ppermute | solution.py:45
  49.0 14.4 %collective-permute-start.9 = (bf16[256,512]{1,0:T(8,128)(2,1)S(1)}, bf16[256,512]{1,0:T(8,128)(2,1)}, u32[]{:S(2)}, u32[]{:S(2)}) collective-permute-start(bf16[256,512]{1,0:T(8,128)(2,1)S(1)} %pad_maximum_fusion.3), channel_id=1, source_target_pairs={{0,4},{1,5},{2,6},{3,7},{4,0},{5,1},{6,2},{7,3},{8,12},{9,13},{10,... | collective-permute-start | bytes 786440 | tf_op jit(solution)/shard_map/ppermute | solution.py:45
  52.0 12.1 %collective-permute-start.8 = (bf16[256,512]{1,0:T(8,128)(2,1)S(1)}, bf16[256,512]{1,0:T(8,128)(2,1)}, u32[]{:S(2)}, u32[]{:S(2)}) collective-permute-start(bf16[256,512]{1,0:T(8,128)(2,1)S(1)} %pad_maximum_fusion.3), channel_id=1, source_target_pairs={{0,2},{1,3},{2,0},{3,1},{4,6},{5,7},{6,4},{7,5},{8,10},{9,11},{10,... | collective-permute-start | bytes 786440 | tf_op jit(solution)/shard_map/ppermute | solution.py:45
  63.4 7.9 %copy-start.28 = (bf16[2,128,1024]{2,1,0:T(8,128)(2,1)S(1)}, bf16[2,128,1024]{2,1,0:T(8,128)(2,1)}, u32[]{:S(2)}) copy-start(bf16[2,128,1024]{2,1,0:T(8,128)(2,1)} %copy-done.27) | copy-start | bytes 1572868
  65.2 1.5 collective-permute-start.11
  69.0 25.1 %copy-start.18 = (bf16[4,256,512]{2,1,0:T(8,128)(2,1)}, bf16[4,256,512]{2,1,0:T(8,128)(2,1)S(1)}, u32[]{:S(2)}) copy-start(bf16[4,256,512]{2,1,0:T(8,128)(2,1)S(1)} %pad_maximum_fusion.refs_0_) | copy-start | bytes 3145732
  69.0 25.3 %collective-permute-start.14 = (bf16[4,256,512]{2,1,0:T(8,128)(2,1)S(1)}, bf16[4,256,512]{2,1,0:T(8,128)(2,1)S(1)}, u32[]{:S(2)}, u32[]{:S(2)}) collective-permute-start(bf16[4,256,512]{2,1,0:T(8,128)(2,1)S(1)} %pad_maximum_fusion.refs_0_), channel_id=1, source_target_pairs={{0,1},{1,0},{2,3},{3,2},{4,5},{5,4},{6,7},{7,6},{8,9},{9,8},{10,11... | collective-permute-start | bytes 3145736 | tf_op jit(solution)/shard_map/ppermute | solution.py:45
  70.4 6.7 %collective-permute-start.12 = (f32[48,1024]{1,0:T(8,128)S(1)}, f32[48,1024]{1,0:T(8,128)S(1)}, u32[]{:S(2)}, u32[]{:S(2)}) collective-permute-start(f32[48,1024]{1,0:T(8,128)S(1)} %select_add_fusion.1), channel_id=1, source_target_pairs={{0,16},{8,24},{16,0},{24,8},{1,17},{9,25},{17,1},{25,9},{2,18},{10... | collective-permute-start | bytes 589832 | tf_op jit(solution)/shard_map/ppermute | solution.py:45
  71.3 27.0 %collective-permute-start.15 = (bf16[2,128,1024]{2,1,0:T(8,128)(2,1)S(1)}, bf16[2,128,1024]{2,1,0:T(8,128)(2,1)}, u32[]{:S(2)}, u32[]{:S(2)}) collective-permute-start(bf16[2,128,1024]{2,1,0:T(8,128)(2,1)S(1)} %bitcast.115), channel_id=1, source_target_pairs={{0,8},{8,0},{16,24},{24,16},{1,9},{9,1},{17,25},{25,17},{2,10},{10... | collective-permute-start | bytes 1572872 | tf_op jit(solution)/shard_map/ppermute | solution.py:45
  71.3 27.0 %collective-permute-start.16 = (bf16[2,128,1024]{2,1,0:T(8,128)(2,1)S(1)}, bf16[2,128,1024]{2,1,0:T(8,128)(2,1)}, u32[]{:S(2)}, u32[]{:S(2)}) collective-permute-start(bf16[2,128,1024]{2,1,0:T(8,128)(2,1)S(1)} %copy-done.28), channel_id=1, source_target_pairs={{0,8},{8,0},{16,24},{24,16},{1,9},{9,1},{17,25},{25,17},{2,10},{10... | collective-permute-start | bytes 1572872 | tf_op jit(solution)/shard_map/ppermute | solution.py:45
  77.1 1.4 collective-permute-start.13
  112.7 22.8 %collective-permute-start.17 = (bf16[4,64,1024]{2,1,0:T(8,128)(2,1)}, bf16[4,64,1024]{2,1,0:T(8,128)(2,1)S(1)}, u32[]{:S(2)}, u32[]{:S(2)}) collective-permute-start(bf16[4,64,1024]{2,1,0:T(8,128)(2,1)} %get-tuple-element.157), channel_id=1, source_target_pairs={{0,1},{1,0},{2,3},{3,2},{4,5},{5,4},{6,7},{7,6},{8,9},{9,8},{10,11... | collective-permute-start | bytes 1572872 | tf_op jit(solution)/shard_map/ppermute | solution.py:45
  114.2 57.2 %all-to-all-start.1 = ((bf16[32,32,512]{2,1,0:T(8,128)(2,1)}), bf16[32,32,512]{2,1,0:T(8,128)(2,1)S(1)}, u32[]{:S(2)}, u32[]{:S(2)}) async-start(bf16[32,32,512]{2,1,0:T(8,128)(2,1)} %bitcast.120), calls=%async_computation.1 | async-start | bytes 2097152 | tf_op jit(solution)/shard_map/all_to_all | solution.py:1088
  117.0 22.7 %collective-permute-start.18 = (bf16[2,128,1024]{2,1,0:T(8,128)(2,1)}, bf16[2,128,1024]{2,1,0:T(8,128)(2,1)S(1)}, u32[]{:S(2)}, u32[]{:S(2)}) collective-permute-start(bf16[2,128,1024]{2,1,0:T(8,128)(2,1)} %get-tuple-element.165), channel_id=1, source_target_pairs={{0,8},{8,0},{16,24},{24,16},{1,9},{9,1},{17,25},{25,17},{2,10},{10... | collective-permute-start | bytes 1572872 | tf_op jit(solution)/shard_map/ppermute | solution.py:45
  117.1 40.8 %collective-permute-start.19 = (bf16[2,128,1024]{2,1,0:T(8,128)(2,1)}, bf16[2,128,1024]{2,1,0:T(8,128)(2,1)S(1)}, u32[]{:S(2)}, u32[]{:S(2)}) collective-permute-start(bf16[2,128,1024]{2,1,0:T(8,128)(2,1)} %get-tuple-element.166), channel_id=1, source_target_pairs={{0,16},{8,24},{16,0},{24,8},{1,17},{9,25},{17,1},{25,9},{2,18},{10... | collective-permute-start | bytes 1572872 | tf_op jit(solution)/shard_map/ppermute | solution.py:45
  118.7 39.2 %collective-permute-start.20 = (bf16[2,128,1024]{2,1,0:T(8,128)(2,1)}, bf16[2,128,1024]{2,1,0:T(8,128)(2,1)}, u32[]{:S(2)}, u32[]{:S(2)}) collective-permute-start(bf16[2,128,1024]{2,1,0:T(8,128)(2,1)} %get-tuple-element.167), channel_id=1, source_target_pairs={{0,24},{8,16},{16,8},{24,0},{1,25},{9,17},{17,9},{25,1},{2,26},{10... | collective-permute-start | bytes 1572872 | tf_op jit(solution)/shard_map/ppermute | solution.py:45
  138.5 19.4 %collective-permute-start.23 = (bf16[64,1024]{1,0:T(8,128)(2,1)}, bf16[64,1024]{1,0:T(8,128)(2,1)S(1)}, u32[]{:S(2)}, u32[]{:S(2)}) collective-permute-start(bf16[64,1024]{1,0:T(8,128)(2,1)} %get-tuple-element.293), channel_id=1, source_target_pairs={{0,6},{1,7},{2,4},{3,5},{4,2},{5,3},{6,0},{7,1},{8,14},{9,15},{10,... | collective-permute-start | bytes 393224 | tf_op jit(solution)/shard_map/ppermute | solution.py:45
  139.7 18.3 %collective-permute-start.22 = (bf16[64,1024]{1,0:T(8,128)(2,1)}, bf16[64,1024]{1,0:T(8,128)(2,1)S(1)}, u32[]{:S(2)}, u32[]{:S(2)}) collective-permute-start(bf16[64,1024]{1,0:T(8,128)(2,1)} %get-tuple-element.294), channel_id=1, source_target_pairs={{0,4},{1,5},{2,6},{3,7},{4,0},{5,1},{6,2},{7,3},{8,12},{9,13},{10,... | collective-permute-start | bytes 393224 | tf_op jit(solution)/shard_map/ppermute | solution.py:45
  139.7 18.2 %copy-start.25 = (bf16[2,128,1024]{2,1,0:T(8,128)(2,1)}, bf16[2,128,1024]{2,1,0:T(8,128)(2,1)S(1)}, u32[]{:S(2)}) copy-start(bf16[2,128,1024]{2,1,0:T(8,128)(2,1)S(1)} %collective-permute-done.18) | copy-start | bytes 1572868
  139.7 18.3 %collective-permute-start.21 = (bf16[64,1024]{1,0:T(8,128)(2,1)}, bf16[64,1024]{1,0:T(8,128)(2,1)S(1)}, u32[]{:S(2)}, u32[]{:S(2)}) collective-permute-start(bf16[64,1024]{1,0:T(8,128)(2,1)} %get-tuple-element.295), channel_id=1, source_target_pairs={{0,2},{1,3},{2,0},{3,1},{4,6},{5,7},{6,4},{7,5},{8,10},{9,11},{10,... | collective-permute-start | bytes 393224 | tf_op jit(solution)/shard_map/ppermute | solution.py:45
  157.9 11.4 %copy-start.26 = (bf16[2,128,1024]{2,1,0:T(8,128)(2,1)}, bf16[2,128,1024]{2,1,0:T(8,128)(2,1)S(1)}, u32[]{:S(2)}) copy-start(bf16[2,128,1024]{2,1,0:T(8,128)(2,1)S(1)} %collective-permute-done.19) | copy-start | bytes 1572868
  157.9 23.7 %copy-start.34 = (bf16[64,1024]{1,0:T(8,128)(2,1)}, bf16[64,1024]{1,0:T(8,128)(2,1)S(1)}, u32[]{:S(2)}) copy-start(bf16[64,1024]{1,0:T(8,128)(2,1)S(1)} %collective-permute-done.22) | copy-start | bytes 393220
  158.0 23.7 %copy-start.36 = (bf16[64,1024]{1,0:T(8,128)(2,1)}, bf16[64,1024]{1,0:T(8,128)(2,1)S(1)}, u32[]{:S(2)}) copy-start(bf16[64,1024]{1,0:T(8,128)(2,1)S(1)} %collective-permute-done.21) | copy-start | bytes 393220
  159.7 1.5 collective-permute-start.24
  162.2 7.0 %collective-permute-start.25 = (f32[48,1024]{1,0:T(8,128)S(1)}, f32[48,1024]{1,0:T(8,128)S(1)}, u32[]{:S(2)}, u32[]{:S(2)}) collective-permute-start(f32[48,1024]{1,0:T(8,128)S(1)} %select_add_fusion), channel_id=1, source_target_pairs={{0,16},{8,24},{16,0},{24,8},{1,17},{9,25},{17,1},{25,9},{2,18},{10... | collective-permute-start | bytes 589832 | tf_op jit(solution)/shard_map/ppermute | solution.py:45
  169.3 1.4 collective-permute-start.26
  181.7 32.5 %all-to-all-start.2 = ((bf16[32,32,512]{2,1,0:T(8,128)(2,1)}), bf16[32,32,512]{2,1,0:T(8,128)(2,1)S(1)}, u32[]{:S(2)}, u32[]{:S(2)}) async-start(bf16[32,32,512]{2,1,0:T(8,128)(2,1)} %bitcast.121), calls=%async_computation.2 | async-start | bytes 2097152 | tf_op jit(solution)/shard_map/all_to_all | solution.py:1107
  186.2 15.1 %collective-permute-start.27 = (bf16[4,64,192]{2,1,0:T(8,128)(2,1)}, bf16[4,64,192]{2,1,0:T(8,128)(2,1)}, u32[]{:S(2)}, u32[]{:S(2)}) collective-permute-start(bf16[4,64,192]{2,1,0:T(8,128)(2,1)} %fusion.7), channel_id=1, source_target_pairs={{0,1},{1,0},{2,3},{3,2},{4,5},{5,4},{6,7},{7,6},{8,9},{9,8},{10,11... | collective-permute-start | bytes 294920 | tf_op jit(solution)/shard_map/ppermute | solution.py:45
  187.8 14.5 %copy-start.17 = (bf16[2,1,128,1024]{3,2,1,0:T(8,128)(2,1)S(1)}, bf16[2,1,128,1024]{3,2,1,0:T(8,128)(2,1)}, u32[]{:S(2)}) copy-start(bf16[2,1,128,1024]{3,2,1,0:T(8,128)(2,1)} %param.16) | copy-start | bytes 1572868
  202.2 6.7 %copy-start.23 = (f32[2,128,1024]{2,1,0:T(8,128)S(1)}, f32[2,128,1024]{2,1,0:T(8,128)}, u32[]{:S(2)}) copy-start(f32[2,128,1024]{2,1,0:T(8,128)} %get-tuple-element.192) | copy-start | bytes 3145732
  202.2 6.6 %collective-permute-start.29 = (bf16[2,128,1024]{2,1,0:T(8,128)(2,1)}, bf16[2,128,1024]{2,1,0:T(8,128)(2,1)S(1)}, u32[]{:S(2)}, u32[]{:S(2)}) collective-permute-start(bf16[2,128,1024]{2,1,0:T(8,128)(2,1)} %get-tuple-element.193), channel_id=1, source_target_pairs={{0,8},{8,0},{16,24},{24,16},{1,9},{9,1},{17,25},{25,17},{2,10},{10... | collective-permute-start | bytes 1572872 | tf_op jit(solution)/shard_map/ppermute | solution.py:45
  205.3 8.9 %copy-start = (f32[32,4096]{1,0:T(8,128)S(1)}, f32[32,4096]{1,0:T(8,128)}, u32[]{:S(2)}) copy-start(f32[32,4096]{1,0:T(8,128)} %refs_0_.1) | copy-start | bytes 1572868
  205.3 8.9 %copy-start.14 = (f32[32]{0:T(128)S(1)}, f32[32]{0:T(128)}, u32[]{:S(2)}) copy-start(f32[32]{0:T(128)} %param.24) | copy-start | bytes 388
  205.3 6.0 %collective-permute-start.31 = (bf16[64,192]{1,0:T(8,128)(2,1)S(1)}, bf16[64,192]{1,0:T(8,128)(2,1)S(1)}, u32[]{:S(2)}, u32[]{:S(2)}) collective-permute-start(bf16[64,192]{1,0:T(8,128)(2,1)S(1)} %get-tuple-element.300), channel_id=1, source_target_pairs={{0,2},{1,3},{2,0},{3,1},{4,6},{5,7},{6,4},{7,5},{8,10},{9,11},{10,... | collective-permute-start | bytes 73736 | tf_op jit(solution)/shard_map/ppermute | solution.py:45
  205.4 6.0 %collective-permute-start.33 = (bf16[64,192]{1,0:T(8,128)(2,1)S(1)}, bf16[64,192]{1,0:T(8,128)(2,1)S(1)}, u32[]{:S(2)}, u32[]{:S(2)}) collective-permute-start(bf16[64,192]{1,0:T(8,128)(2,1)S(1)} %get-tuple-element.301), channel_id=1, source_target_pairs={{0,6},{1,7},{2,4},{3,5},{4,2},{5,3},{6,0},{7,1},{8,14},{9,15},{10,... | collective-permute-start | bytes 73736 | tf_op jit(solution)/shard_map/ppermute | solution.py:45
  206.8 7.3 %collective-permute-start.32 = (bf16[64,192]{1,0:T(8,128)(2,1)S(1)}, bf16[64,192]{1,0:T(8,128)(2,1)S(1)}, u32[]{:S(2)}, u32[]{:S(2)}) collective-permute-start(bf16[64,192]{1,0:T(8,128)(2,1)S(1)} %get-tuple-element.302), channel_id=1, source_target_pairs={{0,4},{1,5},{2,6},{3,7},{4,0},{5,1},{6,2},{7,3},{8,12},{9,13},{10,... | collective-permute-start | bytes 73736 | tf_op jit(solution)/shard_map/ppermute | solution.py:45
  208.9 11.0 %collective-permute-start.28 = (bf16[2,128,1024]{2,1,0:T(8,128)(2,1)}, bf16[2,128,1024]{2,1,0:T(8,128)(2,1)}, u32[]{:S(2)}, u32[]{:S(2)}) collective-permute-start(bf16[2,128,1024]{2,1,0:T(8,128)(2,1)} %get-tuple-element.191), channel_id=1, source_target_pairs={{0,8},{8,0},{16,24},{24,16},{1,9},{9,1},{17,25},{25,17},{2,10},{10... | collective-permute-start | bytes 1572872 | tf_op jit(solution)/shard_map/ppermute | solution.py:45
  209.8 15.1 %collective-permute-start.30 = (bf16[2,128,1024]{2,1,0:T(8,128)(2,1)}, bf16[2,128,1024]{2,1,0:T(8,128)(2,1)}, u32[]{:S(2)}, u32[]{:S(2)}) collective-permute-start(bf16[2,128,1024]{2,1,0:T(8,128)(2,1)} %add_convert_fusion), channel_id=1, source_target_pairs={{0,16},{8,24},{16,0},{24,8},{1,17},{9,25},{17,1},{25,9},{2,18},{10... | collective-permute-start | bytes 1572872 | tf_op jit(solution)/shard_map/ppermute | solution.py:45
  216.2 11.5 %all-to-all-start.3 = ((f32[32,1,128]{2,1,0:T(1,128)}), f32[32,1,128]{2,1,0:T(1,128)S(1)}, u32[]{:S(2)}, u32[]{:S(2)}) async-start(f32[32,1,128]{2,1,0:T(1,128)} %broadcast_in_dim.25), calls=%async_computation.3 | async-start | bytes 32768 | tf_op jit(solution)/shard_map/all_to_all | solution.py:1131
  222.4 5.3 %copy-start.2 = (f32[2,32,4096]{2,1,0:T(8,128)S(1)}, f32[2,32,4096]{2,1,0:T(8,128)}, u32[]{:S(2)}) copy-start(f32[2,32,4096]{2,1,0:T(8,128)} %refs_7_.1) | copy-start | bytes 3145732
  222.4 5.3 %copy-start.3 = (f32[2,64,1024]{2,1,0:T(8,128)S(1)}, f32[2,64,1024]{2,1,0:T(8,128)}, u32[]{:S(2)}) copy-start(f32[2,64,1024]{2,1,0:T(8,128)} %refs_8_.1) | copy-start | bytes 1572868
  222.4 5.3 %copy-start.5 = (f32[32,4096]{1,0:T(8,128)S(1)}, f32[32,4096]{1,0:T(8,128)}, u32[]{:S(2)}) copy-start(f32[32,4096]{1,0:T(8,128)} %copy-done.4) | copy-start | bytes 1572868
  222.4 5.3 %copy-start.8 = (f32[2,64,96]{2,1,0:T(8,128)S(1)}, f32[2,64,96]{2,1,0:T(8,128)}, u32[]{:S(2)}) copy-start(f32[2,64,96]{2,1,0:T(8,128)} %refs_9_.1) | copy-start | bytes 147460
  222.4 5.3 %copy-start.9 = (f32[2,64,64]{2,1,0:T(8,128)S(1)}, f32[2,64,64]{2,1,0:T(8,128)}, u32[]{:S(2)}) copy-start(f32[2,64,64]{2,1,0:T(8,128)} %refs_10_.1) | copy-start | bytes 98308
  222.4 5.3 %copy-start.11 = (f32[2,16,64]{2,1,0:T(8,128)S(1)}, f32[2,16,64]{2,1,0:T(8,128)}, u32[]{:S(2)}) copy-start(f32[2,16,64]{2,1,0:T(8,128)} %refs_12_.1) | copy-start | bytes 24580
  222.5 5.3 %copy-start.13 = (f32[2,7,64]{2,0,1:T(2,128)S(1)}, f32[2,7,64]{2,0,1:T(2,128)}, u32[]{:S(2)}) copy-start(f32[2,7,64]{2,0,1:T(2,128)} %param.29) | copy-start | bytes 10756
  222.5 5.3 %copy-start.15 = (f32[2,32]{1,0:T(2,128)S(1)}, f32[2,32]{1,0:T(2,128)}, u32[]{:S(2)}) copy-start(f32[2,32]{1,0:T(2,128)} %param.31) | copy-start | bytes 772
  (12 other events, 21.3 us)
where the time goes:
time: 231 us; the launch traced here: 230 us
  Pallas kernels  94.2 us (41%)
  waiting for transfers between devices  62.4 us (27%)
  starting transfers between devices  44.7 us (19%)
  other arithmetic  18.7 us (8%)
  local copies, waits for them, and re-layouts  8.64 us (4%)
    ppermute x34, waiting for transfers between devices, swap(): return lax.ppermute(x, axis, [(i, i ^ mask) for i in range(peers)])  58.2 us
    ppermute x34, starting transfers between devices, swap(): return lax.ppermute(x, axis, [(i, i ^ mask) for i in range(peers)])  30.4 us
    pallas_call x2, Pallas kernels, scan_backward(): pl.pallas_call(backward_kernel, grid=(blocks,), in_specs=[pl.BlockSpec((W...  28.5 us
    pallas_call x1, Pallas kernels, scan_forward(): pl.pallas_call(forward_kernel, grid=(seqs, blocks), in_specs=[pl.BlockSpe...  14.9 us
    pallas_call x1, Pallas kernels, middle(): pl.pallas_call(middle_kernel, grid_spec=pltpu.PrefetchScalarGridSpec(num_...  14.4 us
    pallas_call x1, Pallas kernels, leave(): pl.pallas_call(leave_kernel, grid=(seqs, blocks), in_specs=[pl.BlockSpec(...  10.3 us
    pallas_call x1, Pallas kernels, enter(): pl.pallas_call(enter_kernel, grid_spec=pltpu.PrefetchScalarGridSpec(num_s...  7.95 us
    pallas_call x1, Pallas kernels, rows_back(): pl.pallas_call(rows_back_kernel, grid_spec=pltpu.PrefetchScalarGridSpec(n...  6.71 us
  transfers between devices with their start and end apart: 38, of which 18 were waited for; matrix products, arithmetic and copies ran while one was open for 7% of the time, Pallas kernels for 29%

commit v1 on v0

--- a/solution.py
+++ b/solution.py
@@ -80,48 +80,42 @@
     return [x] + [swap(x, "fsdp", m * (peers // depth)) for m in range(1, depth)]
 
 
-def gather_near(far):
-    far = jnp.stack(far)
-    near = lax.axis_size("fsdp") // far.shape[0]
-    return [far] + [swap(far, "fsdp", m) for m in range(1, near)]
-
-
-def merge_near(nears):
-    parts = jnp.stack(nears, axis=1)
-    return in_order(parts.reshape((-1,) + parts.shape[2:]), "fsdp")
-
-
-def reduce_dp_near(parts):
-    return [parts[p] + swap(parts[p + 1], "dp", 1).astype(f32) for p in range(0, len(parts), 2)]
-
-
-def send_dp_far(parts):
-    for mask in masks("dp")[1:-1]:
+def swap_near(x):
+    near = lax.axis_size("fsdp") // min(4, lax.axis_size("fsdp"))
+    return [swap(x, "fsdp", m) for m in range(1, near)]
+
+
+def merge_near(far, own, rest):
+    nears = [far] + [[one] + list(stack) for one, stack in zip(own, rest)]
+    parts = jnp.stack([part for both in zip(*nears) for part in both])
+    return in_order(parts, "fsdp")
+
+
+def send_dp_near(parts):
+    moved = [swap(part, "dp", 1) for part in parts[1::2]]
+    sums = [kept + part.astype(f32) for kept, part in zip(parts[2::2], moved[1:])]
+    return [parts[0], moved[0]], [part.astype(bf16) for part in sums]
+
+
+def send_dp_far(mine, parts):
+    for mask in masks("dp")[1:]:
+        moved = [swap(part, "dp", mask) for part in parts[0::2]]
+        mine = mine + [moved[0]]
         parts = [
-            parts[p] + swap(parts[p + 1].astype(bf16), "dp", mask).astype(f32)
-            for p in range(0, len(parts), 2)
+            (kept.astype(f32) + part.astype(f32)).astype(bf16)
+            for kept, part in zip(parts[1::2], moved[1:])
         ]
-    return [parts[0]] + [
-        swap(part.astype(bf16), "dp", masks("dp")[-1]) for part in parts[1:]
-    ]
-
-
-def send_dp(parts):
-    return [parts[0]] + [swap(parts[m], "dp", m) for m in range(1, len(parts))]
-
-
-def sum_dp_near(x):
-    high = (lax.axis_index("dp") & 1) != 0
-    split = x.reshape((2, x.shape[0] // 2) + x.shape[1:])
-    mine = jnp.where(high, split[1], split[0])
-    other = jnp.where(high, split[0], split[1])
+    return mine
+
+
+def sum_dp_near(mine, other):
     return mine + swap(other, "dp", 1)
 
 
-def sum_dp_far(mine):
+def sum_dp_far(mine, sent):
     high = (lax.axis_index("dp") & 1) != 0
     for mask in masks("dp")[1:]:
-        mine = mine + swap(mine, "dp", mask)
+        mine = mine + swap(mine.astype(sent), "dp", mask).astype(f32)
     mine = mine.astype(bf16)
     other = swap(mine, "dp", 1)
     both = jnp.where(high, jnp.stack([other, mine]), jnp.stack([mine, other]))
@@ -132,7 +126,7 @@
     mine = parts[0].astype(f32)
     for m in range(1, len(parts)):
         mine = mine + swap(parts[m].astype(bf16), "fsdp", m).astype(f32)
-    return mine
+    return [mine[0]] + [mine[d].astype(bf16) for d in range(1, mine.shape[0])]
 
 
 def split_near(x):
@@ -143,20 +137,24 @@
 
 
 def send_far(mine):
-    depth = mine.shape[0]
-    near = lax.axis_size("fsdp") // depth
-    return [mine[0]] + [
-        swap(mine[m].astype(bf16), "fsdp", m * near) for m in range(1, depth)
-    ]
+    near = lax.axis_size("fsdp") // len(mine)
+    return mine[:1] + [swap(mine[m], "fsdp", m * near) for m in range(1, len(mine))]
+
+
+def by_near(refs, depth):
+    parts = []
+    for ref in refs:
+        parts += [ref] if len(ref.shape) == 2 else [ref.at[d] for d in range(ref.shape[0])]
+    return [parts[k : k + depth] for k in range(0, len(parts), depth)]
 
 
 def assemble_first_kernel(me_ref, *refs):
-    raws = refs[:-6]
     w_ref, small_ref, gain_ref, a_ref, chan_ref, gains = refs[-6:]
-    near = len(raws)
-    depth = raws[0].shape[0]
     model, width = w_ref.shape
-    peers = near * depth
+    peers = lax.axis_size("fsdp")
+    depth = min(4, peers)
+    near = peers // depth
+    raws = by_near(refs[:-6], depth)
     own = width // peers
     fold = width // SMALL
     here = model // peers
@@ -169,13 +167,13 @@
             j = me_ref[1] ^ (d * near + m)
             for k in range(dps):
                 to = pl.multiple_of((k * peers + j) * own_in, own_in)
-                w_ref[pl.ds(to, own_in), :] = raws[m][d, k * own_in : (k + 1) * own_in, :]
-                row = raws[m][d, here : here + 16, 0:128].astype(f32)[k : k + 1]
+                w_ref[pl.ds(to, own_in), :] = raws[m][d][k * own_in : (k + 1) * own_in, :]
+                row = raws[m][d][here : here + 16, 0:128].astype(f32)[k : k + 1]
                 gains[pl.ds(k * peers + j, 1), :] = row
             for f in range(fold):
                 to = pl.multiple_of(j * own + f * stretch, stretch)
-                small_ref[pl.ds(to, stretch), :] = raws[m][
-                    d, at_small : at_small + stretch, f * SMALL : (f + 1) * SMALL
+                small_ref[pl.ds(to, stretch), :] = raws[m][d][
+                    at_small : at_small + stretch, f * SMALL : (f + 1) * SMALL
                 ]
     row = lax.broadcasted_iota(jnp.int32, (own_in, model), 0)
     column = lax.broadcasted_iota(jnp.int32, (own_in, model), 1)
@@ -190,12 +188,12 @@
 
 
 def assemble_second_kernel(me_ref, *refs):
-    raws = refs[:-2]
     wg_ref, wo_ref = refs[-2:]
-    near = len(raws)
-    depth = raws[0].shape[0]
     model, width = wg_ref.shape
-    peers = near * depth
+    peers = lax.axis_size("fsdp")
+    depth = min(4, peers)
+    near = peers // depth
+    raws = by_near(refs[:-2], depth)
     own = width // peers
     here = model // peers
     dps = lax.axis_size("dp")
@@ -205,15 +203,16 @@
             j = me_ref[1] ^ (d * near + m)
             for k in range(dps):
                 to = pl.multiple_of((k * peers + j) * own_in, own_in)
-                wg_ref[pl.ds(to, own_in), :] = raws[m][d, k * own_in : (k + 1) * own_in, :]
+                wg_ref[pl.ds(to, own_in), :] = raws[m][d][k * own_in : (k + 1) * own_in, :]
             for c in range(model // width):
                 to = pl.multiple_of(j * own, own)
-                wo_ref[pl.ds(to, own), c * width : (c + 1) * width] = raws[m][
-                    d, here + c * own : here + (c + 1) * own, :
+                wo_ref[pl.ds(to, own), c * width : (c + 1) * width] = raws[m][d][
+                    here + c * own : here + (c + 1) * own, :
                 ]
 
 
-def assemble(kernel, name, me, raws, shapes, scratch):
+def assemble(kernel, name, me, far, own, rest, shapes, scratch):
+    raws = far + [part for both in zip(own, rest) for part in both]
     whole = pl.BlockSpec(memory_space=pltpu.VMEM)
     return pl.pallas_call(
         kernel,
@@ -221,7 +220,7 @@
         out_specs=[whole] * len(shapes),
         out_shape=[jax.ShapeDtypeStruct(shape, dtype) for shape, dtype in shapes],
         scratch_shapes=scratch,
-        compiler_params=params(60),
+        compiler_params=params(24),
         cost_estimate=cost(2),
         name=name,
     )(me, *raws)
@@ -254,9 +253,16 @@
     return [pl.BlockSpec((1, piece, model), lambda s, b, me: (s, 0, 0))] * dps
 
 
+def halve(mine_ref, other_ref, rows, me):
+    low, high = rows[: WIDE // 2], rows[WIDE // 2 :]
+    odd = me % 2 == 1
+    mine_ref[...] = jnp.where(odd, high, low)
+    other_ref[...] = jnp.where(odd, low, high)
+
+
 def enter_kernel(me_ref, gain_ref, w_ref, chan_ref, wx_ref, *refs):
-    tok_refs = refs[:-7]
-    normed_ref, conv_ref, pre_ref, act_ref, xt_ref, padded, whole = refs[-7:]
+    tok_refs = refs[:-8]
+    normed_ref, conv_ref, pre_ref, act_ref, xt_ref, other_ref, padded, whole = refs[-8:]
     block = pl.program_id(1)
     rows = conv_ref.shape[1]
 
@@ -282,7 +288,7 @@
     pre_ref[0] = pre
     act = (pre * jax.nn.sigmoid(pre)).astype(bf16)
     act_ref[0] = act
-    xt_ref[...] = dot(wx_ref[:, 0:WIDE], act, 0, 1)
+    halve(xt_ref, other_ref, dot(wx_ref[:, 0:WIDE], act, 0, 1), me_ref[0])
 
 
 def enter(me, gain, w, chan, wx, tok):
@@ -316,7 +322,8 @@
                 pl.BlockSpec((1, rows, width), at),
                 pl.BlockSpec((1, rows, width), at),
                 pl.BlockSpec((1, rows, width), at),
-                pl.BlockSpec((WIDE, rows), lambda s, b, me: (0, s * blocks + b)),
+                pl.BlockSpec((WIDE // 2, rows), lambda s, b, me: (0, s * blocks + b)),
+                pl.BlockSpec((WIDE // 2, rows), lambda s, b, me: (0, s * blocks + b)),
             ],
             scratch_shapes=[pltpu.VMEM((rows + 8, width), f32), pltpu.VMEM((length, model), bf16)],
         ),
@@ -325,7 +332,8 @@
             jax.ShapeDtypeStruct((seqs, length, width), bf16),
             jax.ShapeDtypeStruct((seqs, length, width), f32),
             jax.ShapeDtypeStruct((seqs, length, width), bf16),
-            jax.ShapeDtypeStruct((WIDE, seqs * length), f32),
+            jax.ShapeDtypeStruct((WIDE // 2, seqs * length), f32),
+            jax.ShapeDtypeStruct((WIDE // 2, seqs * length), f32),
         ],
         compiler_params=params(60),
         cost_estimate=cost(7),
@@ -527,7 +535,7 @@
                 pltpu.VMEM((rows, model), f32),
             ],
         ),
-        out_shape=piece_shapes(dps, seqs, piece, model, dps)
+        out_shape=piece_shapes(dps, seqs, piece, model, 2)
         + [jax.ShapeDtypeStruct((depth, own, model), bf16)] * near
         + [
             jax.ShapeDtypeStruct((seqs, length, width), f32),
@@ -542,6 +550,7 @@
 
 
 def backward_kernel(
+    me_ref,
     xt_ref,
     act_ref,
     dt_ref,
@@ -554,12 +563,16 @@
     dtw_ref,
     *refs,
 ):
-    gsp_ref, gact_ref, gxt_ref, galog_ref, carried, total, g_buf, q_buf = refs[-8:]
-    first = pl.program_id(0) == pl.num_programs(0) - 1
-
-    @pl.when(pl.program_id(0) == 0)
+    gsp_ref, gact_ref, mine_ref, other_ref, galog_ref = refs[-10:-5]
+    carried, total, g_buf, q_buf, gxt_ref = refs[-5:]
+    first = pl.program_id(1) == pl.num_programs(1) - 1
+
+    @pl.when(pl.program_id(1) == 0)
     def _():
         carried[...] = jnp.zeros_like(carried)
+
+    @pl.when((pl.program_id(0) == 0) & (pl.program_id(1) == 0))
+    def _():
         total[...] = jnp.zeros_like(total)
 
     columns = xt_ref[...].astype(f32)
@@ -610,29 +623,31 @@
     carried[...] = p
     total[...] = acc
     gxt_ref[0:R, :] = dot(dtw_ref[:, AT_DT : AT_DT + R], gsp_ref[0], 0, 1)
+    halve(mine_ref, other_ref, gxt_ref[...], me_ref[0])
     galog_ref[...] = acc * a_now
 
 
-def scan_backward(s, earlier, xt, act, dt, sp, ggi, chan, a_matrix, states, dtw):
+def scan_backward(me, xt, act, dt, sp, ggi, chan, a_matrix, states, dtw):
     seqs, length, width = act.shape
     blocks = length // ROWS
 
-    def back(b):
+    def back(s, b):
         return (s, blocks - 1 - b, 0)
 
-    def before(b):
+    def before(s, b):
         return (s, jnp.maximum((blocks - 1 - b) * ROWS - 1, 0), 0)
 
-    def flat(b):
+    def flat(s, b):
         return (0, s * blocks + blocks - 1 - b)
 
-    def fixed(b):
+    def fixed(s, b):
         return (0, 0)
 
     return pl.pallas_call(
         backward_kernel,
-        grid=(blocks,),
+        grid=(seqs, blocks),
         in_specs=[
+            pl.BlockSpec(memory_space=pltpu.SMEM),
             pl.BlockSpec((WIDE, ROWS), flat),
             pl.BlockSpec((1, ROWS, width), back),
             pl.BlockSpec((1, ROWS, width), back),
@@ -643,18 +658,19 @@
             pl.BlockSpec((1, ROWS * N, width), back),
             pl.BlockSpec((1, N, width), before),
             pl.BlockSpec((width, SMALL), fixed),
-        ]
-        + [pl.BlockSpec(memory_space=pl.ANY)] * len(earlier),
+        ],
         out_specs=[
             pl.BlockSpec((1, ROWS, width), back),
             pl.BlockSpec((1, ROWS, width), back),
-            pl.BlockSpec((WIDE, ROWS), flat),
+            pl.BlockSpec((WIDE // 2, ROWS), flat),
+            pl.BlockSpec((WIDE // 2, ROWS), flat),
             pl.BlockSpec((N, width), fixed),
         ],
         out_shape=[
             jax.ShapeDtypeStruct((seqs, length, width), bf16),
             jax.ShapeDtypeStruct((seqs, length, width), f32),
-            jax.ShapeDtypeStruct((WIDE, seqs * length), f32),
+            jax.ShapeDtypeStruct((WIDE // 2, seqs * length), f32),
+            jax.ShapeDtypeStruct((WIDE // 2, seqs * length), f32),
             jax.ShapeDtypeStruct((N, width), f32),
         ],
         scratch_shapes=[
@@ -662,12 +678,12 @@
             pltpu.VMEM((N, width), f32),
             pltpu.VMEM((ROWS * N, width), bf16),
             pltpu.VMEM((ROWS * N, width), bf16),
+            pltpu.VMEM((WIDE, ROWS), f32),
         ],
-        input_output_aliases={10 + k: k for k in range(len(earlier))},
         compiler_params=params(60),
-        cost_estimate=cost(16),
-        name=f"scan_backward_{s}",
-    )(xt, act, dt, sp, ggi, chan, a_matrix, states, states, dtw, *earlier)
+        cost_estimate=cost(28),
+        name="scan_backward",
+    )(me, xt, act, dt, sp, ggi, chan, a_matrix, states, states, dtw)
 
 
 def leave_kernel(
@@ -894,7 +910,7 @@
     gchan_ref[...] = turned[WIDE + R + N : WIDE + R + N + KW + 3, :own]
     grad = turned[GRADS : GRADS + 1, :own_in] / gain_ref[...].astype(bf16).astype(f32)
     ggain_ref[...] = grad
-    squares_ref[...] = total + squares(grad)
+    squares_ref[...] = jnp.broadcast_to((total + squares(grad))[None], squares_ref.shape)
 
 
 def collect(conv, gate, out, small, w, gain):
@@ -907,7 +923,7 @@
         (KW + 3, own),
         (N, own),
         (1, own_in),
-        (1, 128),
+        (conv.shape[0], 1, 128),
     ]
     whole = pl.BlockSpec(memory_space=pltpu.VMEM)
     return pl.pallas_call(
@@ -1019,11 +1035,22 @@
     here = dps * own_in
     gain_rows = jnp.pad(in_parts[:, 2 * own_in], ((0, -dps % 16), (0, 0)))
     first = jnp.concatenate([in_parts[:, :own_in].reshape(here, width), gain_rows, packed])
+    out_low = out_weight.astype(bf16).reshape(own, model // width, width).transpose(1, 0, 2)
+    second = [
+        in_parts[:, own_in : 2 * own_in].reshape(here, width),
+        out_low.reshape(-1, width),
+    ]
+    second = jnp.concatenate(second)
     tok = parts_dp_far(tokens.reshape(seqs, piece, model))
-    first, tok = lax.optimization_barrier((gather_far(first), tok))
+    first_own = swap_near(first)
+    second_own = swap_near(second)
+    first, tok, first_own, second_own = lax.optimization_barrier(
+        (gather_far(first), tok, first_own, second_own)
+    )
     cot = parts_dp_far(after(cotangent.reshape(seqs, piece, model), first))
     tok = parts_dp_near(tok)
-    first, cot = lax.optimization_barrier((gather_near(first), cot))
+    first_rest = swap_near(jnp.stack(first[1:]))
+    first, first_rest, cot = lax.optimization_barrier((first, first_rest, cot))
 
     def own_columns(parts):
         parts = parts.reshape(fsdps, dps, own_in, width)
@@ -1035,6 +1062,8 @@
             "assemble_first",
             me,
             first,
+            first_own,
+            first_rest,
             [
                 ((model, width), bf16),
                 ((width, SMALL), bf16),
@@ -1045,7 +1074,7 @@
             [pltpu.VMEM((model // own_in, 128), f32)],
         )
     else:
-        merged = merge_near(first)
+        merged = merge_near(first, first_own, first_rest)
         w_conv = own_columns(merged[:, :here])
         gain = merged[:, here : here + dps, :own_in].transpose(1, 0, 2)
         gain = gain.reshape(1, model).astype(f32)
@@ -1054,30 +1083,26 @@
         a_matrix = -jnp.exp(rest[:N])
         chan = rest[N : N + 8]
 
-    out_low = out_weight.astype(bf16).reshape(own, model // width, width).transpose(1, 0, 2)
-    second = [
-        in_parts[:, own_in : 2 * own_in].reshape(here, width),
-        out_low.reshape(-1, width),
-    ]
-    far = gather_far(jnp.concatenate(second))
-    normed, conv, pre, act, xt = enter(me, gain, w_conv, chan, small, tok)
+    far = gather_far(second)
+    normed, conv, pre, act, *xt = enter(me, gain, w_conv, chan, small, tok)
     cot = parts_dp_near(cot)
     xt, far = lax.optimization_barrier((xt, far))
-    xt = sum_dp_near(xt)
-    xt, far = lax.optimization_barrier((xt, far))
-    second = gather_near(far)
-    xt = sum_dp_far(xt)
+    xt = sum_dp_near(*xt)
+    second_rest = swap_near(jnp.stack(after(far[1:], xt)))
+    xt = sum_dp_far(xt, f32)
     if aligned:
         w_gate, w_out = assemble(
             assemble_second_kernel,
             "assemble_second",
             me,
-            second,
+            far,
+            second_own,
+            second_rest,
             [((model, width), bf16), ((width, model), bf16)],
             [],
         )
     else:
-        merged = merge_near(second)
+        merged = merge_near(far, second_own, second_rest)
         w_gate = own_columns(merged[:, :here])
         w_out = merged[:, here:].reshape(fsdps, model // width, own, width)
         w_out = w_out.transpose(0, 2, 1, 3).reshape(width, model)
@@ -1087,32 +1112,31 @@
     ggi, ggp, gin_gate, gskip = outs[dps + near :]
     gate_parts = lax.all_to_all(gin_gate.reshape(-1, own_in, width), both, 0, 0, tiled=True)
     gout_near = reduce_near(gout)
-    out_rows = send_dp(part)
-
-    back = ()
-    galog = []
-    for s in reversed(range(seqs)):
-        *back, one = scan_backward(s, back, xt, act, dt, step_pre, ggi, chan, a_matrix, states, small)
-        galog.append(one)
-        if s == seqs - 1:
-            ggi, gout_near = lax.optimization_barrier((ggi, gout_near))
-    gsp, gact, gxt = back
-    gout_far = send_far(gout_near)
-    gxt, out_rows, gout_far = lax.optimization_barrier((gxt, out_rows, gout_far))
-    gxt = sum_dp_far(sum_dp_near(gxt))
+    out_mine, out_parts = send_dp_near(part)
+
+    gsp, gact, *gxt, galog = scan_backward(
+        me, xt, act, dt, step_pre, ggi, chan, a_matrix, states, small
+    )
+    gxt, out_mine, gout_near = lax.optimization_barrier((gxt, out_mine, gout_near))
+    gxt = sum_dp_near(*gxt)
+    gout_far = send_far(list(after(gout_near, gxt)))
+    out_rows = send_dp_far(list(out_mine), list(after(out_parts, gxt)))
+    gxt = sum_dp_far(gxt, bf16)
     gxt, gate_parts = lax.optimization_barrier((gxt, gate_parts))
     gci, gin_conv, small_grad = leave(
-        gact, gxt, xt, gsp, small, pre, conv, act, normed, chan, gskip, galog
+        gact, gxt, xt, gsp, small, pre, conv, act, normed, chan, gskip, [galog]
     )
+    gin_conv, gout_far, out_rows = lax.optimization_barrier((gin_conv, gout_far, out_rows))
     conv_parts = lax.all_to_all(gin_conv.reshape(-1, own_in, width), both, 0, 0, tiled=True)
     grad_out = sum(part.astype(f32) for part in gout_far)
+    small_near = reduce_near(split_near(small_grad.reshape(fsdps, own, GRADS)))
+    part_back = rows_back(me, gci, ggp, w_conv, w_gate, dps)
+    back_mine, back_parts = send_dp_near(part_back)
+    small_near, back_parts = lax.optimization_barrier((small_near, back_parts))
+    own_small = sum(part.astype(f32) for part in send_far(list(small_near)))
+    part_back = send_dp_far(back_mine, list(back_parts))
     out_rows = sum(part.astype(f32) for part in out_rows).reshape(tokens.shape)
     block_output = (tokens.astype(f32) + out_rows).astype(bf16)
-    small_near = reduce_near(split_near(small_grad.reshape(fsdps, own, GRADS)))
-    part_back = rows_back(me, gci, ggp, w_conv, w_gate, dps)
-    small_near, part_back = lax.optimization_barrier((small_near, part_back))
-    own_small = sum(part.astype(f32) for part in send_far(small_near))
-    part_back = send_dp_far(reduce_dp_near(part_back))
 
     def flat2(x):
         return x.reshape(x.shape[:-1] + (1, x.shape[-1]))
@@ -1128,9 +1152,7 @@
         gain,
         after(part_back, squares),
     ).reshape(tokens.shape)
-    squares = lax.all_to_all(
-        jnp.broadcast_to(squares[None], (dps * fsdps, 1, 128)), both, 0, 0, tiled=True
-    )
+    squares = lax.all_to_all(squares, both, 0, 0, tiled=True)
     weights = (in_weight, out_weight, xproj_weight, dtproj_weight, chan_params, a_log, flat2(norm_gain))
     moments = (
         in_moments,

time: 231 us -> 222 us (0.961)
  starting transfers between devices: 44.7 us -> 63.7 us
  waiting for transfers between devices: 62.4 us -> 44.3 us
  Pallas kernels: 94.2 us -> 87.7 us
  other arithmetic: 18.7 us -> 14 us
    ppermute x34 -> x36, waiting for transfers between devices: 58.2 us -> 39.7 us  [swap(): return lax.ppermute(x, axis, [(i, i ^ mask) for i in range(peers)])]
    ppermute x34 -> x36, starting transfers between devices: 30.4 us -> 43 us  [swap(): return lax.ppermute(x, axis, [(i, i ^ mask) for i in range(peers)])]
    add x4 -> x1, other arithmetic: 4.84 us -> 0.02 us  [shards(): own_small = sum((part.astype(f32) for part in send_far(list(small_near))))]
    all_to_all x1, starting transfers between devices: 2.82 us -> 7.13 us  [shards(): lax.all_to_all(gin_gate.reshape(-1, own_in, width), both, 0, 0, tiled=True)]
    pallas_call x2, Pallas kernels: 5.56 us -> 1.48 us  [assemble(): pl.pallas_call(kernel, in_specs=[pl.BlockSpec(memory_space=pltpu.SMEM)] +...]
    pallas_call x2 -> x1, Pallas kernels: 28.5 us -> 25.7 us  [scan_backward(): pl.pallas_call(backward_kernel, grid=(seqs, blocks), in_specs=[pl.BlockSp...]
    all_to_all x1, starting transfers between devices: 3.6 us -> 6.22 us  [shards(): lax.all_to_all(gin_conv.reshape(-1, own_in, width), both, 0, 0, tiled=True)]
    convert_element_type x1 -> x3, other arithmetic: 0.95 us -> 3.38 us  [the longest x2 3.35 us: send_dp_near(): return ([parts[0], moved[0]], [part.astype(bf16) for part in sums])]
  transfers between devices with their start and end apart: 38 -> 40, of which waited for: 18 -> 15; matrix products, arithmetic and copies ran while one was open for 7% -> 6% of each run, Pallas kernels for 29% -> 32%
where the time goes in v1:
time: 222 us; the launch traced here: 221 us
  Pallas kernels  87.7 us (40%)
  starting transfers between devices  63.7 us (29%)
  waiting for transfers between devices  44.3 us (20%)
  other arithmetic  14 us (6%)
  local copies, waits for them, and re-layouts  10.2 us (5%)
    ppermute x36, starting transfers between devices, swap(): return lax.ppermute(x, axis, [(i, i ^ mask) for i in range(peers)])  43 us
    ppermute x36, waiting for transfers between devices, swap(): return lax.ppermute(x, axis, [(i, i ^ mask) for i in range(peers)])  39.7 us
    pallas_call x1, Pallas kernels, scan_backward(): pl.pallas_call(backward_kernel, grid=(seqs, blocks), in_specs=[pl.BlockSp...  25.7 us
    pallas_call x1, Pallas kernels, scan_forward(): pl.pallas_call(forward_kernel, grid=(seqs, blocks), in_specs=[pl.BlockSpe...  15 us
    pallas_call x1, Pallas kernels, middle(): pl.pallas_call(middle_kernel, grid_spec=pltpu.PrefetchScalarGridSpec(num_...  14.3 us
    pallas_call x1, Pallas kernels, leave(): pl.pallas_call(leave_kernel, grid=(seqs, blocks), in_specs=[pl.BlockSpec(...  10.3 us
    pallas_call x1, Pallas kernels, enter(): pl.pallas_call(enter_kernel, grid_spec=pltpu.PrefetchScalarGridSpec(num_s...  7.66 us
    all_to_all x1, starting transfers between devices, shards(): lax.all_to_all(gin_gate.reshape(-1, own_in, width), both, 0, 0, tiled=True)  7.13 us
  transfers between devices with their start and end apart: 40, of which 15 were waited for; matrix products, arithmetic and copies ran while one was open for 6% of the time, Pallas kernels for 32%

profile of v1, /device:TPU:0, one launch (start us, length us, event | category | flops | bytes accessed | tf_op | source)
XLA Modules:
  0.0 221.4 jit_solution(13573689873757722301)
XLA Ops:
  0.7 1.1 convert_element_type.117
  3.0 0.8 copy.70
  3.8 4.2 %all-to-all-start = ((bf16[4,72,512]{2,1,0:T(8,128)(2,1)}), bf16[4,72,512]{2,1,0:T(8,128)(2,1)S(1)}, u32[]{:S(2)}, u32[]{:S(2)}) async-start(bf16[4,72,512]{2,1,0:T(8,128)(2,1)} %copy.70), calls=%async_computation | async-start | bytes 589824 | tf_op jit(solution)/shard_map/all_to_all | solution.py:1017
  8.0 2.2 %collective-permute-start.3 = (bf16[2,128,1024]{2,1,0:T(8,128)(2,1)}, bf16[2,128,1024]{2,1,0:T(8,128)(2,1)}, u32[]{:S(2)}, u32[]{:S(2)}) collective-permute-start(bf16[2,128,1024]{2,1,0:T(8,128)(2,1)} %bitcast.12.refs_0_.tok_ref), channel_id=1, source_target_pairs={{0,16},{8,24},{16,0},{24,8},{1,17},{9,25},{17,1},{25,9},{2,18},{10... | collective-permute-start | bytes 1572872 | tf_op jit(solution)/shard_map/ppermute | solution.py:45
  10.8 4.2 %all-to-all-done = bf16[4,72,512]{2,1,0:T(8,128)(2,1)S(1)} async-done(((bf16[4,72,512]{2,1,0:T(8,128)(2,1)}), bf16[4,72,512]{2,1,0:T(8,128)(2,1)S(1)}, u32[]{:S(2)}, u32[]{:S(2)}) %all-to-all-start) | async-done | bytes 294944 | tf_op jit(solution)/shard_map/all_to_all | solution.py:1017
  15.1 2.1 collective-permute-start
  17.3 1.6 collective-permute-start.5
  18.8 2.6 %collective-permute-start.1 = (bf16[176,512]{1,0:T(8,128)(2,1)S(1)}, bf16[176,512]{1,0:T(8,128)(2,1)S(1)}, u32[]{:S(2)}, u32[]{:S(2)}) collective-permute-start(bf16[176,512]{1,0:T(8,128)(2,1)S(1)} %fusion.6.refs_0_), channel_id=1, source_target_pairs={{0,4},{1,5},{2,6},{3,7},{4,0},{5,1},{6,2},{7,3},{8,12},{9,13},{10,... | collective-permute-start | bytes 540680 | tf_op jit(solution)/shard_map/ppermute | solution.py:45
  21.8 3.1 %collective-permute-start.4 = (bf16[176,512]{1,0:T(8,128)(2,1)S(1)}, bf16[176,512]{1,0:T(8,128)(2,1)S(1)}, u32[]{:S(2)}, u32[]{:S(2)}) collective-permute-start(bf16[176,512]{1,0:T(8,128)(2,1)S(1)} %fusion.6.refs_0_), channel_id=1, source_target_pairs={{0,1},{1,0},{2,3},{3,2},{4,5},{5,4},{6,7},{7,6},{8,9},{9,8},{10,11... | collective-permute-start | bytes 540680 | tf_op jit(solution)/shard_map/ppermute | solution.py:45
  25.0 9.1 %collective-permute-done.1.refs_2_ = bf16[176,512]{1,0:T(8,128)(2,1)S(1)} collective-permute-done((bf16[176,512]{1,0:T(8,128)(2,1)S(1)}, bf16[176,512]{1,0:T(8,128)(2,1)S(1)}, u32[]{:S(2)}, u32[]{:S(2)}) %collective-permute-start.1) | collective-permute-done | bytes 180256 | tf_op jit(solution)/shard_map/ppermute | solution.py:45
  34.1 1.1 collective-permute-start.6
  36.2 2.6 %collective-permute-start.10 = (bf16[256,512]{1,0:T(8,128)(2,1)S(1)}, bf16[256,512]{1,0:T(8,128)(2,1)S(1)}, u32[]{:S(2)}, u32[]{:S(2)}) collective-permute-start(bf16[256,512]{1,0:T(8,128)(2,1)S(1)} %pad_maximum_fusion.3.refs_0_), channel_id=1, source_target_pairs={{0,2},{1,3},{2,0},{3,1},{4,6},{5,7},{6,4},{7,5},{8,10},{9,11},{10,... | collective-permute-start | bytes 786440 | tf_op jit(solution)/shard_map/ppermute | solution.py:45
  38.8 6.0 %collective-permute-done.7.refs_2_ = bf16[2,128,1024]{2,1,0:T(8,128)(2,1)} collective-permute-done((bf16[2,128,1024]{2,1,0:T(8,128)(2,1)}, bf16[2,128,1024]{2,1,0:T(8,128)(2,1)}, u32[]{:S(2)}, u32[]{:S(2)}) %collective-permute-start.7) | collective-permute-done | bytes 524320 | tf_op jit(solution)/shard_map/ppermute | solution.py:45
  44.8 6.3 %collective-permute-start.11 = (bf16[256,512]{1,0:T(8,128)(2,1)S(1)}, bf16[256,512]{1,0:T(8,128)(2,1)S(1)}, u32[]{:S(2)}, u32[]{:S(2)}) collective-permute-start(bf16[256,512]{1,0:T(8,128)(2,1)S(1)} %pad_maximum_fusion.3.refs_0_), channel_id=1, source_target_pairs={{0,4},{1,5},{2,6},{3,7},{4,0},{5,1},{6,2},{7,3},{8,12},{9,13},{10,... | collective-permute-start | bytes 786440 | tf_op jit(solution)/shard_map/ppermute | solution.py:45
  51.1 1.2 collective-permute-start.12
  52.3 0.8 assemble_first.1
  53.2 1.0 copy-done.1
  54.1 0.7 copy-done.3
  56.0 7.7 %enter.1 = (bf16[2,512,1024]{2,1,0:T(8,128)(2,1)}, bf16[2,512,512]{2,1,0:T(8,128)(2,1)}, f32[2,512,512]{2,1,0:T(8,128)}, bf16[2,512,512]{2,1,0:T(8,128)(2,1)}, f32[48,1024]{1,0:T(8,128)}, /*index=5*/f32[48,1024]{1,0:T(8,128)}) custom-call(s32[2]{0:T(128)} %copy-done.17, f32[1,1024]{1,0:T(1,128)} %copy-done.20, bf16[1024,512]{1,0:T(8,128)(2,1)} %copy-done.1, ...), custom_call_target="tpu_custom_call" | custom-call | flops 560000000 | bytes 2100000 | tf_op jit(solution)/shard_map/enter/pallas_call | solution.py:308
  63.7 3.3 %collective-permute-done.11.refs_2_ = bf16[256,512]{1,0:T(8,128)(2,1)S(1)} collective-permute-done((bf16[256,512]{1,0:T(8,128)(2,1)S(1)}, bf16[256,512]{1,0:T(8,128)(2,1)S(1)}, u32[]{:S(2)}, u32[]{:S(2)}) %collective-permute-start.11) | collective-permute-done | bytes 262176 | tf_op jit(solution)/shard_map/ppermute | solution.py:45
  67.0 1.7 collective-permute-done.13
  68.7 0.9 add.55
  69.6 1.0 pad_maximum_fusion
  70.6 1.9 collective-permute-start.16
  72.5 0.7 collective-permute-start.14
  73.7 5.4 %collective-permute-done.14 = f32[48,1024]{1,0:T(8,128)S(1)} collective-permute-done((f32[48,1024]{1,0:T(8,128)S(1)}, f32[48,1024]{1,0:T(8,128)S(1)}, u32[]{:S(2)}, u32[]{:S(2)}) %collective-permute-start.14) | collective-permute-done | bytes 196640 | tf_op jit(solution)/shard_map/ppermute | solution.py:45
  79.3 1.3 collective-permute-done.15
  80.5 0.7 maximum_select_fusion
  81.2 15.0 %scan_forward.1 = (f32[2,512,512]{2,1,0:T(8,128)}, bf16[2,8192,512]{2,1,0:T(8,128)(2,1)}, f32[2,512,512]{2,1,0:T(8,128)}, f32[2,512,512]{2,1,0:T(8,128)}) custom-call(bf16[96,1024]{1,0:T(8,128)(2,1)} %bitcast.105, bf16[2,512,512]{2,1,0:T(8,128)(2,1)} %get-tuple-element.155.act_ref, bf16[512,256]{1,0:T(8,128)(2,1)} %copy-done.3, f32[8,512]{1,0:T(8,128)} %copy-done.10, ...), custom_call_target="tpu_custom_call" | custom-call | flops 1440000000 | bytes 5400000 | tf_op jit(solution)/shard_map/scan_forward/pallas_call | solution.py:405
  96.3 0.7 assemble_second.1
  97.0 1.0 copy-done.2
  98.0 1.0 copy-done.4
  99.0 14.3 %middle.1 = (f32[2,128,1024]{2,1,0:T(8,128)}, bf16[2,128,1024]{2,1,0:T(8,128)(2,1)}, f32[2,128,1024]{2,1,0:T(8,128)}, bf16[2,128,1024]{2,1,0:T(8,128)(2,1)}, bf1...) custom-call(s32[2]{0:T(128)} %copy-done.17, ...), custom_call_target="tpu_custom_call" | custom-call | flops 720000000 | bytes 2700000 | tf_op jit(solution)/shard_map/middle/pallas_call | solution.py:510
  113.6 7.1 %all-to-all-start.1 = ((bf16[32,32,512]{2,1,0:T(8,128)(2,1)}), bf16[32,32,512]{2,1,0:T(8,128)(2,1)S(1)}, u32[]{:S(2)}, u32[]{:S(2)}) async-start(bf16[32,32,512]{2,1,0:T(8,128)(2,1)} %bitcast.111), calls=%async_computation.1 | async-start | bytes 2097152 | tf_op jit(solution)/shard_map/all_to_all | solution.py:1113
  120.9 25.7 %scan_backward.1 = (bf16[2,512,512]{2,1,0:T(8,128)(2,1)}, f32[2,512,512]{2,1,0:T(8,128)}, f32[48,1024]{1,0:T(8,128)}, f32[48,1024]{1,0:T(8,128)}, f32[16,512]{1,0:T(8,128)}) custom-call(s32[2]{0:T(128)} %copy-done.17, bf16[96,1024]{1,0:T(8,128)(2,1)} %bitcast.106, bf16[2,512,512]{2,1,0:T(8,128)(2,1)} %get-tuple-element.155.act_ref, ...), custom_call_target="tpu_custom_call" | custom-call | flops 2240000000 | bytes 8400000 | tf_op jit(solution)/shard_map/scan_backward/pallas_call | solution.py:646
  146.8 0.8 slice_bitcast_fusion.1
  147.6 0.7 slice_bitcast_fusion
  148.7 1.1 collective-permute-done.21
  149.9 1.7 collective-permute-start.22
  151.5 1.2 add_convert_fusion.1
  153.2 1.8 collective-permute-done.22
  155.1 1.7 collective-permute-start.24
  156.8 2.4 %collective-permute-start.25 = (bf16[64,1024]{1,0:T(8,128)(2,1)}, bf16[64,1024]{1,0:T(8,128)(2,1)S(1)}, u32[]{:S(2)}, u32[]{:S(2)}) collective-permute-start(bf16[64,1024]{1,0:T(8,128)(2,1)} %get-tuple-element.198), channel_id=1, source_target_pairs={{0,4},{1,5},{2,6},{3,7},{4,0},{5,1},{6,2},{7,3},{8,12},{9,13},{10,... | collective-permute-start | bytes 393224 | tf_op jit(solution)/shard_map/ppermute | solution.py:45
  159.6 0.7 maximum_select_fusion.1
  160.3 10.3 %leave.1 = (bf16[2,512,512]{2,1,0:T(8,128)(2,1)}, bf16[1024,512]{1,0:T(8,128)(2,1)}, f32[512,192]{1,0:T(8,128)}) custom-call(f32[2,512,512]{2,1,0:T(8,128)} %get-tuple-element.175.gact_ref, bf16[96,1024]{1,0:T(8,128)(2,1)} %bitcast.114, bf16[96,1024]{1,0:T(8,128)(2,1)} %bitcast.107, bf16[2,512,512]{2,1,0:T(8,128)(2,1)} %get-tuple-element.186.gsp_ref, ...), custom_call_target="tpu_custom_call" | custom-call | flops 640000000 | bytes 2400000 | tf_op jit(solution)/shard_map/leave/pallas_call | solution.py:769
  170.6 0.8 copy-done.29
  171.4 6.2 %all-to-all-start.2 = ((bf16[32,32,512]{2,1,0:T(8,128)(2,1)}), bf16[32,32,512]{2,1,0:T(8,128)(2,1)S(1)}, u32[]{:S(2)}, u32[]{:S(2)}) async-start(bf16[32,32,512]{2,1,0:T(8,128)(2,1)} %bitcast.112), calls=%async_computation.2 | async-start | bytes 2097152 | tf_op jit(solution)/shard_map/all_to_all | solution.py:1130
  178.5 1.8 collective-permute-start.30
  180.2 6.6 %rows_back.1 = (f32[2,128,1024]{2,1,0:T(8,128)}, bf16[2,128,1024]{2,1,0:T(8,128)(2,1)}, f32[2,128,1024]{2,1,0:T(8,128)}, bf16[2,128,1024]{2,1,0:T(8,128)(2,1)}) custom-call(s32[2]{0:T(128)} %copy-done.17, bf16[2,512,512]{2,1,0:T(8,128)(2,1)} %get-tuple-element.208.gci_ref, bf16[2,512,512]{2,1,0:T(8,128)(2,1)} %get-tuple-element.209.ggp_ref, ...), custom_call_target="tpu_custom_call" | custom-call | flops 400000000 | bytes 1500000 | tf_op jit(solution)/shard_map/rows_back/pallas_call | solution.py:826
  187.4 6.5 %collective-permute-done.30 = bf16[4,64,192]{2,1,0:T(8,128)(2,1)} collective-permute-done((bf16[4,64,192]{2,1,0:T(8,128)(2,1)}, bf16[4,64,192]{2,1,0:T(8,128)(2,1)}, u32[]{:S(2)}, u32[]{:S(2)}) %collective-permute-start.30) | collective-permute-done | bytes 98336 | tf_op jit(solution)/shard_map/ppermute | solution.py:45
  193.9 1.0 fusion.9
  194.9 2.2 add_convert_fusion
  197.1 2.0 collective-permute-start.34
  199.0 2.4 %collective-permute-start.35 = (bf16[64,192]{1,0:T(8,128)(2,1)S(1)}, bf16[64,192]{1,0:T(8,128)(2,1)S(1)}, u32[]{:S(2)}, u32[]{:S(2)}) collective-permute-start(bf16[64,192]{1,0:T(8,128)(2,1)S(1)} %get-tuple-element.225), channel_id=1, source_target_pairs={{0,6},{1,7},{2,4},{3,5},{4,2},{5,3},{6,0},{7,1},{8,14},{9,15},{10,... | collective-permute-start | bytes 73736 | tf_op jit(solution)/shard_map/ppermute | solution.py:45
  201.5 1.0 convert_add_fusion.1.out_ref.refs_15_
  202.4 1.5 collective-permute-start.32
  204.0 2.4 %collective-permute-done.34 = bf16[64,192]{1,0:T(8,128)(2,1)S(1)} collective-permute-done((bf16[64,192]{1,0:T(8,128)(2,1)S(1)}, bf16[64,192]{1,0:T(8,128)(2,1)S(1)}, u32[]{:S(2)}, u32[]{:S(2)}) %collective-permute-start.34) | collective-permute-done | bytes 24608 | tf_op jit(solution)/shard_map/ppermute | solution.py:45
  206.6 1.2 collect.1
  207.8 0.8 copy-done.8
  208.6 3.1 %all-to-all-start.3 = ((f32[32,1,128]{2,1,0:T(1,128)}), f32[32,1,128]{2,1,0:T(1,128)S(1)}, u32[]{:S(2)}, u32[]{:S(2)}) async-start(f32[32,1,128]{2,1,0:T(1,128)} %get-tuple-element.226), calls=%async_computation.3 | async-start | bytes 32768 | tf_op jit(solution)/shard_map/all_to_all | solution.py:1155
  211.7 2.8 %fusion.1 = bf16[2,1,128,1024]{3,2,1,0:T(8,128)(2,1)} fusion(bf16[2,128,1024]{2,1,0:T(8,128)(2,1)} %copy-done.29, f32[2,128,1024]{2,1,0:T(8,128)} %get-tuple-element.205, bf16[2,128,1024]{2,1,0:T(8,128)(2,1)} %collective-permute-done.19, bf16[2,1,128,1024]{3,2,1,0:T(8,128)(2,1)} %param.16), kind=kLoop, calls=%fused_computation.12 | loop fusion | flops 1835008 | bytes 3145728
  214.5 1.0 collective-permute-done.32.refs_2_
  215.5 3.1 %finish.1 = f32[2,128,1024]{2,1,0:T(8,128)} custom-call(bf16[2,128,1024]{2,1,0:T(8,128)(2,1)} %bitcast.12.refs_0_.tok_ref, bf16[2,128,1024]{2,1,0:T(8,128)(2,1)} %bitcast.19.refs_0_.cot_ref, f32[1,1024]{1,0:T(1,128)} %copy-done.20, f32[2,128,1024]{2,1,0:T(8,128)} %get-tuple-element.227.refs_0_, bf16[2,128,1024]{2,1,0:T(8,128)(2,1)} %collective-permute-done.29.refs_1_, ...), custom_call_target="tpu_custom_call" | custom-call | flops 240000000 | bytes 900000 | tf_op jit(solution)/shard_map/finish/pallas_call | solution.py:862
  218.8 2.5 %adam.1 = (f32[2,32,4096]{2,1,0:T(8,128)}, f32[32,4096]{1,0:T(8,128)}, f32[2,64,1024]{2,1,0:T(8,128)}, f32[64,1024]{1,0:T(8,128)}, f32[2,64,96]{2,1,0:T(8,128)},...) custom-call(f32[32,1,128]{2,1,0:T(1,128)S(1)} %all-to-all-done.3.squ, ...), custom_call_target="tpu_custom_call" | custom-call | flops 320000000 | bytes 1200000 | tf_op jit(solution)/shard_map/adam/pallas_call | solution.py:970
  (148 shorter events, 9.2 us)
Async XLA Ops:
  0.7 9.6 %copy-start.15 = (f32[16,64]{1,0:T(8,128)S(1)}, f32[16,64]{1,0:T(8,128)}, u32[]{:S(2)}) copy-start(f32[16,64]{1,0:T(8,128)} %refs_5_.1) | copy-start | bytes 12292
  0.7 9.7 %copy-start.21 = (f32[7,64]{1,0:T(8,128)S(1)}, f32[7,64]{1,0:T(8,128)}, u32[]{:S(2)}) copy-start(f32[7,64]{1,0:T(8,128)} %refs_4_.1) | copy-start | bytes 5380
  0.7 9.8 %copy-start.12 = (f32[64,64]{1,0:T(8,128)S(1)}, f32[64,64]{1,0:T(8,128)}, u32[]{:S(2)}) copy-start(f32[64,64]{1,0:T(8,128)} %refs_3_.1) | copy-start | bytes 49156
  0.7 9.9 %copy-start.11 = (f32[64,96]{1,0:T(8,128)S(1)}, f32[64,96]{1,0:T(8,128)}, u32[]{:S(2)}) copy-start(f32[64,96]{1,0:T(8,128)} %refs_2_.1) | copy-start | bytes 73732
  0.7 9.9 %copy-start.5 = (f32[64,1024]{1,0:T(8,128)S(1)}, f32[64,1024]{1,0:T(8,128)}, u32[]{:S(2)}) copy-start(f32[64,1024]{1,0:T(8,128)} %refs_1_.1) | copy-start | bytes 786436
  3.8 11.3 %all-to-all-start = ((bf16[4,72,512]{2,1,0:T(8,128)(2,1)}), bf16[4,72,512]{2,1,0:T(8,128)(2,1)S(1)}, u32[]{:S(2)}, u32[]{:S(2)}) async-start(bf16[4,72,512]{2,1,0:T(8,128)(2,1)} %copy.70), calls=%async_computation | async-start | bytes 589824 | tf_op jit(solution)/shard_map/all_to_all | solution.py:1017
  8.0 26.0 %collective-permute-start.3 = (bf16[2,128,1024]{2,1,0:T(8,128)(2,1)}, bf16[2,128,1024]{2,1,0:T(8,128)(2,1)}, u32[]{:S(2)}, u32[]{:S(2)}) collective-permute-start(bf16[2,128,1024]{2,1,0:T(8,128)(2,1)} %bitcast.12.refs_0_.tok_ref), channel_id=1, source_target_pairs={{0,16},{8,24},{16,0},{24,8},{1,17},{9,25},{17,1},{25,9},{2,18},{10... | collective-permute-start | bytes 1572872 | tf_op jit(solution)/shard_map/ppermute | solution.py:45
  15.1 6.7 %collective-permute-start = (bf16[176,512]{1,0:T(8,128)(2,1)S(1)}, bf16[176,512]{1,0:T(8,128)(2,1)S(1)}, u32[]{:S(2)}, u32[]{:S(2)}) collective-permute-start(bf16[176,512]{1,0:T(8,128)(2,1)S(1)} %fusion.6.refs_0_), channel_id=1, source_target_pairs={{0,2},{1,3},{2,0},{3,1},{4,6},{5,7},{6,4},{7,5},{8,10},{9,11},{10,... | collective-permute-start | bytes 540680 | tf_op jit(solution)/shard_map/ppermute | solution.py:45
  17.3 16.8 %collective-permute-start.5 = (bf16[256,512]{1,0:T(8,128)(2,1)S(1)}, bf16[256,512]{1,0:T(8,128)(2,1)S(1)}, u32[]{:S(2)}, u32[]{:S(2)}) collective-permute-start(bf16[256,512]{1,0:T(8,128)(2,1)S(1)} %pad_maximum_fusion.3.refs_0_), channel_id=1, source_target_pairs={{0,1},{1,0},{2,3},{3,2},{4,5},{5,4},{6,7},{7,6},{8,9},{9,8},{10,11... | collective-permute-start | bytes 786440 | tf_op jit(solution)/shard_map/ppermute | solution.py:45
  18.8 15.2 %collective-permute-start.1 = (bf16[176,512]{1,0:T(8,128)(2,1)S(1)}, bf16[176,512]{1,0:T(8,128)(2,1)S(1)}, u32[]{:S(2)}, u32[]{:S(2)}) collective-permute-start(bf16[176,512]{1,0:T(8,128)(2,1)S(1)} %fusion.6.refs_0_), channel_id=1, source_target_pairs={{0,4},{1,5},{2,6},{3,7},{4,0},{5,1},{6,2},{7,3},{8,12},{9,13},{10,... | collective-permute-start | bytes 540680 | tf_op jit(solution)/shard_map/ppermute | solution.py:45
  21.4 12.6 %collective-permute-start.2 = (bf16[176,512]{1,0:T(8,128)(2,1)S(1)}, bf16[176,512]{1,0:T(8,128)(2,1)S(1)}, u32[]{:S(2)}, u32[]{:S(2)}) collective-permute-start(bf16[176,512]{1,0:T(8,128)(2,1)S(1)} %fusion.6.refs_0_), channel_id=1, source_target_pairs={{0,6},{1,7},{2,4},{3,5},{4,2},{5,3},{6,0},{7,1},{8,14},{9,15},{10,... | collective-permute-start | bytes 540680 | tf_op jit(solution)/shard_map/ppermute | solution.py:45
  21.8 12.2 %collective-permute-start.4 = (bf16[176,512]{1,0:T(8,128)(2,1)S(1)}, bf16[176,512]{1,0:T(8,128)(2,1)S(1)}, u32[]{:S(2)}, u32[]{:S(2)}) collective-permute-start(bf16[176,512]{1,0:T(8,128)(2,1)S(1)} %fusion.6.refs_0_), channel_id=1, source_target_pairs={{0,1},{1,0},{2,3},{3,2},{4,5},{5,4},{6,7},{7,6},{8,9},{9,8},{10,11... | collective-permute-start | bytes 540680 | tf_op jit(solution)/shard_map/ppermute | solution.py:45
  34.1 17.0 %collective-permute-start.6 = (bf16[3,176,512]{2,1,0:T(8,128)(2,1)S(1)}, bf16[3,176,512]{2,1,0:T(8,128)(2,1)S(1)}, u32[]{:S(2)}, u32[]{:S(2)}) collective-permute-start(bf16[3,176,512]{2,1,0:T(8,128)(2,1)S(1)} %pad_maximum_fusion.1), channel_id=1, source_target_pairs={{0,1},{1,0},{2,3},{3,2},{4,5},{5,4},{6,7},{7,6},{8,9},{9,8},{10,11... | collective-permute-start | bytes 1622024 | tf_op jit(solution)/shard_map/ppermute | solution.py:45
  35.2 9.7 %collective-permute-start.7 = (bf16[2,128,1024]{2,1,0:T(8,128)(2,1)}, bf16[2,128,1024]{2,1,0:T(8,128)(2,1)}, u32[]{:S(2)}, u32[]{:S(2)}) collective-permute-start(bf16[2,128,1024]{2,1,0:T(8,128)(2,1)} %bitcast.19.refs_0_.cot_ref), channel_id=1, source_target_pairs={{0,16},{8,24},{16,0},{24,8},{1,17},{9,25},{17,1},{25,9},{2,18},{10... | collective-permute-start | bytes 1572872 | tf_op jit(solution)/shard_map/ppermute | solution.py:45
  35.7 20.3 %collective-permute-start.8 = (bf16[2,128,1024]{2,1,0:T(8,128)(2,1)}, bf16[2,128,1024]{2,1,0:T(8,128)(2,1)}, u32[]{:S(2)}, u32[]{:S(2)}) collective-permute-start(bf16[2,128,1024]{2,1,0:T(8,128)(2,1)} %bitcast.12.refs_0_.tok_ref), channel_id=1, source_target_pairs={{0,8},{8,0},{16,24},{24,16},{1,9},{9,1},{17,25},{25,17},{2,10},{10... | collective-permute-start | bytes 1572872 | tf_op jit(solution)/shard_map/ppermute | solution.py:45
  35.7 20.3 %collective-permute-start.9 = (bf16[2,128,1024]{2,1,0:T(8,128)(2,1)}, bf16[2,128,1024]{2,1,0:T(8,128)(2,1)}, u32[]{:S(2)}, u32[]{:S(2)}) collective-permute-start(bf16[2,128,1024]{2,1,0:T(8,128)(2,1)} %collective-permute-done.3.refs_2_), channel_id=1, source_target_pairs={{0,8},{8,0},{16,24},{24,16},{1,9},{9,1},{17,25},{25,17},{2,10},{10... | collective-permute-start | bytes 1572872 | tf_op jit(solution)/shard_map/ppermute | solution.py:45
  36.2 27.5 %collective-permute-start.10 = (bf16[256,512]{1,0:T(8,128)(2,1)S(1)}, bf16[256,512]{1,0:T(8,128)(2,1)S(1)}, u32[]{:S(2)}, u32[]{:S(2)}) collective-permute-start(bf16[256,512]{1,0:T(8,128)(2,1)S(1)} %pad_maximum_fusion.3.refs_0_), channel_id=1, source_target_pairs={{0,2},{1,3},{2,0},{3,1},{4,6},{5,7},{6,4},{7,5},{8,10},{9,11},{10,... | collective-permute-start | bytes 786440 | tf_op jit(solution)/shard_map/ppermute | solution.py:45
  44.8 22.2 %collective-permute-start.11 = (bf16[256,512]{1,0:T(8,128)(2,1)S(1)}, bf16[256,512]{1,0:T(8,128)(2,1)S(1)}, u32[]{:S(2)}, u32[]{:S(2)}) collective-permute-start(bf16[256,512]{1,0:T(8,128)(2,1)S(1)} %pad_maximum_fusion.3.refs_0_), channel_id=1, source_target_pairs={{0,4},{1,5},{2,6},{3,7},{4,0},{5,1},{6,2},{7,3},{8,12},{9,13},{10,... | collective-permute-start | bytes 786440 | tf_op jit(solution)/shard_map/ppermute | solution.py:45
  51.1 15.9 %collective-permute-start.12 = (bf16[256,512]{1,0:T(8,128)(2,1)S(1)}, bf16[256,512]{1,0:T(8,128)(2,1)S(1)}, u32[]{:S(2)}, u32[]{:S(2)}) collective-permute-start(bf16[256,512]{1,0:T(8,128)(2,1)S(1)} %pad_maximum_fusion.3.refs_0_), channel_id=1, source_target_pairs={{0,6},{1,7},{2,4},{3,5},{4,2},{5,3},{6,0},{7,1},{8,14},{9,15},{10,... | collective-permute-start | bytes 786440 | tf_op jit(solution)/shard_map/ppermute | solution.py:45
  52.3 3.7 %copy-start.17 = (s32[2]{0:T(128)}, s32[2]{0:T(128)S(1)}, u32[]{:S(2)}) copy-start(s32[2]{0:T(128)S(1)} %pad_add_fusion.me_ref) | copy-start | bytes 28
  56.0 14.6 %copy-start.16 = (f32[16,512]{1,0:T(8,128)}, f32[16,512]{1,0:T(8,128)S(1)}, u32[]{:S(2)}) copy-start(f32[16,512]{1,0:T(8,128)S(1)} %get-tuple-element.156.a_ref) | copy-start | bytes 98308
  67.0 1.7 collective-permute-start.13
  70.6 25.7 %collective-permute-start.16 = (bf16[3,256,512]{2,1,0:T(8,128)(2,1)}, bf16[3,256,512]{2,1,0:T(8,128)(2,1)S(1)}, u32[]{:S(2)}, u32[]{:S(2)}) collective-permute-start(bf16[3,256,512]{2,1,0:T(8,128)(2,1)} %pad_maximum_fusion), channel_id=1, source_target_pairs={{0,1},{1,0},{2,3},{3,2},{4,5},{5,4},{6,7},{7,6},{8,9},{9,8},{10,11... | collective-permute-start | bytes 2359304 | tf_op jit(solution)/shard_map/ppermute | solution.py:45
  72.5 6.7 %collective-permute-start.14 = (f32[48,1024]{1,0:T(8,128)S(1)}, f32[48,1024]{1,0:T(8,128)S(1)}, u32[]{:S(2)}, u32[]{:S(2)}) collective-permute-start(f32[48,1024]{1,0:T(8,128)S(1)} %add.55), channel_id=1, source_target_pairs={{0,16},{8,24},{16,0},{24,8},{1,17},{9,25},{17,1},{25,9},{2,18},{10... | collective-permute-start | bytes 589832 | tf_op jit(solution)/shard_map/ppermute | solution.py:45
  73.2 25.8 %collective-permute-start.17 = (bf16[2,128,1024]{2,1,0:T(8,128)(2,1)}, bf16[2,128,1024]{2,1,0:T(8,128)(2,1)}, u32[]{:S(2)}, u32[]{:S(2)}) collective-permute-start(bf16[2,128,1024]{2,1,0:T(8,128)(2,1)} %bitcast.19.refs_0_.cot_ref), channel_id=1, source_target_pairs={{0,8},{8,0},{16,24},{24,16},{1,9},{9,1},{17,25},{25,17},{2,10},{10... | collective-permute-start | bytes 1572872 | tf_op jit(solution)/shard_map/ppermute | solution.py:45
  73.2 25.8 %collective-permute-start.18 = (bf16[2,128,1024]{2,1,0:T(8,128)(2,1)}, bf16[2,128,1024]{2,1,0:T(8,128)(2,1)}, u32[]{:S(2)}, u32[]{:S(2)}) collective-permute-start(bf16[2,128,1024]{2,1,0:T(8,128)(2,1)} %collective-permute-done.7.refs_2_), channel_id=1, source_target_pairs={{0,8},{8,0},{16,24},{24,16},{1,9},{9,1},{17,25},{25,17},{2,10},{10... | collective-permute-start | bytes 1572872 | tf_op jit(solution)/shard_map/ppermute | solution.py:45
  79.2 1.4 collective-permute-start.15
  81.2 15.1 %copy-start.18 = (s32[2]{0:T(128)S(1)}, s32[2]{0:T(128)}, u32[]{:S(2)}) copy-start(s32[2]{0:T(128)} %copy-done.17) | copy-start | bytes 28
  113.3 33.3 %collective-permute-start.20 = (bf16[4,64,1024]{2,1,0:T(8,128)(2,1)}, bf16[4,64,1024]{2,1,0:T(8,128)(2,1)S(1)}, u32[]{:S(2)}, u32[]{:S(2)}) collective-permute-start(bf16[4,64,1024]{2,1,0:T(8,128)(2,1)} %get-tuple-element.181), channel_id=1, source_target_pairs={{0,1},{1,0},{2,3},{3,2},{4,5},{5,4},{6,7},{7,6},{8,9},{9,8},{10,11... | collective-permute-start | bytes 1572872 | tf_op jit(solution)/shard_map/ppermute | solution.py:45
  113.6 34.7 %collective-permute-start.19 = (bf16[2,128,1024]{2,1,0:T(8,128)(2,1)}, bf16[2,128,1024]{2,1,0:T(8,128)(2,1)}, u32[]{:S(2)}, u32[]{:S(2)}) collective-permute-start(bf16[2,128,1024]{2,1,0:T(8,128)(2,1)} %get-tuple-element.179), channel_id=1, source_target_pairs={{0,8},{8,0},{16,24},{24,16},{1,9},{9,1},{17,25},{25,17},{2,10},{10... | collective-permute-start | bytes 1572872 | tf_op jit(solution)/shard_map/ppermute | solution.py:45
  113.6 46.6 %all-to-all-start.1 = ((bf16[32,32,512]{2,1,0:T(8,128)(2,1)}), bf16[32,32,512]{2,1,0:T(8,128)(2,1)S(1)}, u32[]{:S(2)}, u32[]{:S(2)}) async-start(bf16[32,32,512]{2,1,0:T(8,128)(2,1)} %bitcast.111), calls=%async_computation.1 | async-start | bytes 2097152 | tf_op jit(solution)/shard_map/all_to_all | solution.py:1113
  120.8 30.8 %collective-permute-start.27 = (bf16[2,128,1024]{2,1,0:T(8,128)(2,1)}, bf16[2,128,1024]{2,1,0:T(8,128)(2,1)}, u32[]{:S(2)}, u32[]{:S(2)}) collective-permute-start(bf16[2,128,1024]{2,1,0:T(8,128)(2,1)} %get-tuple-element.203), channel_id=1, source_target_pairs={{0,8},{8,0},{16,24},{24,16},{1,9},{9,1},{17,25},{25,17},{2,10},{10... | collective-permute-start | bytes 1572872 | tf_op jit(solution)/shard_map/ppermute | solution.py:45
  120.9 25.7 %copy-start.27 = (bf16[4,64,1024]{2,1,0:T(8,128)(2,1)S(1)}, bf16[4,64,1024]{2,1,0:T(8,128)(2,1)}, u32[]{:S(2)}) copy-start(bf16[4,64,1024]{2,1,0:T(8,128)(2,1)} %get-tuple-element.180) | copy-start | bytes 1572868
  146.6 4.9 %copy-start.26 = (f32[2,128,1024]{2,1,0:T(8,128)S(1)}, f32[2,128,1024]{2,1,0:T(8,128)}, u32[]{:S(2)}) copy-start(f32[2,128,1024]{2,1,0:T(8,128)} %get-tuple-element.202) | copy-start | bytes 3145732
  148.3 1.5 collective-permute-start.21
  149.9 5.1 %collective-permute-start.22 = (bf16[48,1024]{1,0:T(8,128)(2,1)S(1)}, bf16[48,1024]{1,0:T(8,128)(2,1)S(1)}, u32[]{:S(2)}, u32[]{:S(2)}) collective-permute-start(bf16[48,1024]{1,0:T(8,128)(2,1)S(1)} %get-tuple-element.321), channel_id=1, source_target_pairs={{0,16},{8,24},{16,0},{24,8},{1,17},{9,25},{17,1},{25,9},{2,18},{10... | collective-permute-start | bytes 294920 | tf_op jit(solution)/shard_map/ppermute | solution.py:45
  152.7 17.9 %collective-permute-start.28 = (bf16[2,128,1024]{2,1,0:T(8,128)(2,1)S(1)}, bf16[2,128,1024]{2,1,0:T(8,128)(2,1)S(1)}, u32[]{:S(2)}, u32[]{:S(2)}) collective-permute-start(bf16[2,128,1024]{2,1,0:T(8,128)(2,1)S(1)} %add_convert_fusion.1), channel_id=1, source_target_pairs={{0,16},{8,24},{16,0},{24,8},{1,17},{9,25},{17,1},{25,9},{2,18},{10... | collective-permute-start | bytes 1572872 | tf_op jit(solution)/shard_map/ppermute | solution.py:45
  155.0 4.5 %collective-permute-start.23 = (bf16[48,1024]{1,0:T(8,128)(2,1)S(1)}, bf16[48,1024]{1,0:T(8,128)(2,1)S(1)}, u32[]{:S(2)}, u32[]{:S(2)}) collective-permute-start(bf16[48,1024]{1,0:T(8,128)(2,1)S(1)} %add_convert_fusion.2), channel_id=1, source_target_pairs={{0,8},{8,0},{16,24},{24,16},{1,9},{9,1},{17,25},{25,17},{2,10},{10... | collective-permute-start | bytes 294920 | tf_op jit(solution)/shard_map/ppermute | solution.py:45
  155.1 15.5 %collective-permute-start.24 = (bf16[64,1024]{1,0:T(8,128)(2,1)}, bf16[64,1024]{1,0:T(8,128)(2,1)S(1)}, u32[]{:S(2)}, u32[]{:S(2)}) collective-permute-start(bf16[64,1024]{1,0:T(8,128)(2,1)} %get-tuple-element.197), channel_id=1, source_target_pairs={{0,2},{1,3},{2,0},{3,1},{4,6},{5,7},{6,4},{7,5},{8,10},{9,11},{10,... | collective-permute-start | bytes 393224 | tf_op jit(solution)/shard_map/ppermute | solution.py:45
  156.8 13.8 %collective-permute-start.25 = (bf16[64,1024]{1,0:T(8,128)(2,1)}, bf16[64,1024]{1,0:T(8,128)(2,1)S(1)}, u32[]{:S(2)}, u32[]{:S(2)}) collective-permute-start(bf16[64,1024]{1,0:T(8,128)(2,1)} %get-tuple-element.198), channel_id=1, source_target_pairs={{0,4},{1,5},{2,6},{3,7},{4,0},{5,1},{6,2},{7,3},{8,12},{9,13},{10,... | collective-permute-start | bytes 393224 | tf_op jit(solution)/shard_map/ppermute | solution.py:45
  159.2 11.4 %collective-permute-start.26 = (bf16[64,1024]{1,0:T(8,128)(2,1)}, bf16[64,1024]{1,0:T(8,128)(2,1)}, u32[]{:S(2)}, u32[]{:S(2)}) collective-permute-start(bf16[64,1024]{1,0:T(8,128)(2,1)} %get-tuple-element.199), channel_id=1, source_target_pairs={{0,6},{1,7},{2,4},{3,5},{4,2},{5,3},{6,0},{7,1},{8,14},{9,15},{10,... | collective-permute-start | bytes 393224 | tf_op jit(solution)/shard_map/ppermute | solution.py:45
  170.5 7.1 %copy-start.28 = (f32[512,192]{1,0:T(8,128)S(1)}, f32[512,192]{1,0:T(8,128)}, u32[]{:S(2)}) copy-start(f32[512,192]{1,0:T(8,128)} %get-tuple-element.212) | copy-start | bytes 1179652
  170.6 16.8 %copy-start.31 = (bf16[64,1024]{1,0:T(8,128)(2,1)}, bf16[64,1024]{1,0:T(8,128)(2,1)S(1)}, u32[]{:S(2)}) copy-start(bf16[64,1024]{1,0:T(8,128)(2,1)S(1)} %collective-permute-done.24) | copy-start | bytes 393220
  170.6 16.8 %copy-start.33 = (bf16[64,1024]{1,0:T(8,128)(2,1)}, bf16[64,1024]{1,0:T(8,128)(2,1)S(1)}, u32[]{:S(2)}) copy-start(bf16[64,1024]{1,0:T(8,128)(2,1)S(1)} %collective-permute-done.25) | copy-start | bytes 393220
  171.4 35.2 %all-to-all-start.2 = ((bf16[32,32,512]{2,1,0:T(8,128)(2,1)}), bf16[32,32,512]{2,1,0:T(8,128)(2,1)S(1)}, u32[]{:S(2)}, u32[]{:S(2)}) async-start(bf16[32,32,512]{2,1,0:T(8,128)(2,1)} %bitcast.112), calls=%async_computation.2 | async-start | bytes 2097152 | tf_op jit(solution)/shard_map/all_to_all | solution.py:1130
  178.5 15.4 %collective-permute-start.30 = (bf16[4,64,192]{2,1,0:T(8,128)(2,1)}, bf16[4,64,192]{2,1,0:T(8,128)(2,1)}, u32[]{:S(2)}, u32[]{:S(2)}) collective-permute-start(bf16[4,64,192]{2,1,0:T(8,128)(2,1)} %fusion.7), channel_id=1, source_target_pairs={{0,1},{1,0},{2,3},{3,2},{4,5},{5,4},{6,7},{7,6},{8,9},{9,8},{10,11... | collective-permute-start | bytes 294920 | tf_op jit(solution)/shard_map/ppermute | solution.py:45
  186.8 14.6 %copy-start.25 = (f32[64,1024]{1,0:T(8,128)S(1)}, f32[64,1024]{1,0:T(8,128)}, u32[]{:S(2)}) copy-start(f32[64,1024]{1,0:T(8,128)} %slice_bitcast_fusion) | copy-start | bytes 786436
  186.8 8.1 %collective-permute-start.31 = (bf16[2,128,1024]{2,1,0:T(8,128)(2,1)}, bf16[2,128,1024]{2,1,0:T(8,128)(2,1)S(1)}, u32[]{:S(2)}, u32[]{:S(2)}) collective-permute-start(bf16[2,128,1024]{2,1,0:T(8,128)(2,1)} %get-tuple-element.214), channel_id=1, source_target_pairs={{0,8},{8,0},{16,24},{24,16},{1,9},{9,1},{17,25},{25,17},{2,10},{10... | collective-permute-start | bytes 1572872 | tf_op jit(solution)/shard_map/ppermute | solution.py:45
  186.9 19.8 %copy-start = (f32[32,4096]{1,0:T(8,128)S(1)}, f32[32,4096]{1,0:T(8,128)}, u32[]{:S(2)}) copy-start(f32[32,4096]{1,0:T(8,128)} %refs_0_.1) | copy-start | bytes 1572868
  186.9 19.8 %copy-start.23 = (f32[32]{0:T(128)S(1)}, f32[32]{0:T(128)}, u32[]{:S(2)}) copy-start(f32[32]{0:T(128)} %param.24) | copy-start | bytes 388
  186.9 27.6 %collective-permute-start.29 = (bf16[2,128,1024]{2,1,0:T(8,128)(2,1)}, bf16[2,128,1024]{2,1,0:T(8,128)(2,1)}, u32[]{:S(2)}, u32[]{:S(2)}) collective-permute-start(bf16[2,128,1024]{2,1,0:T(8,128)(2,1)} %get-tuple-element.211), channel_id=1, source_target_pairs={{0,8},{8,0},{16,24},{24,16},{1,9},{9,1},{17,25},{25,17},{2,10},{10... | collective-permute-start | bytes 1572872 | tf_op jit(solution)/shard_map/ppermute | solution.py:45
  193.9 7.6 %copy-start.32 = (bf16[64,1024]{1,0:T(8,128)(2,1)S(1)}, bf16[64,1024]{1,0:T(8,128)(2,1)}, u32[]{:S(2)}) copy-start(bf16[64,1024]{1,0:T(8,128)(2,1)} %copy-done.31) | copy-start | bytes 393220
  193.9 7.6 %copy-start.34 = (bf16[64,1024]{1,0:T(8,128)(2,1)S(1)}, bf16[64,1024]{1,0:T(8,128)(2,1)}, u32[]{:S(2)}) copy-start(bf16[64,1024]{1,0:T(8,128)(2,1)} %copy-done.33) | copy-start | bytes 393220
  197.1 6.9 %collective-permute-start.33 = (bf16[64,192]{1,0:T(8,128)(2,1)S(1)}, bf16[64,192]{1,0:T(8,128)(2,1)S(1)}, u32[]{:S(2)}, u32[]{:S(2)}) collective-permute-start(bf16[64,192]{1,0:T(8,128)(2,1)S(1)} %get-tuple-element.223), channel_id=1, source_target_pairs={{0,2},{1,3},{2,0},{3,1},{4,6},{5,7},{6,4},{7,5},{8,10},{9,11},{10,... | collective-permute-start | bytes 73736 | tf_op jit(solution)/shard_map/ppermute | solution.py:45
  197.1 9.3 %collective-permute-start.34 = (bf16[64,192]{1,0:T(8,128)(2,1)S(1)}, bf16[64,192]{1,0:T(8,128)(2,1)S(1)}, u32[]{:S(2)}, u32[]{:S(2)}) collective-permute-start(bf16[64,192]{1,0:T(8,128)(2,1)S(1)} %get-tuple-element.224), channel_id=1, source_target_pairs={{0,4},{1,5},{2,6},{3,7},{4,0},{5,1},{6,2},{7,3},{8,12},{9,13},{10,... | collective-permute-start | bytes 73736 | tf_op jit(solution)/shard_map/ppermute | solution.py:45
  199.0 7.3 %collective-permute-start.35 = (bf16[64,192]{1,0:T(8,128)(2,1)S(1)}, bf16[64,192]{1,0:T(8,128)(2,1)S(1)}, u32[]{:S(2)}, u32[]{:S(2)}) collective-permute-start(bf16[64,192]{1,0:T(8,128)(2,1)S(1)} %get-tuple-element.225), channel_id=1, source_target_pairs={{0,6},{1,7},{2,4},{3,5},{4,2},{5,3},{6,0},{7,1},{8,14},{9,15},{10,... | collective-permute-start | bytes 73736 | tf_op jit(solution)/shard_map/ppermute | solution.py:45
  202.4 13.1 %collective-permute-start.32 = (bf16[2,128,1024]{2,1,0:T(8,128)(2,1)}, bf16[2,128,1024]{2,1,0:T(8,128)(2,1)}, u32[]{:S(2)}, u32[]{:S(2)}) collective-permute-start(bf16[2,128,1024]{2,1,0:T(8,128)(2,1)} %add_convert_fusion), channel_id=1, source_target_pairs={{0,16},{8,24},{16,0},{24,8},{1,17},{9,25},{17,1},{25,9},{2,18},{10... | collective-permute-start | bytes 1572872 | tf_op jit(solution)/shard_map/ppermute | solution.py:45
  208.6 10.1 %all-to-all-start.3 = ((f32[32,1,128]{2,1,0:T(1,128)}), f32[32,1,128]{2,1,0:T(1,128)S(1)}, u32[]{:S(2)}, u32[]{:S(2)}) async-start(f32[32,1,128]{2,1,0:T(1,128)} %get-tuple-element.226), calls=%async_computation.3 | async-start | bytes 32768 | tf_op jit(solution)/shard_map/all_to_all | solution.py:1155
  215.5 3.3 %copy-start.9 = (f32[32,4096]{1,0:T(8,128)S(1)}, f32[32,4096]{1,0:T(8,128)}, u32[]{:S(2)}) copy-start(f32[32,4096]{1,0:T(8,128)} %copy-done.8) | copy-start | bytes 1572868
  215.5 3.3 %copy-start.13 = (f32[2,64,96]{2,1,0:T(8,128)S(1)}, f32[2,64,96]{2,1,0:T(8,128)}, u32[]{:S(2)}) copy-start(f32[2,64,96]{2,1,0:T(8,128)} %refs_9_.1) | copy-start | bytes 147460
  215.5 3.3 %copy-start.14 = (f32[2,64,64]{2,1,0:T(8,128)S(1)}, f32[2,64,64]{2,1,0:T(8,128)}, u32[]{:S(2)}) copy-start(f32[2,64,64]{2,1,0:T(8,128)} %refs_10_.1) | copy-start | bytes 98308
  215.5 3.3 %copy-start.19 = (f32[2,16,64]{2,1,0:T(8,128)S(1)}, f32[2,16,64]{2,1,0:T(8,128)}, u32[]{:S(2)}) copy-start(f32[2,16,64]{2,1,0:T(8,128)} %refs_12_.1) | copy-start | bytes 24580
  215.5 3.3 %copy-start.22 = (f32[2,7,64]{2,0,1:T(2,128)S(1)}, f32[2,7,64]{2,0,1:T(2,128)}, u32[]{:S(2)}) copy-start(f32[2,7,64]{2,0,1:T(2,128)} %param.29) | copy-start | bytes 10756
  215.5 3.3 %copy-start.24 = (f32[2,32]{1,0:T(2,128)S(1)}, f32[2,32]{1,0:T(2,128)}, u32[]{:S(2)}) copy-start(f32[2,32]{1,0:T(2,128)} %param.31) | copy-start | bytes 772
  (12 other events, 17.9 us)

commit v2 on v1

--- a/solution.py
+++ b/solution.py
@@ -211,7 +211,7 @@
                 ]
 
 
-def assemble(kernel, name, me, far, own, rest, shapes, scratch):
+def assemble(kernel, name, me, far, own, rest, shapes, scratch, mib):
     raws = far + [part for both in zip(own, rest) for part in both]
     whole = pl.BlockSpec(memory_space=pltpu.VMEM)
     return pl.pallas_call(
@@ -220,7 +220,7 @@
         out_specs=[whole] * len(shapes),
         out_shape=[jax.ShapeDtypeStruct(shape, dtype) for shape, dtype in shapes],
         scratch_shapes=scratch,
-        compiler_params=params(24),
+        compiler_params=params(mib),
         cost_estimate=cost(2),
         name=name,
     )(me, *raws)
@@ -360,7 +360,7 @@
 
 
 def forward_kernel(
-    xt_ref, act_ref, dtw_ref, chan_ref, a_ref, gate_in_ref, h_ref, dt_ref, sp_ref, state, push
+    xt_ref, act_ref, dtw_ref, chan_ref, a_ref, gate_in_ref, h_ref, dt_ref, state, push
 ):
     @pl.when(pl.program_id(1) == 0)
     def _():
@@ -370,7 +370,6 @@
     rows_in = columns.T
     rank = rows_in[:, :R].astype(bf16)
     pre = dot(rank, dtw_ref[:, AT_DT : AT_DT + R], 1, 1) + chan_ref[KW + 1 : KW + 2, :]
-    sp_ref[0] = pre
     steps = softplus(pre)
     dt_ref[0] = steps
     push[...] = steps * act_ref[0].astype(f32)
@@ -416,12 +415,10 @@
             pl.BlockSpec((1, ROWS, width), at),
             pl.BlockSpec((1, ROWS * N, width), at),
             pl.BlockSpec((1, ROWS, width), at),
-            pl.BlockSpec((1, ROWS, width), at),
         ],
         out_shape=[
             jax.ShapeDtypeStruct((seqs, length, width), f32),
             jax.ShapeDtypeStruct((seqs, length * N, width), bf16),
-            jax.ShapeDtypeStruct((seqs, length, width), f32),
             jax.ShapeDtypeStruct((seqs, length, width), f32),
         ],
         scratch_shapes=[pltpu.VMEM((N, width), f32), pltpu.VMEM((ROWS, width), f32)],
@@ -554,7 +551,6 @@
     xt_ref,
     act_ref,
     dt_ref,
-    sp_ref,
     ggi_ref,
     chan_ref,
     a_ref,
@@ -580,6 +576,8 @@
     a_now = a_ref[...]
     scaled = a_now * LOG2E
     read = columns[R + N :]
+    rank = rows_in[:, :R].astype(bf16)
+    pre = dot(rank, dtw_ref[:, AT_DT : AT_DT + R], 1, 1) + chan_ref[KW + 1 : KW + 2, :]
     ones = own_columns_of(T).astype(f32).astype(bf16)
     drives = spread(rows_in[:, R : R + N])
     ggi_low = ggi_ref[0].astype(bf16)
@@ -607,7 +605,7 @@
         along = dot(ones, q_buf[states, :], 1, 0)
         act_now = act_ref[0, here, :].astype(f32)
         grad_steps = along + act_now * pulled
-        gsp_ref[0, here, :] = (grad_steps * jax.nn.sigmoid(sp_ref[0, here, :])).astype(bf16)
+        gsp_ref[0, here, :] = (grad_steps * jax.nn.sigmoid(pre[here])).astype(bf16)
         gact_ref[0, here, :] = (
             pulled * dt_ref[0, here, :] + chan_ref[KW + 2 : KW + 3, :] * ggi_ref[0, here, :]
         )
@@ -627,7 +625,7 @@
     galog_ref[...] = acc * a_now
 
 
-def scan_backward(me, xt, act, dt, sp, ggi, chan, a_matrix, states, dtw):
+def scan_backward(me, xt, act, dt, ggi, chan, a_matrix, states, dtw):
     seqs, length, width = act.shape
     blocks = length // ROWS
 
@@ -649,7 +647,6 @@
         in_specs=[
             pl.BlockSpec(memory_space=pltpu.SMEM),
             pl.BlockSpec((WIDE, ROWS), flat),
-            pl.BlockSpec((1, ROWS, width), back),
             pl.BlockSpec((1, ROWS, width), back),
             pl.BlockSpec((1, ROWS, width), back),
             pl.BlockSpec((1, ROWS, width), back),
@@ -683,7 +680,7 @@
         compiler_params=params(60),
         cost_estimate=cost(28),
         name="scan_backward",
-    )(me, xt, act, dt, sp, ggi, chan, a_matrix, states, states, dtw)
+    )(me, xt, act, dt, ggi, chan, a_matrix, states, states, dtw)
 
 
 def leave_kernel(
@@ -1043,10 +1040,7 @@
     second = jnp.concatenate(second)
     tok = parts_dp_far(tokens.reshape(seqs, piece, model))
     first_own = swap_near(first)
-    second_own = swap_near(second)
-    first, tok, first_own, second_own = lax.optimization_barrier(
-        (gather_far(first), tok, first_own, second_own)
-    )
+    first, tok, first_own = lax.optimization_barrier((gather_far(first), tok, first_own))
     cot = parts_dp_far(after(cotangent.reshape(seqs, piece, model), first))
     tok = parts_dp_near(tok)
     first_rest = swap_near(jnp.stack(first[1:]))
@@ -1072,6 +1066,7 @@
                 ((8, width), f32),
             ],
             [pltpu.VMEM((model // own_in, 128), f32)],
+            60,
         )
     else:
         merged = merge_near(first, first_own, first_rest)
@@ -1088,6 +1083,7 @@
     cot = parts_dp_near(cot)
     xt, far = lax.optimization_barrier((xt, far))
     xt = sum_dp_near(*xt)
+    second_own = swap_near(after(far[0], xt))
     second_rest = swap_near(jnp.stack(after(far[1:], xt)))
     xt = sum_dp_far(xt, f32)
     if aligned:
@@ -1100,13 +1096,14 @@
             second_rest,
             [((model, width), bf16), ((width, model), bf16)],
             [],
+            24,
         )
     else:
         merged = merge_near(far, second_own, second_rest)
         w_gate = own_columns(merged[:, :here])
         w_out = merged[:, here:].reshape(fsdps, model // width, own, width)
         w_out = w_out.transpose(0, 2, 1, 3).reshape(width, model)
-    gate_in, states, dt, step_pre = scan_forward(xt, act, small, chan, a_matrix)
+    gate_in, states, dt = scan_forward(xt, act, small, chan, a_matrix)
     outs = middle(me, gate_in, act, normed, w_gate, w_out, cot, near, depth)
     part, gout = outs[:dps], outs[dps : dps + near]
     ggi, ggp, gin_gate, gskip = outs[dps + near :]
@@ -1115,7 +1112,7 @@
     out_mine, out_parts = send_dp_near(part)
 
     gsp, gact, *gxt, galog = scan_backward(
-        me, xt, act, dt, step_pre, ggi, chan, a_matrix, states, small
+        me, xt, act, dt, ggi, chan, a_matrix, states, small
     )
     gxt, out_mine, gout_near = lax.optimization_barrier((gxt, out_mine, gout_near))
     gxt = sum_dp_near(*gxt)

time: 222 us -> 213 us (0.959)
  starting transfers between devices: 63.7 us -> 58.8 us
  waiting for transfers between devices: 44.3 us -> 41.5 us
    all_to_all x1, starting transfers between devices: 7.13 us -> 3.69 us  [shards(): lax.all_to_all(gin_gate.reshape(-1, own_in, width), both, 0, 0, tiled=True)]
    ppermute x36, waiting for transfers between devices: 39.7 us -> 36.9 us  [swap(): return lax.ppermute(x, axis, [(i, i ^ mask) for i in range(peers)])]
    unnamed x74 -> x78, local copies, waits for them, and re-layouts: 6.64 us -> 4.6 us
  transfers between devices with their start and end apart: 40 -> 40, of which waited for: 15 -> 15; matrix products, arithmetic and copies ran while one was open for 6% -> 6% of each run, Pallas kernels for 32% -> 33%
where the time goes in v2:
time: 213 us; the launch traced here: 212 us
  Pallas kernels  87.9 us (41%)
  starting transfers between devices  58.8 us (28%)
  waiting for transfers between devices  41.5 us (19%)
  other arithmetic  14.5 us (7%)
  local copies, waits for them, and re-layouts  8.19 us (4%)
    ppermute x36, starting transfers between devices, swap(): return lax.ppermute(x, axis, [(i, i ^ mask) for i in range(peers)])  41.6 us
    ppermute x36, waiting for transfers between devices, swap(): return lax.ppermute(x, axis, [(i, i ^ mask) for i in range(peers)])  36.9 us
    pallas_call x1, Pallas kernels, scan_backward(): pl.pallas_call(backward_kernel, grid=(seqs, blocks), in_specs=[pl.BlockSp...  24.2 us
    pallas_call x1, Pallas kernels, scan_forward(): pl.pallas_call(forward_kernel, grid=(seqs, blocks), in_specs=[pl.BlockSpe...  14.8 us
    pallas_call x1, Pallas kernels, middle(): pl.pallas_call(middle_kernel, grid_spec=pltpu.PrefetchScalarGridSpec(num_...  14.3 us
    pallas_call x1, Pallas kernels, leave(): pl.pallas_call(leave_kernel, grid=(seqs, blocks), in_specs=[pl.BlockSpec(...  10.3 us
    pallas_call x1, Pallas kernels, enter(): pl.pallas_call(enter_kernel, grid_spec=pltpu.PrefetchScalarGridSpec(num_s...  7.69 us
    pallas_call x1, Pallas kernels, rows_back(): pl.pallas_call(rows_back_kernel, grid_spec=pltpu.PrefetchScalarGridSpec(n...  6.55 us
  transfers between devices with their start and end apart: 40, of which 15 were waited for; matrix products, arithmetic and copies ran while one was open for 6% of the time, Pallas kernels for 33%

profile of v2, /device:TPU:0, one launch (start us, length us, event | category | flops | bytes accessed | tf_op | source)
XLA Modules:
  0.0 212.4 jit_solution(14892872717400465235)
XLA Ops:
  0.7 1.1 convert_element_type.117
  2.1 0.7 convert_bitcast_fusion.1
  3.0 0.8 copy.70
  3.8 4.2 %all-to-all-start = ((bf16[4,72,512]{2,1,0:T(8,128)(2,1)}), bf16[4,72,512]{2,1,0:T(8,128)(2,1)S(1)}, u32[]{:S(2)}, u32[]{:S(2)}) async-start(bf16[4,72,512]{2,1,0:T(8,128)(2,1)} %copy.70), calls=%async_computation | async-start | bytes 589824 | tf_op jit(solution)/shard_map/all_to_all | solution.py:1014
  8.0 2.3 %collective-permute-start.3 = (bf16[2,128,1024]{2,1,0:T(8,128)(2,1)S(1)}, bf16[2,128,1024]{2,1,0:T(8,128)(2,1)}, u32[]{:S(2)}, u32[]{:S(2)}) collective-permute-start(bf16[2,128,1024]{2,1,0:T(8,128)(2,1)S(1)} %bitcast.102), channel_id=1, source_target_pairs={{0,16},{8,24},{16,0},{24,8},{1,17},{9,25},{17,1},{25,9},{2,18},{10... | collective-permute-start | bytes 1572872 | tf_op jit(solution)/shard_map/ppermute | solution.py:45
  10.8 4.3 %all-to-all-done = bf16[4,72,512]{2,1,0:T(8,128)(2,1)S(1)} async-done(((bf16[4,72,512]{2,1,0:T(8,128)(2,1)}), bf16[4,72,512]{2,1,0:T(8,128)(2,1)S(1)}, u32[]{:S(2)}, u32[]{:S(2)}) %all-to-all-start) | async-done | bytes 294944 | tf_op jit(solution)/shard_map/all_to_all | solution.py:1014
  15.1 2.1 collective-permute-start
  17.3 2.6 %collective-permute-start.1 = (bf16[176,512]{1,0:T(8,128)(2,1)S(1)}, bf16[176,512]{1,0:T(8,128)(2,1)S(1)}, u32[]{:S(2)}, u32[]{:S(2)}) collective-permute-start(bf16[176,512]{1,0:T(8,128)(2,1)S(1)} %fusion.6.refs_0_), channel_id=1, source_target_pairs={{0,4},{1,5},{2,6},{3,7},{4,0},{5,1},{6,2},{7,3},{8,12},{9,13},{10,... | collective-permute-start | bytes 540680 | tf_op jit(solution)/shard_map/ppermute | solution.py:45
  19.9 1.7 collective-permute-start.4
  21.6 1.9 collective-permute-done.refs_1_
  23.5 9.7 %collective-permute-done.1.refs_2_ = bf16[176,512]{1,0:T(8,128)(2,1)S(1)} collective-permute-done((bf16[176,512]{1,0:T(8,128)(2,1)S(1)}, bf16[176,512]{1,0:T(8,128)(2,1)S(1)}, u32[]{:S(2)}, u32[]{:S(2)}) %collective-permute-start.1) | collective-permute-done | bytes 180256 | tf_op jit(solution)/shard_map/ppermute | solution.py:45
  33.3 1.6 collective-permute-start.5
  35.7 3.9 %collective-permute-start.10 = (bf16[256,512]{1,0:T(8,128)(2,1)S(1)}, bf16[256,512]{1,0:T(8,128)(2,1)S(1)}, u32[]{:S(2)}, u32[]{:S(2)}) collective-permute-start(bf16[256,512]{1,0:T(8,128)(2,1)S(1)} %pad_maximum_fusion.3.refs_0_), channel_id=1, source_target_pairs={{0,4},{1,5},{2,6},{3,7},{4,0},{5,1},{6,2},{7,3},{8,12},{9,13},{10,... | collective-permute-start | bytes 786440 | tf_op jit(solution)/shard_map/ppermute | solution.py:45
  39.6 5.0 %collective-permute-done.6.refs_2_ = bf16[2,128,1024]{2,1,0:T(8,128)(2,1)} collective-permute-done((bf16[2,128,1024]{2,1,0:T(8,128)(2,1)S(1)}, bf16[2,128,1024]{2,1,0:T(8,128)(2,1)}, u32[]{:S(2)}, u32[]{:S(2)}) %collective-permute-start.6) | collective-permute-done | bytes 524320 | tf_op jit(solution)/shard_map/ppermute | solution.py:45
  44.7 1.6 collective-permute-start.11
  46.2 0.8 copy-done.27
  47.0 4.9 %collective-permute-start.9 = (bf16[256,512]{1,0:T(8,128)(2,1)S(1)}, bf16[256,512]{1,0:T(8,128)(2,1)S(1)}, u32[]{:S(2)}, u32[]{:S(2)}) collective-permute-start(bf16[256,512]{1,0:T(8,128)(2,1)S(1)} %pad_maximum_fusion.3.refs_0_), channel_id=1, source_target_pairs={{0,2},{1,3},{2,0},{3,1},{4,6},{5,7},{6,4},{7,5},{8,10},{9,11},{10,... | collective-permute-start | bytes 786440 | tf_op jit(solution)/shard_map/ppermute | solution.py:45
  52.6 2.6 %assemble_first.1 = (bf16[1024,512]{1,0:T(8,128)(2,1)}, bf16[512,256]{1,0:T(8,128)(2,1)}, f32[1,1024]{1,0:T(1,128)}, f32[16,512]{1,0:T(8,128)}, f32[8,512]{1,0:T(8,128)}) custom-call(s32[2]{0:T(128)} %pad_add_fusion.me_ref, bf16[176,512]{1,0:T(8,128)(2,1)} %copy-done.23, bf16[176,512]{1,0:T(8,128)(2,1)} %copy-done.24, bf16[176,512]{1,0:T(8,128)(2,1)} %copy-done.25, ...), custom_call_target="tpu_custom_call" | custom-call | flops 160000000 | bytes 600000 | tf_op jit(solution)/shard_map/assemble_first/pallas_call | solution.py:217
  55.2 7.7 %enter.1 = (bf16[2,512,1024]{2,1,0:T(8,128)(2,1)}, bf16[2,512,512]{2,1,0:T(8,128)(2,1)}, f32[2,512,512]{2,1,0:T(8,128)}, bf16[2,512,512]{2,1,0:T(8,128)(2,1)}, f32[48,1024]{1,0:T(8,128)}, /*index=5*/f32[48,1024]{1,0:T(8,128)}) custom-call(s32[2]{0:T(128)} %pad_add_fusion.me_ref, f32[1,1024]{1,0:T(1,128)} %get-tuple-element.144.gain_ref, ...), custom_call_target="tpu_custom_call" | custom-call | flops 560000000 | bytes 2100000 | tf_op jit(solution)/shard_map/enter/pallas_call | solution.py:308
  63.0 1.6 collective-permute-done.12
  64.6 0.9 add.55
  65.6 1.0 pad_maximum_fusion
  67.1 1.4 collective-permute-start.13
  69.0 4.8 %collective-permute-done.13 = f32[48,1024]{1,0:T(8,128)S(1)} collective-permute-done((f32[48,1024]{1,0:T(8,128)S(1)}, f32[48,1024]{1,0:T(8,128)S(1)}, u32[]{:S(2)}, u32[]{:S(2)}) %collective-permute-start.13) | collective-permute-done | bytes 196640 | tf_op jit(solution)/shard_map/ppermute | solution.py:45
  73.8 1.6 collective-permute-start.15
  75.4 0.7 maximum_select_fusion
  76.1 14.8 %scan_forward.1 = (f32[2,512,512]{2,1,0:T(8,128)}, bf16[2,8192,512]{2,1,0:T(8,128)(2,1)}, f32[2,512,512]{2,1,0:T(8,128)}) custom-call(bf16[96,1024]{1,0:T(8,128)(2,1)} %bitcast.110, bf16[2,512,512]{2,1,0:T(8,128)(2,1)} %get-tuple-element.154.act_ref, bf16[512,256]{1,0:T(8,128)(2,1)} %get-tuple-element.147.wx_ref.dtw_ref, ...), custom_call_target="tpu_custom_call" | custom-call | flops 1440000000 | bytes 5400000 | tf_op jit(solution)/shard_map/scan_forward/pallas_call | solution.py:404
  91.0 1.0 collective-permute-done.15.refs_4_
  92.0 0.7 assemble_second.1
  92.7 1.0 copy-done.1
  93.6 1.0 copy-done.2
  94.6 14.3 %middle.1 = (f32[2,128,1024]{2,1,0:T(8,128)}, bf16[2,128,1024]{2,1,0:T(8,128)(2,1)}, f32[2,128,1024]{2,1,0:T(8,128)}, bf16[2,128,1024]{2,1,0:T(8,128)(2,1)}, bf1...) custom-call(s32[2]{0:T(128)} %pad_add_fusion.me_ref, ...), custom_call_target="tpu_custom_call" | custom-call | flops 720000000 | bytes 2700000 | tf_op jit(solution)/shard_map/middle/pallas_call | solution.py:507
  109.5 3.7 %all-to-all-start.1 = ((bf16[32,32,512]{2,1,0:T(8,128)(2,1)}), bf16[32,32,512]{2,1,0:T(8,128)(2,1)S(1)}, u32[]{:S(2)}, u32[]{:S(2)}) async-start(bf16[32,32,512]{2,1,0:T(8,128)(2,1)} %bitcast.116), calls=%async_computation.1 | async-start | bytes 2097152 | tf_op jit(solution)/shard_map/all_to_all | solution.py:1110
  113.3 24.2 %scan_backward.1 = (bf16[2,512,512]{2,1,0:T(8,128)(2,1)}, f32[2,512,512]{2,1,0:T(8,128)}, f32[48,1024]{1,0:T(8,128)}, f32[48,1024]{1,0:T(8,128)}, f32[16,512]{1,0:T(8,128)}) custom-call(s32[2]{0:T(128)} %pad_add_fusion.me_ref, bf16[96,1024]{1,0:T(8,128)(2,1)} %bitcast.111, bf16[2,512,512]{2,1,0:T(8,128)(2,1)} %get-tuple-element.154.act_ref, ...), custom_call_target="tpu_custom_call" | custom-call | flops 2240000000 | bytes 8400000 | tf_op jit(solution)/shard_map/scan_backward/pallas_call | solution.py:644
  137.8 0.8 slice_bitcast_fusion.1
  138.5 0.7 slice_bitcast_fusion
  139.7 1.1 collective-permute-done.21
  140.8 1.7 collective-permute-start.22
  142.5 1.2 add_convert_fusion.1
  144.2 1.8 collective-permute-done.22
  146.1 1.7 collective-permute-start.24
  147.7 2.4 %collective-permute-start.25 = (bf16[64,1024]{1,0:T(8,128)(2,1)}, bf16[64,1024]{1,0:T(8,128)(2,1)S(1)}, u32[]{:S(2)}, u32[]{:S(2)}) collective-permute-start(bf16[64,1024]{1,0:T(8,128)(2,1)} %get-tuple-element.196), channel_id=1, source_target_pairs={{0,4},{1,5},{2,6},{3,7},{4,0},{5,1},{6,2},{7,3},{8,12},{9,13},{10,... | collective-permute-start | bytes 393224 | tf_op jit(solution)/shard_map/ppermute | solution.py:45
  150.5 0.7 maximum_select_fusion.1
  151.2 10.3 %leave.1 = (bf16[2,512,512]{2,1,0:T(8,128)(2,1)}, bf16[1024,512]{1,0:T(8,128)(2,1)}, f32[512,192]{1,0:T(8,128)}) custom-call(f32[2,512,512]{2,1,0:T(8,128)} %get-tuple-element.173.gact_ref, bf16[96,1024]{1,0:T(8,128)(2,1)} %bitcast.119, bf16[96,1024]{1,0:T(8,128)(2,1)} %bitcast.112, bf16[2,512,512]{2,1,0:T(8,128)(2,1)} %get-tuple-element.184.gsp_ref, ...), custom_call_target="tpu_custom_call" | custom-call | flops 640000000 | bytes 2400000 | tf_op jit(solution)/shard_map/leave/pallas_call | solution.py:766
  161.6 0.8 copy-done.30
  162.4 6.2 %all-to-all-start.2 = ((bf16[32,32,512]{2,1,0:T(8,128)(2,1)}), bf16[32,32,512]{2,1,0:T(8,128)(2,1)S(1)}, u32[]{:S(2)}, u32[]{:S(2)}) async-start(bf16[32,32,512]{2,1,0:T(8,128)(2,1)} %bitcast.117), calls=%async_computation.2 | async-start | bytes 2097152 | tf_op jit(solution)/shard_map/all_to_all | solution.py:1127
  168.8 0.7 fusion.7
  169.4 1.8 collective-permute-start.30
  171.2 6.6 %rows_back.1 = (f32[2,128,1024]{2,1,0:T(8,128)}, bf16[2,128,1024]{2,1,0:T(8,128)(2,1)}, f32[2,128,1024]{2,1,0:T(8,128)}, bf16[2,128,1024]{2,1,0:T(8,128)(2,1)}) custom-call(s32[2]{0:T(128)} %pad_add_fusion.me_ref, bf16[2,512,512]{2,1,0:T(8,128)(2,1)} %get-tuple-element.206.gci_ref, bf16[2,512,512]{2,1,0:T(8,128)(2,1)} %get-tuple-element.207.ggp_ref, ...), custom_call_target="tpu_custom_call" | custom-call | flops 400000000 | bytes 1500000 | tf_op jit(solution)/shard_map/rows_back/pallas_call | solution.py:823
  178.3 6.5 %collective-permute-done.30 = bf16[4,64,192]{2,1,0:T(8,128)(2,1)} collective-permute-done((bf16[4,64,192]{2,1,0:T(8,128)(2,1)}, bf16[4,64,192]{2,1,0:T(8,128)(2,1)}, u32[]{:S(2)}, u32[]{:S(2)}) %collective-permute-start.30) | collective-permute-done | bytes 98336 | tf_op jit(solution)/shard_map/ppermute | solution.py:45
  184.8 1.0 fusion.9
  185.9 2.2 %add_convert_fusion = bf16[2,128,1024]{2,1,0:T(8,128)(2,1)} fusion(f32[2,128,1024]{2,1,0:T(8,128)} %get-tuple-element.211, bf16[2,128,1024]{2,1,0:T(8,128)(2,1)S(1)} %collective-permute-done.31), kind=kLoop, calls=%fused_computation.2 | loop fusion | flops 786432 | bytes 2097152 | tf_op jit(solution)/shard_map/convert_element_type | solution.py:97
  188.0 2.0 collective-permute-start.34
  190.0 2.4 %collective-permute-start.35 = (bf16[64,192]{1,0:T(8,128)(2,1)S(1)}, bf16[64,192]{1,0:T(8,128)(2,1)S(1)}, u32[]{:S(2)}, u32[]{:S(2)}) collective-permute-start(bf16[64,192]{1,0:T(8,128)(2,1)S(1)} %get-tuple-element.223), channel_id=1, source_target_pairs={{0,6},{1,7},{2,4},{3,5},{4,2},{5,3},{6,0},{7,1},{8,14},{9,15},{10,... | collective-permute-start | bytes 73736 | tf_op jit(solution)/shard_map/ppermute | solution.py:45
  192.4 1.0 convert_add_fusion.1.out_ref.refs_15_
  193.4 1.5 collective-permute-start.32
  194.9 2.4 %collective-permute-done.34 = bf16[64,192]{1,0:T(8,128)(2,1)S(1)} collective-permute-done((bf16[64,192]{1,0:T(8,128)(2,1)S(1)}, bf16[64,192]{1,0:T(8,128)(2,1)S(1)}, u32[]{:S(2)}, u32[]{:S(2)}) %collective-permute-start.34) | collective-permute-done | bytes 24608 | tf_op jit(solution)/shard_map/ppermute | solution.py:45
  197.6 1.2 collect.1
  198.8 0.8 copy-done.6
  199.6 3.1 %all-to-all-start.3 = ((f32[32,1,128]{2,1,0:T(1,128)}), f32[32,1,128]{2,1,0:T(1,128)S(1)}, u32[]{:S(2)}, u32[]{:S(2)}) async-start(f32[32,1,128]{2,1,0:T(1,128)} %get-tuple-element.224), calls=%async_computation.3 | async-start | bytes 32768 | tf_op jit(solution)/shard_map/all_to_all | solution.py:1152
  202.7 2.8 %fusion.1 = bf16[2,1,128,1024]{3,2,1,0:T(8,128)(2,1)} fusion(bf16[2,128,1024]{2,1,0:T(8,128)(2,1)} %copy-done.30, f32[2,128,1024]{2,1,0:T(8,128)} %get-tuple-element.203, bf16[2,128,1024]{2,1,0:T(8,128)(2,1)} %collective-permute-done.19, bf16[2,1,128,1024]{3,2,1,0:T(8,128)(2,1)} %param.16), kind=kLoop, calls=%fused_computation.12 | loop fusion | flops 1835008 | bytes 3145728
  205.5 1.0 collective-permute-done.32.refs_2_
  206.5 3.1 %finish.1 = f32[2,128,1024]{2,1,0:T(8,128)} custom-call(bf16[2,128,1024]{2,1,0:T(8,128)(2,1)} %bitcast.101, bf16[2,128,1024]{2,1,0:T(8,128)(2,1)} %bitcast.105, f32[1,1024]{1,0:T(1,128)} %get-tuple-element.144.gain_ref, f32[2,128,1024]{2,1,0:T(8,128)} %get-tuple-element.225.refs_0_, bf16[2,128,1024]{2,1,0:T(8,128)(2,1)} %collective-permute-done.29.refs_1_, ...), custom_call_target="tpu_custom_call" | custom-call | flops 240000000 | bytes 900000 | tf_op jit(solution)/shard_map/finish/pallas_call | solution.py:859
  209.8 2.5 %adam.1 = (f32[2,32,4096]{2,1,0:T(8,128)}, f32[32,4096]{1,0:T(8,128)}, f32[2,64,1024]{2,1,0:T(8,128)}, f32[64,1024]{1,0:T(8,128)}, f32[2,64,96]{2,1,0:T(8,128)},...) custom-call(f32[32,1,128]{2,1,0:T(1,128)S(1)} %all-to-all-done.3.squ, ...), custom_call_target="tpu_custom_call" | custom-call | flops 320000000 | bytes 1200000 | tf_op jit(solution)/shard_map/adam/pallas_call | solution.py:967
  (152 shorter events, 7.3 us)
Async XLA Ops:
  0.7 7.4 %copy-start.19 = (bf16[2,1,128,1024]{3,2,1,0:T(8,128)(2,1)S(1)}, bf16[2,1,128,1024]{3,2,1,0:T(8,128)(2,1)}, u32[]{:S(2)}) copy-start(bf16[2,1,128,1024]{3,2,1,0:T(8,128)(2,1)} %param.16) | copy-start | bytes 1572868
  0.7 9.6 %copy-start.12 = (f32[16,64]{1,0:T(8,128)S(1)}, f32[16,64]{1,0:T(8,128)}, u32[]{:S(2)}) copy-start(f32[16,64]{1,0:T(8,128)} %refs_5_.1) | copy-start | bytes 12292
  0.7 9.7 %copy-start.15 = (f32[7,64]{1,0:T(8,128)S(1)}, f32[7,64]{1,0:T(8,128)}, u32[]{:S(2)}) copy-start(f32[7,64]{1,0:T(8,128)} %refs_4_.1) | copy-start | bytes 5380
  0.7 9.8 %copy-start.9 = (f32[64,64]{1,0:T(8,128)S(1)}, f32[64,64]{1,0:T(8,128)}, u32[]{:S(2)}) copy-start(f32[64,64]{1,0:T(8,128)} %refs_3_.1) | copy-start | bytes 49156
  0.7 9.9 %copy-start.8 = (f32[64,96]{1,0:T(8,128)S(1)}, f32[64,96]{1,0:T(8,128)}, u32[]{:S(2)}) copy-start(f32[64,96]{1,0:T(8,128)} %refs_2_.1) | copy-start | bytes 73732
  2.8 32.1 %copy-start.20 = (bf16[2,1,128,1024]{3,2,1,0:T(8,128)(2,1)S(1)}, bf16[2,1,128,1024]{3,2,1,0:T(8,128)(2,1)}, u32[]{:S(2)}) copy-start(bf16[2,1,128,1024]{3,2,1,0:T(8,128)(2,1)} %param.17) | copy-start | bytes 1572868
  2.8 32.9 %copy-start.3 = (f32[64,1024]{1,0:T(8,128)S(1)}, f32[64,1024]{1,0:T(8,128)}, u32[]{:S(2)}) copy-start(f32[64,1024]{1,0:T(8,128)} %refs_1_.1) | copy-start | bytes 786436
  3.8 11.3 %all-to-all-start = ((bf16[4,72,512]{2,1,0:T(8,128)(2,1)}), bf16[4,72,512]{2,1,0:T(8,128)(2,1)S(1)}, u32[]{:S(2)}, u32[]{:S(2)}) async-start(bf16[4,72,512]{2,1,0:T(8,128)(2,1)} %copy.70), calls=%async_computation | async-start | bytes 589824 | tf_op jit(solution)/shard_map/all_to_all | solution.py:1014
  8.0 25.2 %collective-permute-start.3 = (bf16[2,128,1024]{2,1,0:T(8,128)(2,1)S(1)}, bf16[2,128,1024]{2,1,0:T(8,128)(2,1)}, u32[]{:S(2)}, u32[]{:S(2)}) collective-permute-start(bf16[2,128,1024]{2,1,0:T(8,128)(2,1)S(1)} %bitcast.102), channel_id=1, source_target_pairs={{0,16},{8,24},{16,0},{24,8},{1,17},{9,25},{17,1},{25,9},{2,18},{10... | collective-permute-start | bytes 1572872 | tf_op jit(solution)/shard_map/ppermute | solution.py:45
  15.1 37.4 %copy-start.23 = (bf16[176,512]{1,0:T(8,128)(2,1)}, bf16[176,512]{1,0:T(8,128)(2,1)S(1)}, u32[]{:S(2)}) copy-start(bf16[176,512]{1,0:T(8,128)(2,1)S(1)} %fusion.6.refs_0_) | copy-start | bytes 540676
  15.1 8.3 %collective-permute-start = (bf16[176,512]{1,0:T(8,128)(2,1)S(1)}, bf16[176,512]{1,0:T(8,128)(2,1)S(1)}, u32[]{:S(2)}, u32[]{:S(2)}) collective-permute-start(bf16[176,512]{1,0:T(8,128)(2,1)S(1)} %fusion.6.refs_0_), channel_id=1, source_target_pairs={{0,2},{1,3},{2,0},{3,1},{4,6},{5,7},{6,4},{7,5},{8,10},{9,11},{10,... | collective-permute-start | bytes 540680 | tf_op jit(solution)/shard_map/ppermute | solution.py:45
  17.3 15.9 %collective-permute-start.1 = (bf16[176,512]{1,0:T(8,128)(2,1)S(1)}, bf16[176,512]{1,0:T(8,128)(2,1)S(1)}, u32[]{:S(2)}, u32[]{:S(2)}) collective-permute-start(bf16[176,512]{1,0:T(8,128)(2,1)S(1)} %fusion.6.refs_0_), channel_id=1, source_target_pairs={{0,4},{1,5},{2,6},{3,7},{4,0},{5,1},{6,2},{7,3},{8,12},{9,13},{10,... | collective-permute-start | bytes 540680 | tf_op jit(solution)/shard_map/ppermute | solution.py:45
  19.9 13.4 %collective-permute-start.2 = (bf16[176,512]{1,0:T(8,128)(2,1)S(1)}, bf16[176,512]{1,0:T(8,128)(2,1)S(1)}, u32[]{:S(2)}, u32[]{:S(2)}) collective-permute-start(bf16[176,512]{1,0:T(8,128)(2,1)S(1)} %fusion.6.refs_0_), channel_id=1, source_target_pairs={{0,6},{1,7},{2,4},{3,5},{4,2},{5,3},{6,0},{7,1},{8,14},{9,15},{10,... | collective-permute-start | bytes 540680 | tf_op jit(solution)/shard_map/ppermute | solution.py:45
  19.9 13.4 %collective-permute-start.4 = (bf16[176,512]{1,0:T(8,128)(2,1)S(1)}, bf16[176,512]{1,0:T(8,128)(2,1)S(1)}, u32[]{:S(2)}, u32[]{:S(2)}) collective-permute-start(bf16[176,512]{1,0:T(8,128)(2,1)S(1)} %fusion.6.refs_0_), channel_id=1, source_target_pairs={{0,1},{1,0},{2,3},{3,2},{4,5},{5,4},{6,7},{7,6},{8,9},{9,8},{10,11... | collective-permute-start | bytes 540680 | tf_op jit(solution)/shard_map/ppermute | solution.py:45
  23.5 29.1 %copy-start.24 = (bf16[176,512]{1,0:T(8,128)(2,1)}, bf16[176,512]{1,0:T(8,128)(2,1)S(1)}, u32[]{:S(2)}) copy-start(bf16[176,512]{1,0:T(8,128)(2,1)S(1)} %collective-permute-done.refs_1_) | copy-start | bytes 540676
  33.2 19.3 %copy-start.25 = (bf16[176,512]{1,0:T(8,128)(2,1)}, bf16[176,512]{1,0:T(8,128)(2,1)S(1)}, u32[]{:S(2)}) copy-start(bf16[176,512]{1,0:T(8,128)(2,1)S(1)} %collective-permute-done.1.refs_2_) | copy-start | bytes 540676
  33.2 19.3 %copy-start.26 = (bf16[176,512]{1,0:T(8,128)(2,1)}, bf16[176,512]{1,0:T(8,128)(2,1)S(1)}, u32[]{:S(2)}) copy-start(bf16[176,512]{1,0:T(8,128)(2,1)S(1)} %collective-permute-done.2.refs_3_) | copy-start | bytes 540676
  33.2 6.4 %copy-start.32 = (bf16[176,512]{1,0:T(8,128)(2,1)}, bf16[176,512]{1,0:T(8,128)(2,1)S(1)}, u32[]{:S(2)}) copy-start(bf16[176,512]{1,0:T(8,128)(2,1)S(1)} %collective-permute-done.4.refs_4_) | copy-start | bytes 540676
  33.3 12.9 %collective-permute-start.5 = (bf16[3,176,512]{2,1,0:T(8,128)(2,1)S(1)}, bf16[3,176,512]{2,1,0:T(8,128)(2,1)S(1)}, u32[]{:S(2)}, u32[]{:S(2)}) collective-permute-start(bf16[3,176,512]{2,1,0:T(8,128)(2,1)S(1)} %pad_maximum_fusion.1), channel_id=1, source_target_pairs={{0,1},{1,0},{2,3},{3,2},{4,5},{5,4},{6,7},{7,6},{8,9},{9,8},{10,11... | collective-permute-start | bytes 1622024 | tf_op jit(solution)/shard_map/ppermute | solution.py:45
  34.9 9.8 %collective-permute-start.6 = (bf16[2,128,1024]{2,1,0:T(8,128)(2,1)S(1)}, bf16[2,128,1024]{2,1,0:T(8,128)(2,1)}, u32[]{:S(2)}, u32[]{:S(2)}) collective-permute-start(bf16[2,128,1024]{2,1,0:T(8,128)(2,1)S(1)} %bitcast.106), channel_id=1, source_target_pairs={{0,16},{8,24},{16,0},{24,8},{1,17},{9,25},{17,1},{25,9},{2,18},{10... | collective-permute-start | bytes 1572872 | tf_op jit(solution)/shard_map/ppermute | solution.py:45
  35.1 20.0 %collective-permute-start.7 = (bf16[2,128,1024]{2,1,0:T(8,128)(2,1)S(1)}, bf16[2,128,1024]{2,1,0:T(8,128)(2,1)}, u32[]{:S(2)}, u32[]{:S(2)}) collective-permute-start(bf16[2,128,1024]{2,1,0:T(8,128)(2,1)S(1)} %bitcast.103), channel_id=1, source_target_pairs={{0,8},{8,0},{16,24},{24,16},{1,9},{9,1},{17,25},{25,17},{2,10},{10... | collective-permute-start | bytes 1572872 | tf_op jit(solution)/shard_map/ppermute | solution.py:45
  35.1 20.0 %collective-permute-start.8 = (bf16[2,128,1024]{2,1,0:T(8,128)(2,1)}, bf16[2,128,1024]{2,1,0:T(8,128)(2,1)}, u32[]{:S(2)}, u32[]{:S(2)}) collective-permute-start(bf16[2,128,1024]{2,1,0:T(8,128)(2,1)} %collective-permute-done.3.refs_2_), channel_id=1, source_target_pairs={{0,8},{8,0},{16,24},{24,16},{1,9},{9,1},{17,25},{25,17},{2,10},{10... | collective-permute-start | bytes 1572872 | tf_op jit(solution)/shard_map/ppermute | solution.py:45
  35.7 27.2 %collective-permute-start.10 = (bf16[256,512]{1,0:T(8,128)(2,1)S(1)}, bf16[256,512]{1,0:T(8,128)(2,1)S(1)}, u32[]{:S(2)}, u32[]{:S(2)}) collective-permute-start(bf16[256,512]{1,0:T(8,128)(2,1)S(1)} %pad_maximum_fusion.3.refs_0_), channel_id=1, source_target_pairs={{0,4},{1,5},{2,6},{3,7},{4,0},{5,1},{6,2},{7,3},{8,12},{9,13},{10,... | collective-permute-start | bytes 786440 | tf_op jit(solution)/shard_map/ppermute | solution.py:45
  44.7 18.2 %collective-permute-start.11 = (bf16[256,512]{1,0:T(8,128)(2,1)S(1)}, bf16[256,512]{1,0:T(8,128)(2,1)S(1)}, u32[]{:S(2)}, u32[]{:S(2)}) collective-permute-start(bf16[256,512]{1,0:T(8,128)(2,1)S(1)} %pad_maximum_fusion.3.refs_0_), channel_id=1, source_target_pairs={{0,6},{1,7},{2,4},{3,5},{4,2},{5,3},{6,0},{7,1},{8,14},{9,15},{10,... | collective-permute-start | bytes 786440 | tf_op jit(solution)/shard_map/ppermute | solution.py:45
  47.0 15.9 %collective-permute-start.9 = (bf16[256,512]{1,0:T(8,128)(2,1)S(1)}, bf16[256,512]{1,0:T(8,128)(2,1)S(1)}, u32[]{:S(2)}, u32[]{:S(2)}) collective-permute-start(bf16[256,512]{1,0:T(8,128)(2,1)S(1)} %pad_maximum_fusion.3.refs_0_), channel_id=1, source_target_pairs={{0,2},{1,3},{2,0},{3,1},{4,6},{5,7},{6,4},{7,5},{8,10},{9,11},{10,... | collective-permute-start | bytes 786440 | tf_op jit(solution)/shard_map/ppermute | solution.py:45
  63.0 1.7 collective-permute-start.12
  66.6 25.4 %collective-permute-start.16 = (bf16[3,256,512]{2,1,0:T(8,128)(2,1)}, bf16[3,256,512]{2,1,0:T(8,128)(2,1)S(1)}, u32[]{:S(2)}, u32[]{:S(2)}) collective-permute-start(bf16[3,256,512]{2,1,0:T(8,128)(2,1)} %pad_maximum_fusion), channel_id=1, source_target_pairs={{0,1},{1,0},{2,3},{3,2},{4,5},{5,4},{6,7},{7,6},{8,9},{9,8},{10,11... | collective-permute-start | bytes 2359304 | tf_op jit(solution)/shard_map/ppermute | solution.py:45
  67.1 6.7 %collective-permute-start.13 = (f32[48,1024]{1,0:T(8,128)S(1)}, f32[48,1024]{1,0:T(8,128)S(1)}, u32[]{:S(2)}, u32[]{:S(2)}) collective-permute-start(f32[48,1024]{1,0:T(8,128)S(1)} %add.55), channel_id=1, source_target_pairs={{0,16},{8,24},{16,0},{24,8},{1,17},{9,25},{17,1},{25,9},{2,18},{10... | collective-permute-start | bytes 589832 | tf_op jit(solution)/shard_map/ppermute | solution.py:45
  68.5 26.1 %collective-permute-start.17 = (bf16[2,128,1024]{2,1,0:T(8,128)(2,1)S(1)}, bf16[2,128,1024]{2,1,0:T(8,128)(2,1)}, u32[]{:S(2)}, u32[]{:S(2)}) collective-permute-start(bf16[2,128,1024]{2,1,0:T(8,128)(2,1)S(1)} %bitcast.107), channel_id=1, source_target_pairs={{0,8},{8,0},{16,24},{24,16},{1,9},{9,1},{17,25},{25,17},{2,10},{10... | collective-permute-start | bytes 1572872 | tf_op jit(solution)/shard_map/ppermute | solution.py:45
  68.5 26.1 %collective-permute-start.18 = (bf16[2,128,1024]{2,1,0:T(8,128)(2,1)}, bf16[2,128,1024]{2,1,0:T(8,128)(2,1)}, u32[]{:S(2)}, u32[]{:S(2)}) collective-permute-start(bf16[2,128,1024]{2,1,0:T(8,128)(2,1)} %collective-permute-done.6.refs_2_), channel_id=1, source_target_pairs={{0,8},{8,0},{16,24},{24,16},{1,9},{9,1},{17,25},{25,17},{2,10},{10... | collective-permute-start | bytes 1572872 | tf_op jit(solution)/shard_map/ppermute | solution.py:45
  73.8 1.7 collective-permute-start.14
  73.8 18.1 %collective-permute-start.15 = (bf16[256,512]{1,0:T(8,128)(2,1)S(1)}, bf16[256,512]{1,0:T(8,128)(2,1)S(1)}, u32[]{:S(2)}, u32[]{:S(2)}) collective-permute-start(bf16[256,512]{1,0:T(8,128)(2,1)S(1)} %pad_maximum_fusion.3.refs_0_), channel_id=1, source_target_pairs={{0,1},{1,0},{2,3},{3,2},{4,5},{5,4},{6,7},{7,6},{8,9},{9,8},{10,11... | collective-permute-start | bytes 786440 | tf_op jit(solution)/shard_map/ppermute | solution.py:45
  76.1 15.9 %copy-start.13 = (s32[2]{0:T(128)S(1)}, s32[2]{0:T(128)}, u32[]{:S(2)}) copy-start(s32[2]{0:T(128)} %pad_add_fusion.me_ref) | copy-start | bytes 28
  108.9 28.7 %collective-permute-start.20 = (bf16[4,64,1024]{2,1,0:T(8,128)(2,1)}, bf16[4,64,1024]{2,1,0:T(8,128)(2,1)S(1)}, u32[]{:S(2)}, u32[]{:S(2)}) collective-permute-start(bf16[4,64,1024]{2,1,0:T(8,128)(2,1)} %get-tuple-element.179), channel_id=1, source_target_pairs={{0,1},{1,0},{2,3},{3,2},{4,5},{5,4},{6,7},{7,6},{8,9},{9,8},{10,11... | collective-permute-start | bytes 1572872 | tf_op jit(solution)/shard_map/ppermute | solution.py:45
  109.5 29.8 %collective-permute-start.19 = (bf16[2,128,1024]{2,1,0:T(8,128)(2,1)}, bf16[2,128,1024]{2,1,0:T(8,128)(2,1)}, u32[]{:S(2)}, u32[]{:S(2)}) collective-permute-start(bf16[2,128,1024]{2,1,0:T(8,128)(2,1)} %get-tuple-element.177), channel_id=1, source_target_pairs={{0,8},{8,0},{16,24},{24,16},{1,9},{9,1},{17,25},{25,17},{2,10},{10... | collective-permute-start | bytes 1572872 | tf_op jit(solution)/shard_map/ppermute | solution.py:45
  109.5 41.7 %all-to-all-start.1 = ((bf16[32,32,512]{2,1,0:T(8,128)(2,1)}), bf16[32,32,512]{2,1,0:T(8,128)(2,1)S(1)}, u32[]{:S(2)}, u32[]{:S(2)}) async-start(bf16[32,32,512]{2,1,0:T(8,128)(2,1)} %bitcast.116), calls=%async_computation.1 | async-start | bytes 2097152 | tf_op jit(solution)/shard_map/all_to_all | solution.py:1110
  113.2 29.3 %collective-permute-start.27 = (bf16[2,128,1024]{2,1,0:T(8,128)(2,1)}, bf16[2,128,1024]{2,1,0:T(8,128)(2,1)}, u32[]{:S(2)}, u32[]{:S(2)}) collective-permute-start(bf16[2,128,1024]{2,1,0:T(8,128)(2,1)} %get-tuple-element.201), channel_id=1, source_target_pairs={{0,8},{8,0},{16,24},{24,16},{1,9},{9,1},{17,25},{25,17},{2,10},{10... | collective-permute-start | bytes 1572872 | tf_op jit(solution)/shard_map/ppermute | solution.py:45
  113.3 24.2 %copy-start.28 = (bf16[4,64,1024]{2,1,0:T(8,128)(2,1)S(1)}, bf16[4,64,1024]{2,1,0:T(8,128)(2,1)}, u32[]{:S(2)}) copy-start(bf16[4,64,1024]{2,1,0:T(8,128)(2,1)} %get-tuple-element.178) | copy-start | bytes 1572868
  137.6 4.9 %copy-start.22 = (f32[2,128,1024]{2,1,0:T(8,128)S(1)}, f32[2,128,1024]{2,1,0:T(8,128)}, u32[]{:S(2)}) copy-start(f32[2,128,1024]{2,1,0:T(8,128)} %get-tuple-element.200) | copy-start | bytes 3145732
  139.3 1.5 collective-permute-start.21
  140.8 5.1 %collective-permute-start.22 = (bf16[48,1024]{1,0:T(8,128)(2,1)S(1)}, bf16[48,1024]{1,0:T(8,128)(2,1)S(1)}, u32[]{:S(2)}, u32[]{:S(2)}) collective-permute-start(bf16[48,1024]{1,0:T(8,128)(2,1)S(1)} %get-tuple-element.319), channel_id=1, source_target_pairs={{0,16},{8,24},{16,0},{24,8},{1,17},{9,25},{17,1},{25,9},{2,18},{10... | collective-permute-start | bytes 294920 | tf_op jit(solution)/shard_map/ppermute | solution.py:45
  143.7 17.9 %collective-permute-start.28 = (bf16[2,128,1024]{2,1,0:T(8,128)(2,1)S(1)}, bf16[2,128,1024]{2,1,0:T(8,128)(2,1)S(1)}, u32[]{:S(2)}, u32[]{:S(2)}) collective-permute-start(bf16[2,128,1024]{2,1,0:T(8,128)(2,1)S(1)} %add_convert_fusion.1), channel_id=1, source_target_pairs={{0,16},{8,24},{16,0},{24,8},{1,17},{9,25},{17,1},{25,9},{2,18},{10... | collective-permute-start | bytes 1572872 | tf_op jit(solution)/shard_map/ppermute | solution.py:45
  146.0 4.5 %collective-permute-start.23 = (bf16[48,1024]{1,0:T(8,128)(2,1)S(1)}, bf16[48,1024]{1,0:T(8,128)(2,1)S(1)}, u32[]{:S(2)}, u32[]{:S(2)}) collective-permute-start(bf16[48,1024]{1,0:T(8,128)(2,1)S(1)} %add_convert_fusion.2), channel_id=1, source_target_pairs={{0,8},{8,0},{16,24},{24,16},{1,9},{9,1},{17,25},{25,17},{2,10},{10... | collective-permute-start | bytes 294920 | tf_op jit(solution)/shard_map/ppermute | solution.py:45
  146.1 15.5 %collective-permute-start.24 = (bf16[64,1024]{1,0:T(8,128)(2,1)}, bf16[64,1024]{1,0:T(8,128)(2,1)S(1)}, u32[]{:S(2)}, u32[]{:S(2)}) collective-permute-start(bf16[64,1024]{1,0:T(8,128)(2,1)} %get-tuple-element.195), channel_id=1, source_target_pairs={{0,2},{1,3},{2,0},{3,1},{4,6},{5,7},{6,4},{7,5},{8,10},{9,11},{10,... | collective-permute-start | bytes 393224 | tf_op jit(solution)/shard_map/ppermute | solution.py:45
  147.7 13.8 %collective-permute-start.25 = (bf16[64,1024]{1,0:T(8,128)(2,1)}, bf16[64,1024]{1,0:T(8,128)(2,1)S(1)}, u32[]{:S(2)}, u32[]{:S(2)}) collective-permute-start(bf16[64,1024]{1,0:T(8,128)(2,1)} %get-tuple-element.196), channel_id=1, source_target_pairs={{0,4},{1,5},{2,6},{3,7},{4,0},{5,1},{6,2},{7,3},{8,12},{9,13},{10,... | collective-permute-start | bytes 393224 | tf_op jit(solution)/shard_map/ppermute | solution.py:45
  150.1 11.4 %collective-permute-start.26 = (bf16[64,1024]{1,0:T(8,128)(2,1)}, bf16[64,1024]{1,0:T(8,128)(2,1)}, u32[]{:S(2)}, u32[]{:S(2)}) collective-permute-start(bf16[64,1024]{1,0:T(8,128)(2,1)} %get-tuple-element.197), channel_id=1, source_target_pairs={{0,6},{1,7},{2,4},{3,5},{4,2},{5,3},{6,0},{7,1},{8,14},{9,15},{10,... | collective-permute-start | bytes 393224 | tf_op jit(solution)/shard_map/ppermute | solution.py:45
  161.5 7.1 %copy-start.29 = (f32[512,192]{1,0:T(8,128)S(1)}, f32[512,192]{1,0:T(8,128)}, u32[]{:S(2)}) copy-start(f32[512,192]{1,0:T(8,128)} %get-tuple-element.210) | copy-start | bytes 1179652
  161.5 16.8 %copy-start.33 = (bf16[64,1024]{1,0:T(8,128)(2,1)}, bf16[64,1024]{1,0:T(8,128)(2,1)S(1)}, u32[]{:S(2)}) copy-start(bf16[64,1024]{1,0:T(8,128)(2,1)S(1)} %collective-permute-done.24) | copy-start | bytes 393220
  161.5 16.8 %copy-start.35 = (bf16[64,1024]{1,0:T(8,128)(2,1)}, bf16[64,1024]{1,0:T(8,128)(2,1)S(1)}, u32[]{:S(2)}) copy-start(bf16[64,1024]{1,0:T(8,128)(2,1)S(1)} %collective-permute-done.25) | copy-start | bytes 393220
  162.4 35.2 %all-to-all-start.2 = ((bf16[32,32,512]{2,1,0:T(8,128)(2,1)}), bf16[32,32,512]{2,1,0:T(8,128)(2,1)S(1)}, u32[]{:S(2)}, u32[]{:S(2)}) async-start(bf16[32,32,512]{2,1,0:T(8,128)(2,1)} %bitcast.117), calls=%async_computation.2 | async-start | bytes 2097152 | tf_op jit(solution)/shard_map/all_to_all | solution.py:1127
  169.4 15.4 %collective-permute-start.30 = (bf16[4,64,192]{2,1,0:T(8,128)(2,1)}, bf16[4,64,192]{2,1,0:T(8,128)(2,1)}, u32[]{:S(2)}, u32[]{:S(2)}) collective-permute-start(bf16[4,64,192]{2,1,0:T(8,128)(2,1)} %fusion.7), channel_id=1, source_target_pairs={{0,1},{1,0},{2,3},{3,2},{4,5},{5,4},{6,7},{7,6},{8,9},{9,8},{10,11... | collective-permute-start | bytes 294920 | tf_op jit(solution)/shard_map/ppermute | solution.py:45
  177.8 14.7 %copy-start.21 = (f32[64,1024]{1,0:T(8,128)S(1)}, f32[64,1024]{1,0:T(8,128)}, u32[]{:S(2)}) copy-start(f32[64,1024]{1,0:T(8,128)} %slice_bitcast_fusion) | copy-start | bytes 786436
  177.8 8.1 %collective-permute-start.31 = (bf16[2,128,1024]{2,1,0:T(8,128)(2,1)}, bf16[2,128,1024]{2,1,0:T(8,128)(2,1)S(1)}, u32[]{:S(2)}, u32[]{:S(2)}) collective-permute-start(bf16[2,128,1024]{2,1,0:T(8,128)(2,1)} %get-tuple-element.212), channel_id=1, source_target_pairs={{0,8},{8,0},{16,24},{24,16},{1,9},{9,1},{17,25},{25,17},{2,10},{10... | collective-permute-start | bytes 1572872 | tf_op jit(solution)/shard_map/ppermute | solution.py:45
  177.8 19.8 %copy-start = (f32[32,4096]{1,0:T(8,128)S(1)}, f32[32,4096]{1,0:T(8,128)}, u32[]{:S(2)}) copy-start(f32[32,4096]{1,0:T(8,128)} %refs_0_.1) | copy-start | bytes 1572868
  177.8 19.8 %copy-start.17 = (f32[32]{0:T(128)S(1)}, f32[32]{0:T(128)}, u32[]{:S(2)}) copy-start(f32[32]{0:T(128)} %param.24) | copy-start | bytes 388
  177.9 27.6 %collective-permute-start.29 = (bf16[2,128,1024]{2,1,0:T(8,128)(2,1)}, bf16[2,128,1024]{2,1,0:T(8,128)(2,1)}, u32[]{:S(2)}, u32[]{:S(2)}) collective-permute-start(bf16[2,128,1024]{2,1,0:T(8,128)(2,1)} %get-tuple-element.209), channel_id=1, source_target_pairs={{0,8},{8,0},{16,24},{24,16},{1,9},{9,1},{17,25},{25,17},{2,10},{10... | collective-permute-start | bytes 1572872 | tf_op jit(solution)/shard_map/ppermute | solution.py:45
  184.8 7.6 %copy-start.34 = (bf16[64,1024]{1,0:T(8,128)(2,1)S(1)}, bf16[64,1024]{1,0:T(8,128)(2,1)}, u32[]{:S(2)}) copy-start(bf16[64,1024]{1,0:T(8,128)(2,1)} %copy-done.33) | copy-start | bytes 393220
  184.8 7.6 %copy-start.36 = (bf16[64,1024]{1,0:T(8,128)(2,1)S(1)}, bf16[64,1024]{1,0:T(8,128)(2,1)}, u32[]{:S(2)}) copy-start(bf16[64,1024]{1,0:T(8,128)(2,1)} %copy-done.35) | copy-start | bytes 393220
  188.0 6.9 %collective-permute-start.33 = (bf16[64,192]{1,0:T(8,128)(2,1)S(1)}, bf16[64,192]{1,0:T(8,128)(2,1)S(1)}, u32[]{:S(2)}, u32[]{:S(2)}) collective-permute-start(bf16[64,192]{1,0:T(8,128)(2,1)S(1)} %get-tuple-element.221), channel_id=1, source_target_pairs={{0,2},{1,3},{2,0},{3,1},{4,6},{5,7},{6,4},{7,5},{8,10},{9,11},{10,... | collective-permute-start | bytes 73736 | tf_op jit(solution)/shard_map/ppermute | solution.py:45
  188.0 9.3 %collective-permute-start.34 = (bf16[64,192]{1,0:T(8,128)(2,1)S(1)}, bf16[64,192]{1,0:T(8,128)(2,1)S(1)}, u32[]{:S(2)}, u32[]{:S(2)}) collective-permute-start(bf16[64,192]{1,0:T(8,128)(2,1)S(1)} %get-tuple-element.222), channel_id=1, source_target_pairs={{0,4},{1,5},{2,6},{3,7},{4,0},{5,1},{6,2},{7,3},{8,12},{9,13},{10,... | collective-permute-start | bytes 73736 | tf_op jit(solution)/shard_map/ppermute | solution.py:45
  190.0 7.3 %collective-permute-start.35 = (bf16[64,192]{1,0:T(8,128)(2,1)S(1)}, bf16[64,192]{1,0:T(8,128)(2,1)S(1)}, u32[]{:S(2)}, u32[]{:S(2)}) collective-permute-start(bf16[64,192]{1,0:T(8,128)(2,1)S(1)} %get-tuple-element.223), channel_id=1, source_target_pairs={{0,6},{1,7},{2,4},{3,5},{4,2},{5,3},{6,0},{7,1},{8,14},{9,15},{10,... | collective-permute-start | bytes 73736 | tf_op jit(solution)/shard_map/ppermute | solution.py:45
  193.4 13.1 %collective-permute-start.32 = (bf16[2,128,1024]{2,1,0:T(8,128)(2,1)}, bf16[2,128,1024]{2,1,0:T(8,128)(2,1)}, u32[]{:S(2)}, u32[]{:S(2)}) collective-permute-start(bf16[2,128,1024]{2,1,0:T(8,128)(2,1)} %add_convert_fusion), channel_id=1, source_target_pairs={{0,16},{8,24},{16,0},{24,8},{1,17},{9,25},{17,1},{25,9},{2,18},{10... | collective-permute-start | bytes 1572872 | tf_op jit(solution)/shard_map/ppermute | solution.py:45
  199.6 10.1 %all-to-all-start.3 = ((f32[32,1,128]{2,1,0:T(1,128)}), f32[32,1,128]{2,1,0:T(1,128)S(1)}, u32[]{:S(2)}, u32[]{:S(2)}) async-start(f32[32,1,128]{2,1,0:T(1,128)} %get-tuple-element.224), calls=%async_computation.3 | async-start | bytes 32768 | tf_op jit(solution)/shard_map/all_to_all | solution.py:1152
  206.5 3.3 %copy-start.11 = (f32[2,64,64]{2,1,0:T(8,128)S(1)}, f32[2,64,64]{2,1,0:T(8,128)}, u32[]{:S(2)}) copy-start(f32[2,64,64]{2,1,0:T(8,128)} %refs_10_.1) | copy-start | bytes 98308
  (14 other events, 32.5 us)

commit v3 on v2

--- a/solution.py
+++ b/solution.py
@@ -1123,7 +1123,7 @@
     gci, gin_conv, small_grad = leave(
         gact, gxt, xt, gsp, small, pre, conv, act, normed, chan, gskip, [galog]
     )
-    gin_conv, gout_far, out_rows = lax.optimization_barrier((gin_conv, gout_far, out_rows))
+    gin_conv, gout_far = lax.optimization_barrier((gin_conv, gout_far))
     conv_parts = lax.all_to_all(gin_conv.reshape(-1, own_in, width), both, 0, 0, tiled=True)
     grad_out = sum(part.astype(f32) for part in gout_far)
     small_near = reduce_near(split_near(small_grad.reshape(fsdps, own, GRADS)))

time: 213 us -> 212 us (level)
    unnamed x78 -> x84, local copies, waits for them, and re-layouts: 4.6 us -> 4.49 us
  transfers between devices with their start and end apart: 40 -> 40, of which waited for: 15 -> 14; matrix products, arithmetic and copies ran while one was open for 6% -> 5% of each run, Pallas kernels for 33% -> 34%
where the time goes in v3:
time: 212 us; the launch traced here: 211 us
  Pallas kernels  87.9 us (41%)
  starting transfers between devices  59.7 us (28%)
  waiting for transfers between devices  42 us (20%)
  other arithmetic  13.6 us (6%)
  local copies, waits for them, and re-layouts  6.71 us (3%)
    ppermute x36, starting transfers between devices, swap(): return lax.ppermute(x, axis, [(i, i ^ mask) for i in range(peers)])  43.1 us
    ppermute x36, waiting for transfers between devices, swap(): return lax.ppermute(x, axis, [(i, i ^ mask) for i in range(peers)])  36.5 us
    pallas_call x1, Pallas kernels, scan_backward(): pl.pallas_call(backward_kernel, grid=(seqs, blocks), in_specs=[pl.BlockSp...  24.2 us
    pallas_call x1, Pallas kernels, scan_forward(): pl.pallas_call(forward_kernel, grid=(seqs, blocks), in_specs=[pl.BlockSpe...  14.8 us
    pallas_call x1, Pallas kernels, middle(): pl.pallas_call(middle_kernel, grid_spec=pltpu.PrefetchScalarGridSpec(num_...  14.2 us
    pallas_call x1, Pallas kernels, leave(): pl.pallas_call(leave_kernel, grid=(seqs, blocks), in_specs=[pl.BlockSpec(...  10.3 us
    pallas_call x1, Pallas kernels, enter(): pl.pallas_call(enter_kernel, grid_spec=pltpu.PrefetchScalarGridSpec(num_s...  7.65 us
    pallas_call x1, Pallas kernels, rows_back(): pl.pallas_call(rows_back_kernel, grid_spec=pltpu.PrefetchScalarGridSpec(n...  6.56 us
  transfers between devices with their start and end apart: 40, of which 14 were waited for; matrix products, arithmetic and copies ran while one was open for 5% of the time, Pallas kernels for 34%

profile of v3, /device:TPU:0, one launch (start us, length us, event | category | flops | bytes accessed | tf_op | source)
XLA Modules:
  0.0 211.5 jit_solution(7460718685139579440)
XLA Ops:
  0.7 1.1 convert_element_type.117
  2.1 0.7 convert_bitcast_fusion.1
  3.0 0.8 copy.70
  3.8 4.2 %all-to-all-start = ((bf16[4,72,512]{2,1,0:T(8,128)(2,1)}), bf16[4,72,512]{2,1,0:T(8,128)(2,1)S(1)}, u32[]{:S(2)}, u32[]{:S(2)}) async-start(bf16[4,72,512]{2,1,0:T(8,128)(2,1)} %copy.70), calls=%async_computation | async-start | bytes 589824 | tf_op jit(solution)/shard_map/all_to_all | solution.py:1014
  8.0 2.3 %collective-permute-start.3 = (bf16[2,128,1024]{2,1,0:T(8,128)(2,1)S(1)}, bf16[2,128,1024]{2,1,0:T(8,128)(2,1)}, u32[]{:S(2)}, u32[]{:S(2)}) collective-permute-start(bf16[2,128,1024]{2,1,0:T(8,128)(2,1)S(1)} %bitcast.102), channel_id=1, source_target_pairs={{0,16},{8,24},{16,0},{24,8},{1,17},{9,25},{17,1},{25,9},{2,18},{10... | collective-permute-start | bytes 1572872 | tf_op jit(solution)/shard_map/ppermute | solution.py:45
  10.8 4.3 %all-to-all-done = bf16[4,72,512]{2,1,0:T(8,128)(2,1)S(1)} async-done(((bf16[4,72,512]{2,1,0:T(8,128)(2,1)}), bf16[4,72,512]{2,1,0:T(8,128)(2,1)S(1)}, u32[]{:S(2)}, u32[]{:S(2)}) %all-to-all-start) | async-done | bytes 294944 | tf_op jit(solution)/shard_map/all_to_all | solution.py:1014
  15.1 2.1 %collective-permute-start = (bf16[176,512]{1,0:T(8,128)(2,1)S(1)}, bf16[176,512]{1,0:T(8,128)(2,1)S(1)}, u32[]{:S(2)}, u32[]{:S(2)}) collective-permute-start(bf16[176,512]{1,0:T(8,128)(2,1)S(1)} %fusion.6.refs_0_), channel_id=1, source_target_pairs={{0,2},{1,3},{2,0},{3,1},{4,6},{5,7},{6,4},{7,5},{8,10},{9,11},{10,... | collective-permute-start | bytes 540680 | tf_op jit(solution)/shard_map/ppermute | solution.py:45
  17.3 2.6 %collective-permute-start.1 = (bf16[176,512]{1,0:T(8,128)(2,1)S(1)}, bf16[176,512]{1,0:T(8,128)(2,1)S(1)}, u32[]{:S(2)}, u32[]{:S(2)}) collective-permute-start(bf16[176,512]{1,0:T(8,128)(2,1)S(1)} %fusion.6.refs_0_), channel_id=1, source_target_pairs={{0,4},{1,5},{2,6},{3,7},{4,0},{5,1},{6,2},{7,3},{8,12},{9,13},{10,... | collective-permute-start | bytes 540680 | tf_op jit(solution)/shard_map/ppermute | solution.py:45
  19.9 1.7 collective-permute-start.4
  21.6 1.9 collective-permute-done.refs_1_
  23.5 9.7 %collective-permute-done.1.refs_2_ = bf16[176,512]{1,0:T(8,128)(2,1)S(1)} collective-permute-done((bf16[176,512]{1,0:T(8,128)(2,1)S(1)}, bf16[176,512]{1,0:T(8,128)(2,1)S(1)}, u32[]{:S(2)}, u32[]{:S(2)}) %collective-permute-start.1) | collective-permute-done | bytes 180256 | tf_op jit(solution)/shard_map/ppermute | solution.py:45
  33.3 1.6 collective-permute-start.5
  35.7 3.9 %collective-permute-start.10 = (bf16[256,512]{1,0:T(8,128)(2,1)S(1)}, bf16[256,512]{1,0:T(8,128)(2,1)S(1)}, u32[]{:S(2)}, u32[]{:S(2)}) collective-permute-start(bf16[256,512]{1,0:T(8,128)(2,1)S(1)} %pad_maximum_fusion.3.refs_0_), channel_id=1, source_target_pairs={{0,4},{1,5},{2,6},{3,7},{4,0},{5,1},{6,2},{7,3},{8,12},{9,13},{10,... | collective-permute-start | bytes 786440 | tf_op jit(solution)/shard_map/ppermute | solution.py:45
  39.6 5.0 %collective-permute-done.6.refs_2_ = bf16[2,128,1024]{2,1,0:T(8,128)(2,1)} collective-permute-done((bf16[2,128,1024]{2,1,0:T(8,128)(2,1)S(1)}, bf16[2,128,1024]{2,1,0:T(8,128)(2,1)}, u32[]{:S(2)}, u32[]{:S(2)}) %collective-permute-start.6) | collective-permute-done | bytes 524320 | tf_op jit(solution)/shard_map/ppermute | solution.py:45
  44.7 1.6 collective-permute-start.11
  46.2 0.8 copy-done.27
  47.0 4.9 %collective-permute-start.9 = (bf16[256,512]{1,0:T(8,128)(2,1)S(1)}, bf16[256,512]{1,0:T(8,128)(2,1)S(1)}, u32[]{:S(2)}, u32[]{:S(2)}) collective-permute-start(bf16[256,512]{1,0:T(8,128)(2,1)S(1)} %pad_maximum_fusion.3.refs_0_), channel_id=1, source_target_pairs={{0,2},{1,3},{2,0},{3,1},{4,6},{5,7},{6,4},{7,5},{8,10},{9,11},{10,... | collective-permute-start | bytes 786440 | tf_op jit(solution)/shard_map/ppermute | solution.py:45
  52.0 0.6 pad_add_fusion.me_ref
  52.6 2.6 %assemble_first.1 = (bf16[1024,512]{1,0:T(8,128)(2,1)}, bf16[512,256]{1,0:T(8,128)(2,1)}, f32[1,1024]{1,0:T(1,128)}, f32[16,512]{1,0:T(8,128)}, f32[8,512]{1,0:T(8,128)}) custom-call(s32[2]{0:T(128)} %pad_add_fusion.me_ref, bf16[176,512]{1,0:T(8,128)(2,1)} %copy-done.23, bf16[176,512]{1,0:T(8,128)(2,1)} %copy-done.24, bf16[176,512]{1,0:T(8,128)(2,1)} %copy-done.25, ...), custom_call_target="tpu_custom_call" | custom-call | flops 160000000 | bytes 600000 | tf_op jit(solution)/shard_map/assemble_first/pallas_call | solution.py:217
  55.2 7.7 %enter.1 = (bf16[2,512,1024]{2,1,0:T(8,128)(2,1)}, bf16[2,512,512]{2,1,0:T(8,128)(2,1)}, f32[2,512,512]{2,1,0:T(8,128)}, bf16[2,512,512]{2,1,0:T(8,128)(2,1)}, f32[48,1024]{1,0:T(8,128)}, /*index=5*/f32[48,1024]{1,0:T(8,128)}) custom-call(s32[2]{0:T(128)} %pad_add_fusion.me_ref, f32[1,1024]{1,0:T(1,128)} %get-tuple-element.141.gain_ref, ...), custom_call_target="tpu_custom_call" | custom-call | flops 560000000 | bytes 2100000 | tf_op jit(solution)/shard_map/enter/pallas_call | solution.py:308
  63.0 1.6 collective-permute-done.12
  64.6 1.0 add.55
  65.6 1.0 pad_maximum_fusion
  66.6 0.5 collective-permute-start.16
  67.1 1.4 collective-permute-start.13
  69.0 4.8 %collective-permute-done.13 = f32[48,1024]{1,0:T(8,128)S(1)} collective-permute-done((f32[48,1024]{1,0:T(8,128)S(1)}, f32[48,1024]{1,0:T(8,128)S(1)}, u32[]{:S(2)}, u32[]{:S(2)}) %collective-permute-start.13) | collective-permute-done | bytes 196640 | tf_op jit(solution)/shard_map/ppermute | solution.py:45
  73.9 1.6 collective-permute-start.15
  75.4 0.7 maximum_select_fusion
  76.1 14.8 %scan_forward.1 = (f32[2,512,512]{2,1,0:T(8,128)}, bf16[2,8192,512]{2,1,0:T(8,128)(2,1)}, f32[2,512,512]{2,1,0:T(8,128)}) custom-call(bf16[96,1024]{1,0:T(8,128)(2,1)} %bitcast.110, bf16[2,512,512]{2,1,0:T(8,128)(2,1)} %get-tuple-element.151.act_ref, bf16[512,256]{1,0:T(8,128)(2,1)} %get-tuple-element.144.wx_ref.dtw_ref, ...), custom_call_target="tpu_custom_call" | custom-call | flops 1440000000 | bytes 5400000 | tf_op jit(solution)/shard_map/scan_forward/pallas_call | solution.py:404
  91.0 1.0 collective-permute-done.15.refs_4_
  92.0 0.7 assemble_second.1
  92.7 1.0 copy-done.1
  93.7 1.0 copy-done.2
  94.6 14.2 %middle.1 = (f32[2,128,1024]{2,1,0:T(8,128)}, bf16[2,128,1024]{2,1,0:T(8,128)(2,1)}, f32[2,128,1024]{2,1,0:T(8,128)}, bf16[2,128,1024]{2,1,0:T(8,128)(2,1)}, bf1...) custom-call(s32[2]{0:T(128)} %pad_add_fusion.me_ref, ...), custom_call_target="tpu_custom_call" | custom-call | flops 720000000 | bytes 2700000 | tf_op jit(solution)/shard_map/middle/pallas_call | solution.py:507
  108.9 0.6 collective-permute-start.20
  109.5 3.6 %all-to-all-start.1 = ((bf16[32,32,512]{2,1,0:T(8,128)(2,1)}), bf16[32,32,512]{2,1,0:T(8,128)(2,1)S(1)}, u32[]{:S(2)}, u32[]{:S(2)}) async-start(bf16[32,32,512]{2,1,0:T(8,128)(2,1)} %bitcast.117), calls=%async_computation.1 | async-start | bytes 2097152 | tf_op jit(solution)/shard_map/all_to_all | solution.py:1110
  113.2 24.2 %scan_backward.1 = (bf16[2,512,512]{2,1,0:T(8,128)(2,1)}, f32[2,512,512]{2,1,0:T(8,128)}, f32[48,1024]{1,0:T(8,128)}, f32[48,1024]{1,0:T(8,128)}, f32[16,512]{1,0:T(8,128)}) custom-call(s32[2]{0:T(128)} %pad_add_fusion.me_ref, bf16[96,1024]{1,0:T(8,128)(2,1)} %bitcast.111, bf16[2,512,512]{2,1,0:T(8,128)(2,1)} %get-tuple-element.151.act_ref, ...), custom_call_target="tpu_custom_call" | custom-call | flops 2240000000 | bytes 8400000 | tf_op jit(solution)/shard_map/scan_backward/pallas_call | solution.py:644
  137.7 0.7 slice_bitcast_fusion
  139.0 1.1 collective-permute-done.22
  140.1 1.7 collective-permute-start.24
  141.8 3.5 %collective-permute-done.24 = bf16[48,1024]{1,0:T(8,128)(2,1)S(1)} collective-permute-done((bf16[48,1024]{1,0:T(8,128)(2,1)S(1)}, bf16[48,1024]{1,0:T(8,128)(2,1)S(1)}, u32[]{:S(2)}, u32[]{:S(2)}) %collective-permute-start.24) | collective-permute-done | bytes 98336 | tf_op jit(solution)/shard_map/ppermute | solution.py:45
  145.9 1.6 collective-permute-start.30
  147.5 2.4 %collective-permute-start.31 = (bf16[64,1024]{1,0:T(8,128)(2,1)S(1)}, bf16[64,1024]{1,0:T(8,128)(2,1)S(1)}, u32[]{:S(2)}, u32[]{:S(2)}) collective-permute-start(bf16[64,1024]{1,0:T(8,128)(2,1)S(1)} %get-tuple-element.206), channel_id=1, source_target_pairs={{0,4},{1,5},{2,6},{3,7},{4,0},{5,1},{6,2},{7,3},{8,12},{9,13},{10,... | collective-permute-start | bytes 393224 | tf_op jit(solution)/shard_map/ppermute | solution.py:45
  150.3 0.7 maximum_select_fusion.1
  151.0 10.3 %leave.1 = (bf16[2,512,512]{2,1,0:T(8,128)(2,1)}, bf16[1024,512]{1,0:T(8,128)(2,1)}, f32[512,192]{1,0:T(8,128)}) custom-call(f32[2,512,512]{2,1,0:T(8,128)} %get-tuple-element.183.gact_ref, bf16[96,1024]{1,0:T(8,128)(2,1)} %bitcast.119, bf16[96,1024]{1,0:T(8,128)(2,1)} %bitcast.112, bf16[2,512,512]{2,1,0:T(8,128)(2,1)} %get-tuple-element.186.gsp_ref, ...), custom_call_target="tpu_custom_call" | custom-call | flops 640000000 | bytes 2400000 | tf_op jit(solution)/shard_map/leave/pallas_call | solution.py:766
  161.3 0.6 copy-done.37
  162.0 5.7 %all-to-all-start.2 = ((bf16[32,32,512]{2,1,0:T(8,128)(2,1)}), bf16[32,32,512]{2,1,0:T(8,128)(2,1)S(1)}, u32[]{:S(2)}, u32[]{:S(2)}) async-start(bf16[32,32,512]{2,1,0:T(8,128)(2,1)} %bitcast.116), calls=%async_computation.2 | async-start | bytes 2097152 | tf_op jit(solution)/shard_map/all_to_all | solution.py:1127
  167.9 1.8 collective-permute-start.27
  169.7 2.0 add_convert_fusion.1
  171.7 1.5 collective-permute-start.23
  173.2 6.6 %rows_back.1 = (f32[2,128,1024]{2,1,0:T(8,128)}, bf16[2,128,1024]{2,1,0:T(8,128)(2,1)}, f32[2,128,1024]{2,1,0:T(8,128)}, bf16[2,128,1024]{2,1,0:T(8,128)(2,1)}) custom-call(s32[2]{0:T(128)} %pad_add_fusion.me_ref, bf16[2,512,512]{2,1,0:T(8,128)(2,1)} %get-tuple-element.191.gci_ref, bf16[2,512,512]{2,1,0:T(8,128)(2,1)} %get-tuple-element.192.ggp_ref, ...), custom_call_target="tpu_custom_call" | custom-call | flops 400000000 | bytes 1500000 | tf_op jit(solution)/shard_map/rows_back/pallas_call | solution.py:823
  180.3 3.4 %collective-permute-done.27 = bf16[4,64,192]{2,1,0:T(8,128)(2,1)S(1)} collective-permute-done((bf16[4,64,192]{2,1,0:T(8,128)(2,1)S(1)}, bf16[4,64,192]{2,1,0:T(8,128)(2,1)S(1)}, u32[]{:S(2)}, u32[]{:S(2)}) %collective-permute-start.27) | collective-permute-done | bytes 98336 | tf_op jit(solution)/shard_map/ppermute | solution.py:45
  183.8 2.2 %add_convert_fusion = bf16[2,128,1024]{2,1,0:T(8,128)(2,1)} fusion(f32[2,128,1024]{2,1,0:T(8,128)} %get-tuple-element.196, bf16[2,128,1024]{2,1,0:T(8,128)(2,1)S(1)} %collective-permute-done.28), kind=kLoop, calls=%fused_computation.2 | loop fusion | flops 786432 | bytes 2097152 | tf_op jit(solution)/shard_map/convert_element_type | solution.py:97
  186.0 2.0 collective-permute-start.34
  188.1 2.3 %collective-permute-start.35 = (bf16[64,192]{1,0:T(8,128)(2,1)S(1)}, bf16[64,192]{1,0:T(8,128)(2,1)S(1)}, u32[]{:S(2)}, u32[]{:S(2)}) collective-permute-start(bf16[64,192]{1,0:T(8,128)(2,1)S(1)} %get-tuple-element.217), channel_id=1, source_target_pairs={{0,6},{1,7},{2,4},{3,5},{4,2},{5,3},{6,0},{7,1},{8,14},{9,15},{10,... | collective-permute-start | bytes 73736 | tf_op jit(solution)/shard_map/ppermute | solution.py:45
  190.5 1.5 collective-permute-start.29
  192.0 4.3 %collective-permute-done.34 = bf16[64,192]{1,0:T(8,128)(2,1)S(1)} collective-permute-done((bf16[64,192]{1,0:T(8,128)(2,1)S(1)}, bf16[64,192]{1,0:T(8,128)(2,1)S(1)}, u32[]{:S(2)}, u32[]{:S(2)}) %collective-permute-start.34) | collective-permute-done | bytes 24608 | tf_op jit(solution)/shard_map/ppermute | solution.py:45
  196.6 1.2 collect.1
  197.8 0.8 copy-done.6
  198.6 3.1 %all-to-all-start.3 = ((f32[32,1,128]{2,1,0:T(1,128)}), f32[32,1,128]{2,1,0:T(1,128)S(1)}, u32[]{:S(2)}, u32[]{:S(2)}) async-start(f32[32,1,128]{2,1,0:T(1,128)} %get-tuple-element.218), calls=%async_computation.3 | async-start | bytes 32768 | tf_op jit(solution)/shard_map/all_to_all | solution.py:1152
  201.7 2.8 %fusion.1 = bf16[2,1,128,1024]{3,2,1,0:T(8,128)(2,1)} fusion(bf16[2,128,1024]{2,1,0:T(8,128)(2,1)} %collective-permute-done.23, f32[2,128,1024]{2,1,0:T(8,128)} %get-tuple-element.176, bf16[2,128,1024]{2,1,0:T(8,128)(2,1)} %copy-done.30, bf16[2,1,128,1024]{3,2,1,0:T(8,128)(2,1)} %param.16), kind=kLoop, calls=%fused_computation.12 | loop fusion | flops 1835008 | bytes 3145728
  204.6 3.1 %finish.1 = f32[2,128,1024]{2,1,0:T(8,128)} custom-call(bf16[2,128,1024]{2,1,0:T(8,128)(2,1)} %bitcast.101, bf16[2,128,1024]{2,1,0:T(8,128)(2,1)} %bitcast.105, f32[1,1024]{1,0:T(1,128)} %get-tuple-element.141.gain_ref, f32[2,128,1024]{2,1,0:T(8,128)} %get-tuple-element.219.refs_0_, bf16[2,128,1024]{2,1,0:T(8,128)(2,1)} %collective-permute-done.26.refs_1_, ...), custom_call_target="tpu_custom_call" | custom-call | flops 240000000 | bytes 900000 | tf_op jit(solution)/shard_map/finish/pallas_call | solution.py:859
  207.7 1.0 all-to-all-done.3.squares_ref
  208.8 2.5 %adam.1 = (f32[2,32,4096]{2,1,0:T(8,128)}, f32[32,4096]{1,0:T(8,128)}, f32[2,64,1024]{2,1,0:T(8,128)}, f32[64,1024]{1,0:T(8,128)}, f32[2,64,96]{2,1,0:T(8,128)},...) custom-call(f32[32,1,128]{2,1,0:T(1,128)S(1)} %all-to-all-done.3.squ, ...), custom_call_target="tpu_custom_call" | custom-call | flops 320000000 | bytes 1200000 | tf_op jit(solution)/shard_map/adam/pallas_call | solution.py:967
  (158 shorter events, 5.8 us)
Async XLA Ops:
  0.7 7.4 %copy-start.19 = (bf16[2,1,128,1024]{3,2,1,0:T(8,128)(2,1)S(1)}, bf16[2,1,128,1024]{3,2,1,0:T(8,128)(2,1)}, u32[]{:S(2)}) copy-start(bf16[2,1,128,1024]{3,2,1,0:T(8,128)(2,1)} %param.16) | copy-start | bytes 1572868
  0.7 9.6 %copy-start.12 = (f32[16,64]{1,0:T(8,128)S(1)}, f32[16,64]{1,0:T(8,128)}, u32[]{:S(2)}) copy-start(f32[16,64]{1,0:T(8,128)} %refs_5_.1) | copy-start | bytes 12292
  0.7 9.7 %copy-start.15 = (f32[7,64]{1,0:T(8,128)S(1)}, f32[7,64]{1,0:T(8,128)}, u32[]{:S(2)}) copy-start(f32[7,64]{1,0:T(8,128)} %refs_4_.1) | copy-start | bytes 5380
  0.7 9.8 %copy-start.9 = (f32[64,64]{1,0:T(8,128)S(1)}, f32[64,64]{1,0:T(8,128)}, u32[]{:S(2)}) copy-start(f32[64,64]{1,0:T(8,128)} %refs_3_.1) | copy-start | bytes 49156
  0.7 9.9 %copy-start.8 = (f32[64,96]{1,0:T(8,128)S(1)}, f32[64,96]{1,0:T(8,128)}, u32[]{:S(2)}) copy-start(f32[64,96]{1,0:T(8,128)} %refs_2_.1) | copy-start | bytes 73732
  2.8 32.1 %copy-start.20 = (bf16[2,1,128,1024]{3,2,1,0:T(8,128)(2,1)S(1)}, bf16[2,1,128,1024]{3,2,1,0:T(8,128)(2,1)}, u32[]{:S(2)}) copy-start(bf16[2,1,128,1024]{3,2,1,0:T(8,128)(2,1)} %param.17) | copy-start | bytes 1572868
  2.8 32.9 %copy-start.3 = (f32[64,1024]{1,0:T(8,128)S(1)}, f32[64,1024]{1,0:T(8,128)}, u32[]{:S(2)}) copy-start(f32[64,1024]{1,0:T(8,128)} %refs_1_.1) | copy-start | bytes 786436
  3.8 11.3 %all-to-all-start = ((bf16[4,72,512]{2,1,0:T(8,128)(2,1)}), bf16[4,72,512]{2,1,0:T(8,128)(2,1)S(1)}, u32[]{:S(2)}, u32[]{:S(2)}) async-start(bf16[4,72,512]{2,1,0:T(8,128)(2,1)} %copy.70), calls=%async_computation | async-start | bytes 589824 | tf_op jit(solution)/shard_map/all_to_all | solution.py:1014
  8.0 25.2 %collective-permute-start.3 = (bf16[2,128,1024]{2,1,0:T(8,128)(2,1)S(1)}, bf16[2,128,1024]{2,1,0:T(8,128)(2,1)}, u32[]{:S(2)}, u32[]{:S(2)}) collective-permute-start(bf16[2,128,1024]{2,1,0:T(8,128)(2,1)S(1)} %bitcast.102), channel_id=1, source_target_pairs={{0,16},{8,24},{16,0},{24,8},{1,17},{9,25},{17,1},{25,9},{2,18},{10... | collective-permute-start | bytes 1572872 | tf_op jit(solution)/shard_map/ppermute | solution.py:45
  15.1 37.4 %copy-start.23 = (bf16[176,512]{1,0:T(8,128)(2,1)}, bf16[176,512]{1,0:T(8,128)(2,1)S(1)}, u32[]{:S(2)}) copy-start(bf16[176,512]{1,0:T(8,128)(2,1)S(1)} %fusion.6.refs_0_) | copy-start | bytes 540676
  15.1 8.3 %collective-permute-start = (bf16[176,512]{1,0:T(8,128)(2,1)S(1)}, bf16[176,512]{1,0:T(8,128)(2,1)S(1)}, u32[]{:S(2)}, u32[]{:S(2)}) collective-permute-start(bf16[176,512]{1,0:T(8,128)(2,1)S(1)} %fusion.6.refs_0_), channel_id=1, source_target_pairs={{0,2},{1,3},{2,0},{3,1},{4,6},{5,7},{6,4},{7,5},{8,10},{9,11},{10,... | collective-permute-start | bytes 540680 | tf_op jit(solution)/shard_map/ppermute | solution.py:45
  17.3 15.9 %collective-permute-start.1 = (bf16[176,512]{1,0:T(8,128)(2,1)S(1)}, bf16[176,512]{1,0:T(8,128)(2,1)S(1)}, u32[]{:S(2)}, u32[]{:S(2)}) collective-permute-start(bf16[176,512]{1,0:T(8,128)(2,1)S(1)} %fusion.6.refs_0_), channel_id=1, source_target_pairs={{0,4},{1,5},{2,6},{3,7},{4,0},{5,1},{6,2},{7,3},{8,12},{9,13},{10,... | collective-permute-start | bytes 540680 | tf_op jit(solution)/shard_map/ppermute | solution.py:45
  19.9 13.4 %collective-permute-start.2 = (bf16[176,512]{1,0:T(8,128)(2,1)S(1)}, bf16[176,512]{1,0:T(8,128)(2,1)S(1)}, u32[]{:S(2)}, u32[]{:S(2)}) collective-permute-start(bf16[176,512]{1,0:T(8,128)(2,1)S(1)} %fusion.6.refs_0_), channel_id=1, source_target_pairs={{0,6},{1,7},{2,4},{3,5},{4,2},{5,3},{6,0},{7,1},{8,14},{9,15},{10,... | collective-permute-start | bytes 540680 | tf_op jit(solution)/shard_map/ppermute | solution.py:45
  19.9 13.4 %collective-permute-start.4 = (bf16[176,512]{1,0:T(8,128)(2,1)S(1)}, bf16[176,512]{1,0:T(8,128)(2,1)S(1)}, u32[]{:S(2)}, u32[]{:S(2)}) collective-permute-start(bf16[176,512]{1,0:T(8,128)(2,1)S(1)} %fusion.6.refs_0_), channel_id=1, source_target_pairs={{0,1},{1,0},{2,3},{3,2},{4,5},{5,4},{6,7},{7,6},{8,9},{9,8},{10,11... | collective-permute-start | bytes 540680 | tf_op jit(solution)/shard_map/ppermute | solution.py:45
  23.5 29.1 %copy-start.24 = (bf16[176,512]{1,0:T(8,128)(2,1)}, bf16[176,512]{1,0:T(8,128)(2,1)S(1)}, u32[]{:S(2)}) copy-start(bf16[176,512]{1,0:T(8,128)(2,1)S(1)} %collective-permute-done.refs_1_) | copy-start | bytes 540676
  33.2 19.3 %copy-start.25 = (bf16[176,512]{1,0:T(8,128)(2,1)}, bf16[176,512]{1,0:T(8,128)(2,1)S(1)}, u32[]{:S(2)}) copy-start(bf16[176,512]{1,0:T(8,128)(2,1)S(1)} %collective-permute-done.1.refs_2_) | copy-start | bytes 540676
  33.2 19.3 %copy-start.26 = (bf16[176,512]{1,0:T(8,128)(2,1)}, bf16[176,512]{1,0:T(8,128)(2,1)S(1)}, u32[]{:S(2)}) copy-start(bf16[176,512]{1,0:T(8,128)(2,1)S(1)} %collective-permute-done.2.refs_3_) | copy-start | bytes 540676
  33.2 19.3 %copy-start.32 = (bf16[176,512]{1,0:T(8,128)(2,1)}, bf16[176,512]{1,0:T(8,128)(2,1)S(1)}, u32[]{:S(2)}) copy-start(bf16[176,512]{1,0:T(8,128)(2,1)S(1)} %collective-permute-done.4.refs_4_) | copy-start | bytes 540676
  33.3 12.9 %collective-permute-start.5 = (bf16[3,176,512]{2,1,0:T(8,128)(2,1)S(1)}, bf16[3,176,512]{2,1,0:T(8,128)(2,1)S(1)}, u32[]{:S(2)}, u32[]{:S(2)}) collective-permute-start(bf16[3,176,512]{2,1,0:T(8,128)(2,1)S(1)} %pad_maximum_fusion.1), channel_id=1, source_target_pairs={{0,1},{1,0},{2,3},{3,2},{4,5},{5,4},{6,7},{7,6},{8,9},{9,8},{10,11... | collective-permute-start | bytes 1622024 | tf_op jit(solution)/shard_map/ppermute | solution.py:45
  34.9 9.8 %collective-permute-start.6 = (bf16[2,128,1024]{2,1,0:T(8,128)(2,1)S(1)}, bf16[2,128,1024]{2,1,0:T(8,128)(2,1)}, u32[]{:S(2)}, u32[]{:S(2)}) collective-permute-start(bf16[2,128,1024]{2,1,0:T(8,128)(2,1)S(1)} %bitcast.106), channel_id=1, source_target_pairs={{0,16},{8,24},{16,0},{24,8},{1,17},{9,25},{17,1},{25,9},{2,18},{10... | collective-permute-start | bytes 1572872 | tf_op jit(solution)/shard_map/ppermute | solution.py:45
  35.1 20.1 %collective-permute-start.7 = (bf16[2,128,1024]{2,1,0:T(8,128)(2,1)S(1)}, bf16[2,128,1024]{2,1,0:T(8,128)(2,1)}, u32[]{:S(2)}, u32[]{:S(2)}) collective-permute-start(bf16[2,128,1024]{2,1,0:T(8,128)(2,1)S(1)} %bitcast.103), channel_id=1, source_target_pairs={{0,8},{8,0},{16,24},{24,16},{1,9},{9,1},{17,25},{25,17},{2,10},{10... | collective-permute-start | bytes 1572872 | tf_op jit(solution)/shard_map/ppermute | solution.py:45
  35.1 20.1 %collective-permute-start.8 = (bf16[2,128,1024]{2,1,0:T(8,128)(2,1)}, bf16[2,128,1024]{2,1,0:T(8,128)(2,1)}, u32[]{:S(2)}, u32[]{:S(2)}) collective-permute-start(bf16[2,128,1024]{2,1,0:T(8,128)(2,1)} %collective-permute-done.3.refs_2_), channel_id=1, source_target_pairs={{0,8},{8,0},{16,24},{24,16},{1,9},{9,1},{17,25},{25,17},{2,10},{10... | collective-permute-start | bytes 1572872 | tf_op jit(solution)/shard_map/ppermute | solution.py:45
  35.7 27.1 %collective-permute-start.10 = (bf16[256,512]{1,0:T(8,128)(2,1)S(1)}, bf16[256,512]{1,0:T(8,128)(2,1)S(1)}, u32[]{:S(2)}, u32[]{:S(2)}) collective-permute-start(bf16[256,512]{1,0:T(8,128)(2,1)S(1)} %pad_maximum_fusion.3.refs_0_), channel_id=1, source_target_pairs={{0,4},{1,5},{2,6},{3,7},{4,0},{5,1},{6,2},{7,3},{8,12},{9,13},{10,... | collective-permute-start | bytes 786440 | tf_op jit(solution)/shard_map/ppermute | solution.py:45
  44.7 18.2 %collective-permute-start.11 = (bf16[256,512]{1,0:T(8,128)(2,1)S(1)}, bf16[256,512]{1,0:T(8,128)(2,1)S(1)}, u32[]{:S(2)}, u32[]{:S(2)}) collective-permute-start(bf16[256,512]{1,0:T(8,128)(2,1)S(1)} %pad_maximum_fusion.3.refs_0_), channel_id=1, source_target_pairs={{0,6},{1,7},{2,4},{3,5},{4,2},{5,3},{6,0},{7,1},{8,14},{9,15},{10,... | collective-permute-start | bytes 786440 | tf_op jit(solution)/shard_map/ppermute | solution.py:45
  47.0 15.9 %collective-permute-start.9 = (bf16[256,512]{1,0:T(8,128)(2,1)S(1)}, bf16[256,512]{1,0:T(8,128)(2,1)S(1)}, u32[]{:S(2)}, u32[]{:S(2)}) collective-permute-start(bf16[256,512]{1,0:T(8,128)(2,1)S(1)} %pad_maximum_fusion.3.refs_0_), channel_id=1, source_target_pairs={{0,2},{1,3},{2,0},{3,1},{4,6},{5,7},{6,4},{7,5},{8,10},{9,11},{10,... | collective-permute-start | bytes 786440 | tf_op jit(solution)/shard_map/ppermute | solution.py:45
  63.0 1.7 collective-permute-start.12
  66.6 25.4 %collective-permute-start.16 = (bf16[3,256,512]{2,1,0:T(8,128)(2,1)}, bf16[3,256,512]{2,1,0:T(8,128)(2,1)S(1)}, u32[]{:S(2)}, u32[]{:S(2)}) collective-permute-start(bf16[3,256,512]{2,1,0:T(8,128)(2,1)} %pad_maximum_fusion), channel_id=1, source_target_pairs={{0,1},{1,0},{2,3},{3,2},{4,5},{5,4},{6,7},{7,6},{8,9},{9,8},{10,11... | collective-permute-start | bytes 2359304 | tf_op jit(solution)/shard_map/ppermute | solution.py:45
  67.1 6.7 %collective-permute-start.13 = (f32[48,1024]{1,0:T(8,128)S(1)}, f32[48,1024]{1,0:T(8,128)S(1)}, u32[]{:S(2)}, u32[]{:S(2)}) collective-permute-start(f32[48,1024]{1,0:T(8,128)S(1)} %add.55), channel_id=1, source_target_pairs={{0,16},{8,24},{16,0},{24,8},{1,17},{9,25},{17,1},{25,9},{2,18},{10... | collective-permute-start | bytes 589832 | tf_op jit(solution)/shard_map/ppermute | solution.py:45
  68.5 26.1 %collective-permute-start.17 = (bf16[2,128,1024]{2,1,0:T(8,128)(2,1)S(1)}, bf16[2,128,1024]{2,1,0:T(8,128)(2,1)}, u32[]{:S(2)}, u32[]{:S(2)}) collective-permute-start(bf16[2,128,1024]{2,1,0:T(8,128)(2,1)S(1)} %bitcast.107), channel_id=1, source_target_pairs={{0,8},{8,0},{16,24},{24,16},{1,9},{9,1},{17,25},{25,17},{2,10},{10... | collective-permute-start | bytes 1572872 | tf_op jit(solution)/shard_map/ppermute | solution.py:45
  68.5 26.1 %collective-permute-start.18 = (bf16[2,128,1024]{2,1,0:T(8,128)(2,1)}, bf16[2,128,1024]{2,1,0:T(8,128)(2,1)}, u32[]{:S(2)}, u32[]{:S(2)}) collective-permute-start(bf16[2,128,1024]{2,1,0:T(8,128)(2,1)} %collective-permute-done.6.refs_2_), channel_id=1, source_target_pairs={{0,8},{8,0},{16,24},{24,16},{1,9},{9,1},{17,25},{25,17},{2,10},{10... | collective-permute-start | bytes 1572872 | tf_op jit(solution)/shard_map/ppermute | solution.py:45
  73.8 1.6 collective-permute-start.14
  73.9 18.1 %collective-permute-start.15 = (bf16[256,512]{1,0:T(8,128)(2,1)S(1)}, bf16[256,512]{1,0:T(8,128)(2,1)S(1)}, u32[]{:S(2)}, u32[]{:S(2)}) collective-permute-start(bf16[256,512]{1,0:T(8,128)(2,1)S(1)} %pad_maximum_fusion.3.refs_0_), channel_id=1, source_target_pairs={{0,1},{1,0},{2,3},{3,2},{4,5},{5,4},{6,7},{7,6},{8,9},{9,8},{10,11... | collective-permute-start | bytes 786440 | tf_op jit(solution)/shard_map/ppermute | solution.py:45
  76.1 15.9 %copy-start.13 = (s32[2]{0:T(128)S(1)}, s32[2]{0:T(128)}, u32[]{:S(2)}) copy-start(s32[2]{0:T(128)} %pad_add_fusion.me_ref) | copy-start | bytes 28
  108.9 28.6 %collective-permute-start.20 = (bf16[4,64,1024]{2,1,0:T(8,128)(2,1)}, bf16[4,64,1024]{2,1,0:T(8,128)(2,1)S(1)}, u32[]{:S(2)}, u32[]{:S(2)}) collective-permute-start(bf16[4,64,1024]{2,1,0:T(8,128)(2,1)} %get-tuple-element.175), channel_id=1, source_target_pairs={{0,1},{1,0},{2,3},{3,2},{4,5},{5,4},{6,7},{7,6},{8,9},{9,8},{10,11... | collective-permute-start | bytes 1572872 | tf_op jit(solution)/shard_map/ppermute | solution.py:45
  109.5 41.4 %all-to-all-start.1 = ((bf16[32,32,512]{2,1,0:T(8,128)(2,1)}), bf16[32,32,512]{2,1,0:T(8,128)(2,1)S(1)}, u32[]{:S(2)}, u32[]{:S(2)}) async-start(bf16[32,32,512]{2,1,0:T(8,128)(2,1)} %bitcast.117), calls=%async_computation.1 | async-start | bytes 2097152 | tf_op jit(solution)/shard_map/all_to_all | solution.py:1110
  113.1 25.4 %collective-permute-start.19 = (bf16[2,128,1024]{2,1,0:T(8,128)(2,1)S(1)}, bf16[2,128,1024]{2,1,0:T(8,128)(2,1)S(1)}, u32[]{:S(2)}, u32[]{:S(2)}) collective-permute-start(bf16[2,128,1024]{2,1,0:T(8,128)(2,1)S(1)} %copy-done.39), channel_id=1, source_target_pairs={{0,8},{8,0},{16,24},{24,16},{1,9},{9,1},{17,25},{25,17},{2,10},{10... | collective-permute-start | bytes 1572872 | tf_op jit(solution)/shard_map/ppermute | solution.py:45
  113.2 24.3 %copy-start.28 = (bf16[4,64,1024]{2,1,0:T(8,128)(2,1)S(1)}, bf16[4,64,1024]{2,1,0:T(8,128)(2,1)}, u32[]{:S(2)}) copy-start(bf16[4,64,1024]{2,1,0:T(8,128)(2,1)} %get-tuple-element.174) | copy-start | bytes 1572868
  138.5 22.7 %copy-start.30 = (bf16[2,128,1024]{2,1,0:T(8,128)(2,1)}, bf16[2,128,1024]{2,1,0:T(8,128)(2,1)S(1)}, u32[]{:S(2)}) copy-start(bf16[2,128,1024]{2,1,0:T(8,128)(2,1)S(1)} %collective-permute-done.19) | copy-start | bytes 1572868
  138.5 1.6 collective-permute-start.22
  140.1 5.1 %collective-permute-start.24 = (bf16[48,1024]{1,0:T(8,128)(2,1)S(1)}, bf16[48,1024]{1,0:T(8,128)(2,1)S(1)}, u32[]{:S(2)}, u32[]{:S(2)}) collective-permute-start(bf16[48,1024]{1,0:T(8,128)(2,1)S(1)} %get-tuple-element.313), channel_id=1, source_target_pairs={{0,16},{8,24},{16,0},{24,8},{1,17},{9,25},{17,1},{25,9},{2,18},{10... | collective-permute-start | bytes 294920 | tf_op jit(solution)/shard_map/ppermute | solution.py:45
  145.3 5.0 %collective-permute-start.25 = (bf16[48,1024]{1,0:T(8,128)(2,1)S(1)}, bf16[48,1024]{1,0:T(8,128)(2,1)S(1)}, u32[]{:S(2)}, u32[]{:S(2)}) collective-permute-start(bf16[48,1024]{1,0:T(8,128)(2,1)S(1)} %add_convert_fusion.2), channel_id=1, source_target_pairs={{0,8},{8,0},{16,24},{24,16},{1,9},{9,1},{17,25},{25,17},{2,10},{10... | collective-permute-start | bytes 294920 | tf_op jit(solution)/shard_map/ppermute | solution.py:45
  145.4 24.3 %collective-permute-start.21 = (bf16[2,128,1024]{2,1,0:T(8,128)(2,1)}, bf16[2,128,1024]{2,1,0:T(8,128)(2,1)}, u32[]{:S(2)}, u32[]{:S(2)}) collective-permute-start(bf16[2,128,1024]{2,1,0:T(8,128)(2,1)} %get-tuple-element.179), channel_id=1, source_target_pairs={{0,8},{8,0},{16,24},{24,16},{1,9},{9,1},{17,25},{25,17},{2,10},{10... | collective-permute-start | bytes 1572872 | tf_op jit(solution)/shard_map/ppermute | solution.py:45
  145.9 15.4 %collective-permute-start.30 = (bf16[64,1024]{1,0:T(8,128)(2,1)S(1)}, bf16[64,1024]{1,0:T(8,128)(2,1)S(1)}, u32[]{:S(2)}, u32[]{:S(2)}) collective-permute-start(bf16[64,1024]{1,0:T(8,128)(2,1)S(1)} %get-tuple-element.205), channel_id=1, source_target_pairs={{0,2},{1,3},{2,0},{3,1},{4,6},{5,7},{6,4},{7,5},{8,10},{9,11},{10,... | collective-permute-start | bytes 393224 | tf_op jit(solution)/shard_map/ppermute | solution.py:45
  147.5 13.8 %collective-permute-start.31 = (bf16[64,1024]{1,0:T(8,128)(2,1)S(1)}, bf16[64,1024]{1,0:T(8,128)(2,1)S(1)}, u32[]{:S(2)}, u32[]{:S(2)}) collective-permute-start(bf16[64,1024]{1,0:T(8,128)(2,1)S(1)} %get-tuple-element.206), channel_id=1, source_target_pairs={{0,4},{1,5},{2,6},{3,7},{4,0},{5,1},{6,2},{7,3},{8,12},{9,13},{10,... | collective-permute-start | bytes 393224 | tf_op jit(solution)/shard_map/ppermute | solution.py:45
  149.9 11.4 %collective-permute-start.32 = (bf16[64,1024]{1,0:T(8,128)(2,1)S(1)}, bf16[64,1024]{1,0:T(8,128)(2,1)S(1)}, u32[]{:S(2)}, u32[]{:S(2)}) collective-permute-start(bf16[64,1024]{1,0:T(8,128)(2,1)S(1)} %get-tuple-element.207), channel_id=1, source_target_pairs={{0,6},{1,7},{2,4},{3,5},{4,2},{5,3},{6,0},{7,1},{8,14},{9,15},{10,... | collective-permute-start | bytes 393224 | tf_op jit(solution)/shard_map/ppermute | solution.py:45
  161.2 6.4 %copy-start.29 = (f32[512,192]{1,0:T(8,128)S(1)}, f32[512,192]{1,0:T(8,128)}, u32[]{:S(2)}) copy-start(f32[512,192]{1,0:T(8,128)} %get-tuple-element.195) | copy-start | bytes 1179652
  161.3 6.5 %copy-start.33 = (bf16[64,1024]{1,0:T(8,128)(2,1)}, bf16[64,1024]{1,0:T(8,128)(2,1)S(1)}, u32[]{:S(2)}) copy-start(bf16[64,1024]{1,0:T(8,128)(2,1)S(1)} %collective-permute-done.30) | copy-start | bytes 393220
  161.3 6.5 %copy-start.35 = (bf16[64,1024]{1,0:T(8,128)(2,1)}, bf16[64,1024]{1,0:T(8,128)(2,1)S(1)}, u32[]{:S(2)}) copy-start(bf16[64,1024]{1,0:T(8,128)(2,1)S(1)} %collective-permute-done.31) | copy-start | bytes 393220
  162.0 34.7 %all-to-all-start.2 = ((bf16[32,32,512]{2,1,0:T(8,128)(2,1)}), bf16[32,32,512]{2,1,0:T(8,128)(2,1)S(1)}, u32[]{:S(2)}, u32[]{:S(2)}) async-start(bf16[32,32,512]{2,1,0:T(8,128)(2,1)} %bitcast.116), calls=%async_computation.2 | async-start | bytes 2097152 | tf_op jit(solution)/shard_map/all_to_all | solution.py:1127
  167.9 15.9 %collective-permute-start.27 = (bf16[4,64,192]{2,1,0:T(8,128)(2,1)S(1)}, bf16[4,64,192]{2,1,0:T(8,128)(2,1)S(1)}, u32[]{:S(2)}, u32[]{:S(2)}) collective-permute-start(bf16[4,64,192]{2,1,0:T(8,128)(2,1)S(1)} %fusion.7), channel_id=1, source_target_pairs={{0,1},{1,0},{2,3},{3,2},{4,5},{5,4},{6,7},{7,6},{8,9},{9,8},{10,11... | collective-permute-start | bytes 294920 | tf_op jit(solution)/shard_map/ppermute | solution.py:45
  171.7 30.0 %collective-permute-start.23 = (bf16[2,128,1024]{2,1,0:T(8,128)(2,1)}, bf16[2,128,1024]{2,1,0:T(8,128)(2,1)}, u32[]{:S(2)}, u32[]{:S(2)}) collective-permute-start(bf16[2,128,1024]{2,1,0:T(8,128)(2,1)} %add_convert_fusion.1), channel_id=1, source_target_pairs={{0,16},{8,24},{16,0},{24,8},{1,17},{9,25},{17,1},{25,9},{2,18},{10... | collective-permute-start | bytes 1572872 | tf_op jit(solution)/shard_map/ppermute | solution.py:45
  179.7 10.7 %copy-start.21 = (f32[64,1024]{1,0:T(8,128)S(1)}, f32[64,1024]{1,0:T(8,128)}, u32[]{:S(2)}) copy-start(f32[64,1024]{1,0:T(8,128)} %slice_bitcast_fusion) | copy-start | bytes 786436
  179.7 10.7 %copy-start.34 = (bf16[64,1024]{1,0:T(8,128)(2,1)S(1)}, bf16[64,1024]{1,0:T(8,128)(2,1)}, u32[]{:S(2)}) copy-start(bf16[64,1024]{1,0:T(8,128)(2,1)} %copy-done.33) | copy-start | bytes 393220
  179.7 10.7 %copy-start.36 = (bf16[64,1024]{1,0:T(8,128)(2,1)S(1)}, bf16[64,1024]{1,0:T(8,128)(2,1)}, u32[]{:S(2)}) copy-start(bf16[64,1024]{1,0:T(8,128)(2,1)} %copy-done.35) | copy-start | bytes 393220
  179.7 10.7 %copy-start.38 = (bf16[64,1024]{1,0:T(8,128)(2,1)S(1)}, bf16[64,1024]{1,0:T(8,128)(2,1)}, u32[]{:S(2)}) copy-start(bf16[64,1024]{1,0:T(8,128)(2,1)} %copy-done.37) | copy-start | bytes 393220
  179.8 4.1 %collective-permute-start.28 = (bf16[2,128,1024]{2,1,0:T(8,128)(2,1)}, bf16[2,128,1024]{2,1,0:T(8,128)(2,1)S(1)}, u32[]{:S(2)}, u32[]{:S(2)}) collective-permute-start(bf16[2,128,1024]{2,1,0:T(8,128)(2,1)} %get-tuple-element.197), channel_id=1, source_target_pairs={{0,8},{8,0},{16,24},{24,16},{1,9},{9,1},{17,25},{25,17},{2,10},{10... | collective-permute-start | bytes 1572872 | tf_op jit(solution)/shard_map/ppermute | solution.py:45
  179.8 16.8 %copy-start = (f32[32,4096]{1,0:T(8,128)S(1)}, f32[32,4096]{1,0:T(8,128)}, u32[]{:S(2)}) copy-start(f32[32,4096]{1,0:T(8,128)} %refs_0_.1) | copy-start | bytes 1572868
  179.8 16.8 %copy-start.17 = (f32[32]{0:T(128)S(1)}, f32[32]{0:T(128)}, u32[]{:S(2)}) copy-start(f32[32]{0:T(128)} %param.24) | copy-start | bytes 388
  179.9 24.7 %collective-permute-start.26 = (bf16[2,128,1024]{2,1,0:T(8,128)(2,1)}, bf16[2,128,1024]{2,1,0:T(8,128)(2,1)}, u32[]{:S(2)}, u32[]{:S(2)}) collective-permute-start(bf16[2,128,1024]{2,1,0:T(8,128)(2,1)} %get-tuple-element.194), channel_id=1, source_target_pairs={{0,8},{8,0},{16,24},{24,16},{1,9},{9,1},{17,25},{25,17},{2,10},{10... | collective-permute-start | bytes 1572872 | tf_op jit(solution)/shard_map/ppermute | solution.py:45
  186.0 4.5 %collective-permute-start.33 = (bf16[64,192]{1,0:T(8,128)(2,1)S(1)}, bf16[64,192]{1,0:T(8,128)(2,1)S(1)}, u32[]{:S(2)}, u32[]{:S(2)}) collective-permute-start(bf16[64,192]{1,0:T(8,128)(2,1)S(1)} %get-tuple-element.215), channel_id=1, source_target_pairs={{0,2},{1,3},{2,0},{3,1},{4,6},{5,7},{6,4},{7,5},{8,10},{9,11},{10,... | collective-permute-start | bytes 73736 | tf_op jit(solution)/shard_map/ppermute | solution.py:45
  186.0 10.3 %collective-permute-start.34 = (bf16[64,192]{1,0:T(8,128)(2,1)S(1)}, bf16[64,192]{1,0:T(8,128)(2,1)S(1)}, u32[]{:S(2)}, u32[]{:S(2)}) collective-permute-start(bf16[64,192]{1,0:T(8,128)(2,1)S(1)} %get-tuple-element.216), channel_id=1, source_target_pairs={{0,4},{1,5},{2,6},{3,7},{4,0},{5,1},{6,2},{7,3},{8,12},{9,13},{10,... | collective-permute-start | bytes 73736 | tf_op jit(solution)/shard_map/ppermute | solution.py:45
  188.1 8.3 %collective-permute-start.35 = (bf16[64,192]{1,0:T(8,128)(2,1)S(1)}, bf16[64,192]{1,0:T(8,128)(2,1)S(1)}, u32[]{:S(2)}, u32[]{:S(2)}) collective-permute-start(bf16[64,192]{1,0:T(8,128)(2,1)S(1)} %get-tuple-element.217), channel_id=1, source_target_pairs={{0,6},{1,7},{2,4},{3,5},{4,2},{5,3},{6,0},{7,1},{8,14},{9,15},{10,... | collective-permute-start | bytes 73736 | tf_op jit(solution)/shard_map/ppermute | solution.py:45
  190.5 14.0 %collective-permute-start.29 = (bf16[2,128,1024]{2,1,0:T(8,128)(2,1)}, bf16[2,128,1024]{2,1,0:T(8,128)(2,1)}, u32[]{:S(2)}, u32[]{:S(2)}) collective-permute-start(bf16[2,128,1024]{2,1,0:T(8,128)(2,1)} %add_convert_fusion), channel_id=1, source_target_pairs={{0,16},{8,24},{16,0},{24,8},{1,17},{9,25},{17,1},{25,9},{2,18},{10... | collective-permute-start | bytes 1572872 | tf_op jit(solution)/shard_map/ppermute | solution.py:45
  198.6 10.1 %all-to-all-start.3 = ((f32[32,1,128]{2,1,0:T(1,128)}), f32[32,1,128]{2,1,0:T(1,128)S(1)}, u32[]{:S(2)}, u32[]{:S(2)}) async-start(f32[32,1,128]{2,1,0:T(1,128)} %get-tuple-element.218), calls=%async_computation.3 | async-start | bytes 32768 | tf_op jit(solution)/shard_map/all_to_all | solution.py:1152
  (17 other events, 47.9 us)
